TPU v7x, 32 devices: a whole 2x2x4 slice. The times are simulated.
32 devices in a mesh: dp: 8 (over z, y), tensor: 4 (over x, core).
Axes of the slice: x: 2, y: 2, z: 4, core: 2. Of those that a mesh axis runs over, the one named last changes fastest.
Arguments:
- tokens: bfloat16 [4, 8, 1024, 768], P(None, 'dp', 'tensor'), may hold values from -6 to 6
- doc_ids: int32 [4, 8, 1024], P(None, 'dp'), may hold values from 0 to 7, never falling along the last dimension, each value on 1 to 800 neighbouring positions
- w_query: bfloat16 [768, 768], P('dp', 'tensor'), may hold values from -0.21875 to 0.21875
- b_query: float32 [768], P('tensor'), may hold values from -3 to 3
- w_key: bfloat16 [768, 768], P('dp', 'tensor'), may hold values from -0.21875 to 0.21875
- w_value: bfloat16 [768, 768], P('dp', 'tensor'), may hold values from -0.21875 to 0.21875
- b_value: float32 [768], P('tensor'), may hold values from -3 to 3
- w_mixer: bfloat16 [768, 768], P('tensor', 'dp'), may hold values from -1.75 to 1.75
- b_mixer: float32 [768], replicated, may hold values from -2 to 2
- gain_one: float32 [768], replicated, may hold values from 0.25 to 1.75
- bias_one: float32 [768], replicated, may hold values from -2 to 2
- w_inner: bfloat16 [768, 3072], P('dp', 'tensor'), may hold values from -0.21875 to 0.21875
- b_inner: float32 [3072], P('tensor'), may hold values from -3 to 3
- w_outer: bfloat16 [3072, 768], P('tensor', 'dp'), may hold values from -0.109375 to 0.109375
- b_outer: float32 [768], replicated, may hold values from -2 to 2
- gain_two: float32 [768], replicated, may hold values from 0.25 to 1.75
- bias_two: float32 [768], replicated, may hold values from -2 to 2
- cotangent: bfloat16 [4, 8, 1024, 768], P(None, 'dp', 'tensor'), may hold values from -6 to 6
Outputs:
- layer_output: bfloat16 [4, 8, 1024, 768], P(None, 'dp', 'tensor')
- d_tokens: float32 [4, 8, 1024, 768], P(None, 'dp', 'tensor')
- dw_query: float32 [768, 768], P('dp', 'tensor')
- db_query: float32 [768], P('tensor')
- dw_key: float32 [768, 768], P('dp', 'tensor')
- dw_value: float32 [768, 768], P('dp', 'tensor')
- db_value: float32 [768], P('tensor')
- dw_mixer: float32 [768, 768], P('tensor', 'dp')
- db_mixer: float32 [768], replicated
- dgain_one: float32 [768], replicated
- dbias_one: float32 [768], replicated
- dw_inner: float32 [768, 3072], P('dp', 'tensor')
- db_inner: float32 [3072], P('tensor')
- dw_outer: float32 [3072, 768], P('tensor', 'dp')
- db_outer: float32 [768], replicated
- dgain_two: float32 [768], replicated
- dbias_two: float32 [768], replicated
Inputs may be any that keep to these rules, and one draw needn't show every extreme that they name: `doc_ids`: within each sequence the numbers never fall; a document is the tokens of one sequence that share a number, and none is longer than 800 tokens.
All inputs are finite; a program needn't handle non-finite values.
Results may differ from a plain program's by a relative error of at most 0.017.
The roundings to bfloat16 on the way count: a program that leaves them out, or rounds other values in their place, can miss the bound.
Values may be sent and summed in bfloat16 or wider, within the bound.
A program may use at most 256 MiB of HBM per device.

v0:
```python
from functools import partial

import jax
import jax.numpy as jnp
from jax import lax
from jax.sharding import PartitionSpec as P

HEAD = 64


def normalize(values, weights, offsets):
    average = jnp.mean(values, axis=-1, keepdims=True)
    centred = values - average
    spread = jnp.mean(centred * centred, axis=-1, keepdims=True)
    return centred * lax.rsqrt(spread + 1e-12) * weights + offsets


def exact_gelu(values):
    return jax.nn.gelu(values, approximate=False)


def contract_rows(left, right):
    return lax.dot_general(
        left, right, (((0,), (0,)), ((), ())), preferred_element_type=jnp.float32
    )


def contract_cols(left, right):
    return lax.dot_general(
        left, right, (((1,), (1,)), ((), ())), preferred_element_type=jnp.float32
    )


def split_heads(values, head_size):
    return values.reshape(values.shape[0], values.shape[1] // head_size, head_size)


def head_scores(q_heads, k_heads, labels, factor):
    scores = (
        jnp.einsum("qhd,khd->hqk", q_heads, k_heads, preferred_element_type=jnp.float32) * factor
    )
    same_doc = labels[:, None] == labels[None, :]
    return jnp.where(same_doc[None], scores, -1e30)


def attend_forward(packed, head_size):
    queries, keys_in, values_in, labels = packed
    factor = head_size ** (-0.5)
    q_heads = split_heads(queries, head_size)
    k_heads = split_heads(keys_in, head_size)
    v_heads = split_heads(values_in, head_size)
    scores = head_scores(q_heads, k_heads, labels, factor)
    highest = jnp.max(scores, axis=-1, keepdims=True)
    raw_weights = jnp.exp(scores - highest)
    totals = jnp.sum(raw_weights, axis=-1, keepdims=True)
    chance_low = (raw_weights / totals).astype(jnp.bfloat16)
    mixed = jnp.einsum("hqk,khd->qhd", chance_low, v_heads, preferred_element_type=jnp.float32)
    attended = mixed.reshape(queries.shape).astype(jnp.bfloat16)
    return (attended, highest[..., 0] + jnp.log(totals[..., 0]))


def attend_backward(packed, head_size):
    queries, keys_in, values_in, labels, logsums, d_attended = packed
    factor = head_size ** (-0.5)
    q_heads = split_heads(queries, head_size)
    k_heads = split_heads(keys_in, head_size)
    v_heads = split_heads(values_in, head_size)
    scores = head_scores(q_heads, k_heads, labels, factor)
    chances = jnp.exp(scores - logsums[..., None])
    chance_low = chances.astype(jnp.bfloat16)
    d_heads = split_heads(d_attended, head_size)
    d_values = jnp.einsum("hqk,qhd->khd", chance_low, d_heads, preferred_element_type=jnp.float32)
    d_chances = jnp.einsum("qhd,khd->hqk", d_heads, v_heads, preferred_element_type=jnp.float32)
    centre = jnp.sum(chances * d_chances, axis=-1, keepdims=True)
    d_scores = (chances * (d_chances - centre)).astype(jnp.bfloat16)
    d_queries = (
        jnp.einsum("hqk,khd->qhd", d_scores, k_heads, preferred_element_type=jnp.float32) * factor
    )
    d_keys = (
        jnp.einsum("hqk,qhd->khd", d_scores, q_heads, preferred_element_type=jnp.float32) * factor
    )
    full_shape = queries.shape
    return (
        d_queries.reshape(full_shape).astype(jnp.bfloat16),
        d_keys.reshape(full_shape).astype(jnp.bfloat16),
        d_values.reshape(full_shape).astype(jnp.bfloat16),
    )


def body(
    tokens,
    doc_ids,
    w_query,
    b_query,
    w_key,
    w_value,
    b_value,
    w_mixer,
    b_mixer,
    gain_one,
    bias_one,
    w_inner,
    b_inner,
    w_outer,
    b_outer,
    gain_two,
    bias_two,
    cotangent,
):
    batches, seq_here, part_len, model_width = tokens.shape
    length = doc_ids.shape[2]
    local_width = w_query.shape[1]
    local_hidden = w_inner.shape[1]
    rows_count = seq_here * length
    shards = (w_query, w_key, w_value, w_mixer, w_inner, w_outer)
    forward_fn = partial(attend_forward, head_size=HEAD)
    backward_fn = partial(attend_backward, head_size=HEAD)
    sum_grads = tuple((jnp.zeros(shard_part.shape, jnp.float32) for shard_part in shards))
    small_sums = (
        jnp.zeros((local_width,), jnp.float32),
        jnp.zeros((local_width,), jnp.float32),
        jnp.zeros((local_hidden,), jnp.float32),
    ) + tuple((jnp.zeros((model_width,), jnp.float32) for slot_number in range(6)))
    results = []
    token_grads = []
    for batch_index in range(batches):
        current = (
            lax.all_gather(shards[0], "dp", axis=0, tiled=True),
            lax.all_gather(shards[1], "dp", axis=0, tiled=True),
            lax.all_gather(shards[2], "dp", axis=0, tiled=True),
            lax.all_gather(shards[3], "dp", axis=1, tiled=True),
            lax.all_gather(shards[4], "dp", axis=0, tiled=True),
            lax.all_gather(shards[5], "dp", axis=1, tiled=True),
        )
        wq_full, wk_full, wv_full, wm_full, wi_full, wo_full = current
        x_here = tokens[batch_index]
        labels = doc_ids[batch_index]
        x_all = lax.all_gather(x_here, "tensor", axis=1, tiled=True)
        token_rows = x_all.reshape(rows_count, model_width)
        queries = (
            jnp.dot(token_rows, wq_full, preferred_element_type=jnp.float32) + b_query
        ).astype(jnp.bfloat16)
        keys_low = jnp.dot(token_rows, wk_full, preferred_element_type=jnp.float32).astype(
            jnp.bfloat16
        )
        values_low = (
            jnp.dot(token_rows, wv_full, preferred_element_type=jnp.float32) + b_value
        ).astype(jnp.bfloat16)
        per_seq = (
            queries.reshape(seq_here, length, local_width),
            keys_low.reshape(seq_here, length, local_width),
            values_low.reshape(seq_here, length, local_width),
            labels,
        )
        attended, logsums = lax.map(forward_fn, per_seq)
        attended_rows = attended.reshape(rows_count, local_width)
        mixed_part = jnp.dot(attended_rows, wm_full, preferred_element_type=jnp.float32).reshape(
            seq_here, length, model_width
        )
        mixed_sum = lax.psum_scatter(mixed_part, "tensor", scatter_dimension=1, tiled=True)
        first_sum = x_here.astype(jnp.float32) + mixed_sum + b_mixer
        normed, first_back = jax.vjp(normalize, first_sum, gain_one, bias_one)
        normed_all = lax.all_gather(normed.astype(jnp.bfloat16), "tensor", axis=1, tiled=True)
        normed_rows = normed_all.reshape(rows_count, model_width)
        inner_pre = jnp.dot(normed_rows, wi_full, preferred_element_type=jnp.float32) + b_inner
        hidden_full, gelu_back = jax.vjp(exact_gelu, inner_pre)
        hidden = hidden_full.astype(jnp.bfloat16)
        outer_part = jnp.dot(hidden, wo_full, preferred_element_type=jnp.float32).reshape(
            seq_here, length, model_width
        )
        outer_sum = lax.psum_scatter(
            outer_part.astype(jnp.bfloat16), "tensor", scatter_dimension=1, tiled=True
        ).astype(jnp.float32)
        second = normed + outer_sum + b_outer
        finished, second_back = jax.vjp(normalize, second, gain_two, bias_two)
        results.append(finished.astype(jnp.bfloat16))
        wq_full, wk_full, wv_full, wm_full, wi_full, wo_full = (
            lax.all_gather(shards[0], "dp", axis=0, tiled=True),
            lax.all_gather(shards[1], "dp", axis=0, tiled=True),
            lax.all_gather(shards[2], "dp", axis=0, tiled=True),
            lax.all_gather(shards[3], "dp", axis=1, tiled=True),
            lax.all_gather(shards[4], "dp", axis=0, tiled=True),
            lax.all_gather(shards[5], "dp", axis=1, tiled=True),
        )
        d_second, d_gain_two, d_bias_two = second_back(cotangent[batch_index].astype(jnp.float32))
        d_outer_all = lax.all_gather(d_second.astype(jnp.bfloat16), "tensor", axis=1, tiled=True)
        d_outer_rows = d_outer_all.reshape(rows_count, model_width)
        grad_outer = contract_rows(hidden, d_outer_rows)
        d_hidden = contract_cols(d_outer_rows, wo_full)
        d_inner = gelu_back(d_hidden)[0].astype(jnp.bfloat16)
        grad_inner = contract_rows(normed_rows, d_inner)
        d_normed_part = contract_cols(d_inner, wi_full).reshape(seq_here, length, model_width)
        d_normed = d_second + lax.psum_scatter(
            d_normed_part, "tensor", scatter_dimension=1, tiled=True
        )
        d_first, d_gain_one, d_bias_one = first_back(d_normed)
        d_mixed_all = lax.all_gather(d_first.astype(jnp.bfloat16), "tensor", axis=1, tiled=True)
        d_mixed_rows = d_mixed_all.reshape(rows_count, model_width)
        grad_mixer = contract_rows(attended_rows, d_mixed_rows)
        d_attended = contract_cols(d_mixed_rows, wm_full).astype(jnp.bfloat16)
        d_queries, d_keys, d_values = lax.map(
            backward_fn, per_seq + (logsums, d_attended.reshape(seq_here, length, local_width))
        )
        dq_rows = d_queries.reshape(rows_count, local_width)
        dk_rows = d_keys.reshape(rows_count, local_width)
        dv_rows = d_values.reshape(rows_count, local_width)
        grad_query = contract_rows(token_rows, dq_rows)
        grad_key = contract_rows(token_rows, dk_rows)
        grad_value = contract_rows(token_rows, dv_rows)
        d_rows = (
            contract_cols(dq_rows, wq_full)
            + contract_cols(dk_rows, wk_full)
            + contract_cols(dv_rows, wv_full)
        )
        d_token_part = d_rows.reshape(seq_here, length, model_width)
        token_grads.append(
            d_first
            + lax.psum_scatter(
                d_token_part.astype(jnp.bfloat16), "tensor", scatter_dimension=1, tiled=True
            ).astype(jnp.float32)
        )
        step_small = (
            jnp.sum(dq_rows.astype(jnp.float32), axis=0),
            jnp.sum(dv_rows.astype(jnp.float32), axis=0),
            jnp.sum(d_inner.astype(jnp.float32), axis=0),
            jnp.sum(d_first, axis=(0, 1)),
            d_gain_one,
            d_bias_one,
            jnp.sum(d_second, axis=(0, 1)),
            d_gain_two,
            d_bias_two,
        )
        small_sums = tuple(
            (summed_old + added_new for summed_old, added_new in zip(small_sums, step_small))
        )
        step_grads = (grad_query, grad_key, grad_value, grad_mixer, grad_inner, grad_outer)
        reduced = (
            lax.psum_scatter(step_grads[0], "dp", scatter_dimension=0, tiled=True),
            lax.psum_scatter(step_grads[1], "dp", scatter_dimension=0, tiled=True),
            lax.psum_scatter(step_grads[2], "dp", scatter_dimension=0, tiled=True),
            lax.psum_scatter(step_grads[3], "dp", scatter_dimension=1, tiled=True),
            lax.psum_scatter(step_grads[4], "dp", scatter_dimension=0, tiled=True),
            lax.psum_scatter(step_grads[5], "dp", scatter_dimension=1, tiled=True),
        )
        sum_grads = tuple(
            (summed_old + added_new for summed_old, added_new in zip(sum_grads, reduced))
        )
    tensor_index = lax.axis_index("tensor")
    groups_count = lax.axis_size("tensor")

    def widen_slice(part_vec, full_len):
        return lax.dynamic_update_slice(
            jnp.zeros((full_len,), jnp.float32), part_vec, (tensor_index * part_vec.shape[0],)
        )

    def narrow_slice(full_vec, piece_len):
        return lax.dynamic_slice_in_dim(full_vec, tensor_index * piece_len, piece_len)

    widened = (
        widen_slice(small_sums[0], local_width * groups_count),
        widen_slice(small_sums[1], local_width * groups_count),
        widen_slice(small_sums[2], local_hidden * groups_count),
    ) + small_sums[3:]
    summed = lax.psum(widened, ("dp", "tensor"))
    return (
        jnp.stack(results),
        jnp.stack(token_grads),
        sum_grads[0],
        narrow_slice(summed[0], local_width),
        sum_grads[1],
        sum_grads[2],
        narrow_slice(summed[1], local_width),
        sum_grads[3],
        summed[3],
        summed[4],
        summed[5],
        sum_grads[4],
        narrow_slice(summed[2], local_hidden),
        sum_grads[5],
        summed[6],
        summed[7],
        summed[8],
    )


def solution(mesh):
    placed = (
        P(None, "dp", "tensor", None),
        P(None, "dp", None),
        P("dp", "tensor"),
        P("tensor"),
        P("dp", "tensor"),
        P("dp", "tensor"),
        P("tensor"),
        P("tensor", "dp"),
        P(),
        P(),
        P(),
        P("dp", "tensor"),
        P("tensor"),
        P("tensor", "dp"),
        P(),
        P(),
        P(),
        P(None, "dp", "tensor", None),
    )
    return jax.shard_map(
        body,
        mesh=mesh,
        in_specs=placed,
        out_specs=(
            P(None, "dp", "tensor", None),
            P(None, "dp", "tensor", None),
            P("dp", "tensor"),
            P("tensor"),
            P("dp", "tensor"),
            P("dp", "tensor"),
            P("tensor"),
            P("tensor", "dp"),
            P(),
            P(),
            P(),
            P("dp", "tensor"),
            P("tensor"),
            P("tensor", "dp"),
            P(),
            P(),
            P(),
        ),
        check_vma=False,
    )
```

profile of v0, /device:TPU:0, one launch (start us, length us, event | category | flops | bytes accessed | tf_op | source)
XLA Modules:
  0.0 1432.1 jit_solution(14090708128089291211)
XLA Ops:
  12.9 33.1 %all_gather.48 = bf16[192,768]{0,1:T(8,128)(2,1)S(1)} all-gather(bf16[192,96]{0,1:T(8,128)(2,1)S(1)} %copy.55), channel_id=1, replica_groups=mesh['dp'=8,'tensor'=4] {'dp'}, dimensions={1}, use_global_device_ids=true | all-gather | bytes 331776 | tf_op jit(solution)/shard_map/all_gather | solution.py:131
  46.0 31.0 %all_gather.46 = bf16[768,192]{1,0:T(8,128)(2,1)S(1)} all-gather(bf16[96,192]{1,0:T(8,128)(2,1)S(1)} %copy-done.119), channel_id=1, replica_groups=mesh['dp'=8,'tensor'=4] {'dp'}, dimensions={0}, use_global_device_ids=true | all-gather | bytes 331776 | tf_op jit(solution)/shard_map/all_gather | solution.py:128
  77.0 31.1 %all_gather.47 = bf16[768,192]{1,0:T(8,128)(2,1)S(1)} all-gather(bf16[96,192]{1,0:T(8,128)(2,1)S(1)} %copy-done.120), channel_id=1, replica_groups=mesh['dp'=8,'tensor'=4] {'dp'}, dimensions={0}, use_global_device_ids=true | all-gather | bytes 331776 | tf_op jit(solution)/shard_map/all_gather | solution.py:129
  108.1 31.0 %all_gather.45 = bf16[768,192]{1,0:T(8,128)(2,1)S(1)} all-gather(bf16[96,192]{1,0:T(8,128)(2,1)S(1)} %copy-done.121), channel_id=1, replica_groups=mesh['dp'=8,'tensor'=4] {'dp'}, dimensions={0}, use_global_device_ids=true | all-gather | bytes 331776 | tf_op jit(solution)/shard_map/all_gather | solution.py:130
  217.4 19.8 %reduce-scatter.35.cloned.1.call-done = f32[1,256,768]{2,1,0:T(8,128)} async-done(((f32[1,1024,768]{2,1,0:T(8,128)}), f32[1,256,768]{2,1,0:T(8,128)}) %reduce-scatter.35.cloned.1.call-update) | async-done | bytes 786448 | tf_op jit(solution)/shard_map/reduce_scatter | solution.py:160
  237.3 40.6 %reduce-scatter.43.cloned.1.call-done = f32[1,256,768]{2,1,0:T(8,128)} async-done(((f32[1,1024,768]{2,1,0:T(8,128)}), f32[1,256,768]{2,1,0:T(8,128)}) %reduce-scatter.43.cloned.1.call-update) | async-done | bytes 786448 | tf_op jit(solution)/shard_map/reduce_scatter | solution.py:160
  277.8 40.7 %reduce-scatter.39.cloned.1.call-done = f32[1,256,768]{2,1,0:T(8,128)} async-done(((f32[1,1024,768]{2,1,0:T(8,128)}), f32[1,256,768]{2,1,0:T(8,128)}) %reduce-scatter.39.cloned.1.call-update) | async-done | bytes 786448 | tf_op jit(solution)/shard_map/reduce_scatter | solution.py:160
  326.2 17.3 %all-gather.31.cloned.1.call-done = bf16[1,1024,768]{2,1,0:T(8,128)(2,1)} async-done(((bf16[1,256,768]{2,1,0:T(8,128)(2,1)}), bf16[1,1024,768]{2,1,0:T(8,128)(2,1)}) %all-gather.31.cloned.1.call-update) | async-done | bytes 1572880 | tf_op jit(solution)/shard_map/all_gather | solution.py:163
  348.3 16.2 %all-gather.29.cloned.1.call-done = bf16[1,1024,768]{2,1,0:T(8,128)(2,1)} async-done(((bf16[1,256,768]{2,1,0:T(8,128)(2,1)}), bf16[1,1024,768]{2,1,0:T(8,128)(2,1)}) %all-gather.29.cloned.1.call-update) | async-done | bytes 1572880 | tf_op jit(solution)/shard_map/all_gather | solution.py:163
  369.3 16.8 %all-gather.23.cloned.1.call-done = bf16[1,1024,768]{2,1,0:T(8,128)(2,1)} async-done(((bf16[1,256,768]{2,1,0:T(8,128)(2,1)}), bf16[1,1024,768]{2,1,0:T(8,128)(2,1)}) %all-gather.23.cloned.1.call-update) | async-done | bytes 1572880 | tf_op jit(solution)/shard_map/all_gather | solution.py:163
  386.2 25.4 %multiply_convert_fusion.7 = (bf16[1024,768]{1,0:T(8,128)(2,1)}, f32[1024,768]{1,0:T(8,128)}, bf16[1024,768]{1,0:T(8,128)(2,1)}, f32[1024,768]{1,0:T(8,128)}, bf...) fusion(f32[768]{0:T(1024)S(1)} %copy-done.185, f32[1024,768]{1,0:T(8,128)} %fusion.106, ...), kind=kOutput, calls=%fused_computation.104 | convolution fusion | flops 1363673088 | bytes 26348544 | tf_op jit(solution)/shard_map/dot_general | solution.py:165
  411.6 18.3 %all-gather.27.cloned.1.call-done = bf16[768,768]{0,1:T(8,128)(2,1)} async-done(((bf16[768,96]{0,1:T(8,128)(2,1)}), bf16[768,768]{0,1:T(8,128)(2,1)}) %all-gather.27.cloned.1.call-update) | async-done | bytes 1179664 | tf_op jit(solution)/shard_map/all_gather | solution.py:133
  443.6 17.3 %reduce-scatter.33.cloned.1.call-done = bf16[1,256,768]{2,1,0:T(8,128)(2,1)} async-done(((bf16[1,1024,768]{2,1,0:T(8,128)(2,1)}), bf16[1,256,768]{2,1,0:T(8,128)(2,1)}) %reduce-scatter.33.cloned.1.call-update) | async-done | bytes 393232 | tf_op jit(solution)/shard_map/reduce_scatter | solution.py:171
  461.0 30.7 %reduce-scatter.41.cloned.1.call-done = bf16[1,256,768]{2,1,0:T(8,128)(2,1)} async-done(((bf16[1,1024,768]{2,1,0:T(8,128)(2,1)}), bf16[1,256,768]{2,1,0:T(8,128)(2,1)}) %reduce-scatter.41.cloned.1.call-update) | async-done | bytes 393232 | tf_op jit(solution)/shard_map/reduce_scatter | solution.py:171
  491.7 30.5 %reduce-scatter.37.cloned.1.call-done = bf16[1,256,768]{2,1,0:T(8,128)(2,1)} async-done(((bf16[1,1024,768]{2,1,0:T(8,128)(2,1)}), bf16[1,256,768]{2,1,0:T(8,128)(2,1)}) %reduce-scatter.37.cloned.1.call-update) | async-done | bytes 393232 | tf_op jit(solution)/shard_map/reduce_scatter | solution.py:171
  526.0 19.4 %all-gather.33.cloned.1.call-done = bf16[1,1024,768]{2,1,0:T(8,128)(2,1)} async-done(((bf16[1,256,768]{2,1,0:T(8,128)(2,1)}), bf16[1,1024,768]{2,1,0:T(8,128)(2,1)}) %all-gather.33.cloned.1.call-update) | async-done | bytes 1572880 | tf_op jit(solution)/shard_map/all_gather | solution.py:163
  545.3 11.0 multiply_convert_fusion.4
  564.3 24.0 %reduce-scatter.45.cloned.1.call-done = bf16[1,256,768]{2,1,0:T(8,128)(2,1)} async-done(((bf16[1,1024,768]{2,1,0:T(8,128)(2,1)}), bf16[1,256,768]{2,1,0:T(8,128)(2,1)}) %reduce-scatter.45.cloned.1.call-update) | async-done | bytes 393232 | tf_op jit(solution)/shard_map/reduce_scatter | solution.py:171
  608.5 10.1 all-gather.39.cloned.1.call-done
  650.6 26.5 %all-gather.35.cloned.1.call-done = bf16[1,1024,768]{2,1,0:T(8,128)(2,1)} async-done(((bf16[1,256,768]{2,1,0:T(8,128)(2,1)}), bf16[1,1024,768]{2,1,0:T(8,128)(2,1)}) %all-gather.35.cloned.1.call-update) | async-done | bytes 1572880 | tf_op jit(solution)/shard_map/all_gather | solution.py:186
  718.2 36.4 %reduce-scatter.47.cloned.1.call-done = f32[1,256,768]{2,1,0:T(8,128)} async-done(((f32[1,1024,768]{2,1,0:T(8,128)}), f32[1,256,768]{2,1,0:T(8,128)}) %reduce-scatter.47.cloned.1.call-update) | async-done | bytes 786448 | tf_op jit(solution)/shard_map/reduce_scatter | solution.py:193
  754.6 41.1 %reduce-scatter.55.cloned.1.call-done = f32[1,256,768]{2,1,0:T(8,128)} async-done(((f32[1,1024,768]{2,1,0:T(8,128)}), f32[1,256,768]{2,1,0:T(8,128)}) %reduce-scatter.55.cloned.1.call-update) | async-done | bytes 786448 | tf_op jit(solution)/shard_map/reduce_scatter | solution.py:193
  811.5 12.9 all-gather.37.cloned.1.call-done
  835.3 10.7 all-gather.49.cloned.1.call-done
  848.7 18.4 %all-gather.45.cloned.1.call-done = bf16[1,1024,768]{2,1,0:T(8,128)(2,1)} async-done(((bf16[1,256,768]{2,1,0:T(8,128)(2,1)}), bf16[1,1024,768]{2,1,0:T(8,128)(2,1)}) %all-gather.45.cloned.1.call-update) | async-done | bytes 1572880 | tf_op jit(solution)/shard_map/all_gather | solution.py:197
  869.8 10.2 multiply_convert_fusion.3
  1038.6 41.6 %all-reduce = (f32[768]{0:T(1024)}, f32[768]{0:T(1024)}, f32[768]{0:T(1024)}, f32[768]{0:T(1024)}, f32[768]{0:T(1024)}, /*index=5*/f32[3072]{0:T(1024)}, f32[768]{0:T(1024)}, f32[768]{0:T(1024)}, f32[768]{0:T(1024)}) all-reduce(f32[768]{0:T(1024)} %dynamic_update_slice.51, ...), channel_id=1, replica_groups=mesh['dp'=8,'tensor'=4] {'dp','tensor'}, use_global_device_ids=true, to_apply=%region_68.69 | all-reduce | flops 9216 | bytes 73728 | tf_op jit(solution)/shard_map/psum | solution.py:264
  1110.3 44.5 %reduce-scatter.65.cloned.1.call-done = f32[768,96]{0,1:T(8,128)} async-done(((f32[768,768]{0,1:T(8,128)}), f32[768,96]{0,1:T(8,128)}) %reduce-scatter.65.cloned.1.call-update) | async-done | bytes 294928 | tf_op jit(solution)/shard_map/reduce_scatter | solution.py:243
  1154.8 72.3 %reduce-scatter.63.cloned.1.call-done = f32[96,768]{1,0:T(8,128)} async-done(((f32[768,768]{1,0:T(8,128)}), f32[96,768]{1,0:T(8,128)}) %reduce-scatter.63.cloned.1.call-update) | async-done | bytes 294928 | tf_op jit(solution)/shard_map/reduce_scatter | solution.py:242
  1227.1 65.9 %reduce-scatter.71.cloned.1.call-done = f32[96,192]{1,0:T(8,128)} async-done(((f32[768,192]{1,0:T(8,128)}), f32[96,192]{1,0:T(8,128)}) %reduce-scatter.71.cloned.1.call-update) | async-done | bytes 73744
  1293.0 65.6 %reduce-scatter.69.cloned.1.call-done = f32[96,192]{1,0:T(8,128)} async-done(((f32[768,192]{1,0:T(8,128)}), f32[96,192]{1,0:T(8,128)}) %reduce-scatter.69.cloned.1.call-update) | async-done | bytes 73744
  1358.5 65.7 %reduce-scatter.67.cloned.1.call-done = f32[96,192]{1,0:T(8,128)} async-done(((f32[768,192]{1,0:T(8,128)}), f32[96,192]{1,0:T(8,128)}) %reduce-scatter.67.cloned.1.call-update) | async-done | bytes 73744
  (705 shorter events, 437.1 us)
Async XLA Ops:
  8.1 131.6 %all-gather.51.cloned.1.call-start = ((), (), s32[]{:S(2)}) async-start(), calls=%async_computation.52 | async-start | bytes 1966080 | tf_op jit(solution)/shard_map/all_gather | solution.py:138
  10.7 147.8 %all-gather.53.cloned.1.call-start = ((), (), s32[]{:S(2)}) async-start(), calls=%async_computation.53 | async-start | bytes 1966080 | tf_op jit(solution)/shard_map/all_gather | solution.py:138
  11.4 166.6 %all-gather.57.cloned.1.call-start = ((), (), s32[]{:S(2)}) async-start(), calls=%async_computation.55 | async-start | bytes 1966080 | tf_op jit(solution)/shard_map/all_gather | solution.py:138
  12.2 185.6 %all-gather.55.cloned.1.call-start = ((), (), s32[]{:S(2)}) async-start(), calls=%async_computation.54 | async-start | bytes 1966080 | tf_op jit(solution)/shard_map/all_gather | solution.py:138
  12.8 204.7 %reduce-scatter.31.cloned.1.call-start = ((), (), s32[]{:S(2)}) async-start(), calls=%async_computation.22 | async-start | bytes 3932160 | tf_op jit(solution)/shard_map/reduce_scatter | solution.py:160
  157.5 79.7 %reduce-scatter.35.cloned.1.call-start = ((), (), s32[]{:S(2)}) async-start(), calls=%async_computation.27 | async-start | bytes 3932160 | tf_op jit(solution)/shard_map/reduce_scatter | solution.py:160
  177.1 100.7 %reduce-scatter.43.cloned.1.call-start = ((), (), s32[]{:S(2)}) async-start(), calls=%async_computation.33 | async-start | bytes 3932160 | tf_op jit(solution)/shard_map/reduce_scatter | solution.py:160
  196.6 121.9 %reduce-scatter.39.cloned.1.call-start = ((), (), s32[]{:S(2)}) async-start(), calls=%async_computation.30 | async-start | bytes 3932160 | tf_op jit(solution)/shard_map/reduce_scatter | solution.py:160
  216.8 109.5 %all-gather.25.cloned.1.call-start = ((), (), s32[]{:S(2)}) async-start(), calls=%async_computation.24 | async-start | bytes 1327104 | tf_op jit(solution)/shard_map/all_gather | solution.py:132
  217.4 126.1 %all-gather.31.cloned.1.call-start = ((), (), s32[]{:S(2)}) async-start(), calls=%async_computation.31 | async-start | bytes 1966080 | tf_op jit(solution)/shard_map/all_gather | solution.py:163
  325.2 104.7 %all-gather.27.cloned.1.call-start = ((), (), s32[]{:S(2)}) async-start(), calls=%async_computation.25 | async-start | bytes 1327104 | tf_op jit(solution)/shard_map/all_gather | solution.py:133
  326.0 135.0 %reduce-scatter.33.cloned.1.call-start = ((), (), s32[]{:S(2)}) async-start(), calls=%async_computation.26 | async-start | bytes 1966080 | tf_op jit(solution)/shard_map/reduce_scatter | solution.py:171
  438.7 83.5 %reduce-scatter.37.cloned.1.call-start = ((), (), s32[]{:S(2)}) async-start(), calls=%async_computation.29 | async-start | bytes 1966080 | tf_op jit(solution)/shard_map/reduce_scatter | solution.py:171
  443.3 102.0 %all-gather.33.cloned.1.call-start = ((), (), s32[]{:S(2)}) async-start(), calls=%async_computation.34 | async-start | bytes 1966080 | tf_op jit(solution)/shard_map/all_gather | solution.py:163
  603.1 74.1 %all-gather.35.cloned.1.call-start = ((), (), s32[]{:S(2)}) async-start(), calls=%async_computation.36 | async-start | bytes 1966080 | tf_op jit(solution)/shard_map/all_gather | solution.py:186
  605.8 91.9 %all-gather.43.cloned.1.call-start = ((), (), s32[]{:S(2)}) async-start(), calls=%async_computation.44 | async-start | bytes 1966080 | tf_op jit(solution)/shard_map/all_gather | solution.py:186
  608.5 100.3 %reduce-scatter.51.cloned.1.call-start = ((), (), s32[]{:S(2)}) async-start(), calls=%async_computation.41 | async-start | bytes 3932160 | tf_op jit(solution)/shard_map/reduce_scatter | solution.py:193
  629.6 84.5 %reduce-scatter.59.cloned.1.call-start = ((), (), s32[]{:S(2)}) async-start(), calls=%async_computation.49 | async-start | bytes 3932160 | tf_op jit(solution)/shard_map/reduce_scatter | solution.py:193
  650.6 104.0 %reduce-scatter.47.cloned.1.call-start = ((), (), s32[]{:S(2)}) async-start(), calls=%async_computation.37 | async-start | bytes 3932160 | tf_op jit(solution)/shard_map/reduce_scatter | solution.py:193
  688.9 106.8 %reduce-scatter.55.cloned.1.call-start = ((), (), s32[]{:S(2)}) async-start(), calls=%async_computation.45 | async-start | bytes 3932160 | tf_op jit(solution)/shard_map/reduce_scatter | solution.py:193
  708.5 115.8 %all-gather.37.cloned.1.call-start = ((), (), s32[]{:S(2)}) async-start(), calls=%async_computation.38 | async-start | bytes 1966080 | tf_op jit(solution)/shard_map/all_gather | solution.py:197
  808.5 79.8 %all-gather.41.cloned.1.call-start = ((), (), s32[]{:S(2)}) async-start(), calls=%async_computation.42 | async-start | bytes 1966080 | tf_op jit(solution)/shard_map/all_gather | solution.py:197
  811.4 286.6 %reduce-scatter.73.cloned.1.call-start = ((), (), s32[]{:S(2)}) async-start(), calls=%async_computation.61 | async-start | bytes 884736
  895.2 204.5 %reduce-scatter.49.cloned.1.call-start = ((), (), s32[]{:S(2)}) async-start(), calls=%async_computation.39 | async-start | bytes 1966080 | tf_op jit(solution)/shard_map/reduce_scatter | solution.py:218
  907.7 194.0 %reduce-scatter.53.cloned.1.call-start = ((), (), s32[]{:S(2)}) async-start(), calls=%async_computation.43 | async-start | bytes 1966080 | tf_op jit(solution)/shard_map/reduce_scatter | solution.py:218
  936.3 167.6 %reduce-scatter.57.cloned.1.call-start = ((), (), s32[]{:S(2)}) async-start(), calls=%async_computation.47 | async-start | bytes 1966080 | tf_op jit(solution)/shard_map/reduce_scatter | solution.py:218
  965.2 140.9 %reduce-scatter.61.cloned.1.call-start = ((), (), s32[]{:S(2)}) async-start(), calls=%async_computation.51 | async-start | bytes 1966080 | tf_op jit(solution)/shard_map/reduce_scatter | solution.py:218
  994.2 160.5 %reduce-scatter.65.cloned.1.call-start = ((), (), s32[]{:S(2)}) async-start(), calls=%async_computation.57 | async-start | bytes 2654208 | tf_op jit(solution)/shard_map/reduce_scatter | solution.py:243
  1004.7 222.4 %reduce-scatter.63.cloned.1.call-start = ((), (), s32[]{:S(2)}) async-start(), calls=%async_computation.56 | async-start | bytes 2654208 | tf_op jit(solution)/shard_map/reduce_scatter | solution.py:242
  1014.8 278.2 %reduce-scatter.71.cloned.1.call-start = ((), (), s32[]{:S(2)}) async-start(), calls=%async_computation.60 | async-start | bytes 884736
  1084.2 274.4 %reduce-scatter.69.cloned.1.call-start = ((), (), s32[]{:S(2)}) async-start(), calls=%async_computation.59 | async-start | bytes 884736
  1091.0 333.3 %reduce-scatter.67.cloned.1.call-start = ((), (), s32[]{:S(2)}) async-start(), calls=%async_computation.58 | async-start | bytes 884736
  (211 other events, 2780.5 us)
Sparse Core Ops, SparseCore 0:
  11.0 22.3 all-gather.50
  35.0 19.6 all-gather.52
  56.2 19.6 all-gather.56
  77.4 19.6 all-gather.54
  157.6 39.0 reduce-scatter.30
  199.3 37.9 reduce-scatter.34
  239.8 37.9 reduce-scatter.42
  280.5 37.9 reduce-scatter.38
  629.7 38.1 reduce-scatter.50
  670.4 43.5 reduce-scatter.58
  716.6 37.9 reduce-scatter.46
  757.7 37.9 reduce-scatter.54
Sparse Core Ops, SparseCore 1:
  219.4 42.5 all-gather.24
  324.0 19.5 all-gather.30
  344.9 19.5 all-gather.28
  366.6 19.5 all-gather.22
  388.4 41.5 all-gather.26
  434.4 26.5 reduce-scatter.32
  463.5 28.1 reduce-scatter.40
  494.1 28.1 reduce-scatter.36
  525.8 19.5 all-gather.32
  560.2 28.1 reduce-scatter.44
  599.1 19.5 all-gather.38
  620.2 19.5 all-gather.46
  641.2 35.9 all-gather.34
  678.7 18.9 all-gather.42
  804.8 19.5 all-gather.36
  826.5 19.5 all-gather.48
  847.6 19.5 all-gather.44
  868.7 19.5 all-gather.40
  895.3 62.5 reduce-scatter.72
  960.6 27.1 reduce-scatter.48
  990.1 28.1 reduce-scatter.52
  1020.8 28.6 reduce-scatter.56
  1052.5 28.7 reduce-scatter.60
  1085.8 68.9 reduce-scatter.64
  1159.1 67.9 reduce-scatter.62
  1231.3 61.6 reduce-scatter.70
  1296.9 61.6 reduce-scatter.68
  1362.6 61.6 reduce-scatter.66
where the time goes:
time: 1440 us; the launch traced here: 1430 us
  waiting for transfers between devices  794 us (55%)
  matrix products  282 us (20%)
  blocking collectives  168 us (12%)
  other arithmetic  102 us (7%)
  local copies, waits for them, and re-layouts  61.9 us (4%)
  between operations  19.1 us (1%)
    unnamed x44, waiting for transfers between devices  202 us
    reduce_scatter x4, waiting for transfers between devices, body(): lax.psum_scatter(outer_part.astype(jnp.bfloat16), 'tensor', scatter_dimen...  103 us
    reduce_scatter x4, waiting for transfers between devices, body(): lax.psum_scatter(mixed_part, 'tensor', scatter_dimension=1, tiled=True)  101 us
    reduce_scatter x4, waiting for transfers between devices, body(): lax.psum_scatter(d_normed_part, 'tensor', scatter_dimension=1, tiled=True)  82.8 us
    reduce_scatter x1, waiting for transfers between devices, body(): lax.psum_scatter(step_grads[4], 'dp', scatter_dimension=0, tiled=True)  72.3 us
    all_gather x4, waiting for transfers between devices, body(): lax.all_gather(normed.astype(jnp.bfloat16), 'tensor', axis=1, tiled=True)  69.6 us
    dot_general x24, matrix products, contract_cols(): lax.dot_general(left, right, (((1,), (1,)), ((), ())), preferred_element_...  56.8 us
    all_gather x4, waiting for transfers between devices, body(): lax.all_gather(d_second.astype(jnp.bfloat16), 'tensor', axis=1, tiled=True)  55.1 us
  transfers between devices with their start and end apart: 40, of which 28 were waited for; matrix products, arithmetic and copies ran while one was open for 25% of the time, Pallas kernels for 0%

commit v1 on v0

v1 whole, which is shorter than its diff:
```python
from functools import partial

import jax
import jax.numpy as jnp
from jax import lax
from jax.experimental import pallas as pl
from jax.experimental.pallas import tpu as pltpu
from jax.sharding import PartitionSpec as P

HEAD = 64
DOCS = 8
PAD = 256
ROWS = 256
LOG2E = 1.4426950408889634
EPS = 1e-12
F32 = jnp.float32
BF16 = jnp.bfloat16


def dot_nn(left, right):
    return lax.dot_general(left, right, (((1,), (0,)), ((), ())), preferred_element_type=F32)


def dot_nt(left, right):
    return lax.dot_general(left, right, (((1,), (1,)), ((), ())), preferred_element_type=F32)


def rows_of(index, size=ROWS):
    return pl.ds(pl.multiple_of(index * size, size), size)


def lane_index(shape):
    return lax.broadcasted_iota(jnp.int32, shape, 1)


def three_parts(values):
    high = values.astype(BF16)
    rest = values - high.astype(F32)
    middle = rest.astype(BF16)
    low = (rest - middle.astype(F32)).astype(BF16)
    return high, middle, low


def head_only(lanes, head):
    return (lanes >= head * HEAD) & (lanes < (head + 1) * HEAD)


def head_and_extra(lanes, head, width):
    extra = width + DOCS + 3 * head
    return (
        head_only(lanes, head)
        | ((lanes >= width) & (lanes < width + DOCS))
        | ((lanes >= extra) & (lanes < extra + 3))
    )


def unpack(block_ref, slot, width):
    part = block_ref[:, slot * width : (slot + 1) * width]
    return jnp.concatenate([part, jnp.zeros((part.shape[0], PAD - width), part.dtype)], axis=1)


def attend_kernel(
    x_ref, a_ref, bq_ref, bv_ref, qaug_ref, kaug_ref, vaug_ref, bm_ref,
    q_ref, k_ref, v_ref, att_ref, first_ref, w_s,
):
    step = pl.program_id(0)
    length, model = x_ref.shape
    width = a_ref.shape[2] // 4
    heads = width // HEAD
    blocks = length // ROWS
    for slot in range(4):
        w_s[slot] = unpack(a_ref.at[0], slot, width)

    @pl.when(step == 0)
    def _():
        first_ref[...] = x_ref[...].astype(F32) + bm_ref[...]

    @pl.loop(0, blocks)
    def _(index):
        rows = rows_of(index)
        x_rows = x_ref[rows, :]
        queries = (dot_nn(x_rows, w_s[0]) + bq_ref[0]).astype(BF16)
        q_ref[0, rows, :] = queries * jnp.asarray(HEAD**-0.5, BF16) + qaug_ref[rows, :]
        keys = dot_nn(x_rows, w_s[1]).astype(BF16)
        k_ref[0, rows, :] = keys + kaug_ref[rows, :]
        values = (dot_nn(x_rows, w_s[2]) + bv_ref[0]).astype(BF16)
        v_ref[0, rows, :] = values + vaug_ref[...]

    @pl.loop(0, blocks)
    def _(index):
        rows = rows_of(index)
        lanes = lane_index((ROWS, PAD))
        queries = q_ref[0, rows, :]
        attended = jnp.zeros((ROWS, PAD), F32)
        extended = queries
        for head in range(heads):
            masked = jnp.where(head_and_extra(lanes, head, width), queries, 0)
            scores = dot_nt(masked, k_ref[0])
            highest = jnp.max(scores, axis=1, keepdims=True)
            raw = jnp.exp2((scores - highest) * LOG2E).astype(BF16)
            mixed = dot_nn(raw, v_ref[0])
            total = mixed[:, width : width + 1]
            attended = jnp.where(head_only(lanes, head), mixed / total, attended)
            parts = three_parts(-(highest + jnp.log(total)))
            for place, part in enumerate(parts):
                here = lanes == width + DOCS + 3 * head + place
                extended = jnp.where(here, jnp.broadcast_to(part, (ROWS, PAD)), extended)
        q_ref[0, rows, :] = extended
        attended = attended.astype(BF16)
        att_ref[0, rows, :] = attended
        first_ref[rows, :] += dot_nt(attended, w_s[3])


def gelu_parts(values):
    phi = jnp.exp2(values * values * (-0.5 * LOG2E)) * 0.3989422804014327
    total = 0.5 + 0.5 * lax.erf(values * 0.7071067811865476)
    return values * total, total + values * phi


def norm_parts(values):
    average = jnp.mean(values, axis=-1, keepdims=True)
    centred = values - average
    spread = jnp.mean(centred * centred, axis=-1, keepdims=True)
    inverse = lax.rsqrt(spread + EPS)
    return centred * inverse, inverse


def norm_back(grads, gain, unit, inverse):
    scaled = grads * gain
    average = jnp.mean(scaled, axis=-1, keepdims=True)
    along = jnp.mean(scaled * unit, axis=-1, keepdims=True)
    return (scaled - average - unit * along) * inverse


def column_sum(values):
    return jnp.sum(values, axis=0, keepdims=True)


def dense_kernel(
    first_in, wi_ref, wo_ref, bi_ref, vec_ref, cot_ref,
    out_ref, dfirst_ref, dmix_ref, gi_ref, go_ref, dbi_ref, small_ref,
    first_ref, second_ref, normed_s, dsec_s, hidden_s, slope_s, low_s, low_t, back_t, dinner_s,
):
    step = pl.program_id(0)
    count = pl.num_programs(0) // 2
    length, model = first_in.shape
    blocks = length // ROWS
    gain_one, bias_one, b_outer, gain_two, bias_two = (vec_ref[i : i + 1, :] for i in range(5))

    @pl.when(step == 0)
    def _():
        copied = pltpu.sync_copy
        copied(first_in, first_ref)

        @pl.loop(0, blocks)
        def _(index):
            rows = rows_of(index)
            unit, _inverse = norm_parts(first_ref[rows, :])
            normed = unit * gain_one + bias_one
            normed_s[rows, :] = normed
            low_s[rows, :] = normed.astype(BF16)
            low_t[:, rows] = normed.astype(BF16).T
            second_ref[rows, :] = normed + b_outer

    @pl.when(step < count)
    def _():
        @pl.loop(0, blocks)
        def _(index):
            rows = rows_of(index)
            inner = dot_nn(low_s[rows, :], wi_ref[0]) + bi_ref[0]
            value, slope = gelu_parts(inner)
            hidden = value.astype(BF16)
            hidden_s[step, rows, :] = hidden
            slope_s[step, rows, :] = slope.astype(BF16)
            second_ref[rows, :] += dot_nt(hidden, wo_ref[0])

    @pl.when(step == count - 1)
    def _():
        small_ref[...] = jnp.zeros_like(small_ref)

        @pl.loop(0, blocks)
        def _(index):
            rows = rows_of(index)
            unit, inverse = norm_parts(second_ref[rows, :])
            out_ref[rows, :] = (unit * gain_two + bias_two).astype(BF16)
            grads = cot_ref[rows, :].astype(F32)
            d_second = norm_back(grads, gain_two, unit, inverse)
            small_ref[0:1, :] += column_sum(d_second)
            small_ref[1:2, :] += column_sum(grads * unit)
            small_ref[2:3, :] += column_sum(grads)
            dsec_s[rows, :] = d_second
            low = d_second.astype(BF16)
            dmix_ref[rows, :] = low
            back_t[:, rows] = low.T

    @pl.when(step >= count)
    def _():
        place = step - count
        dbi_ref[...] = jnp.zeros_like(dbi_ref)

        @pl.loop(0, blocks)
        def _(index):
            rows = rows_of(index)
            d_hidden = dot_nn(dmix_ref[rows, :], wo_ref[0])
            d_inner = (d_hidden * slope_s[place, rows, :].astype(F32)).astype(BF16)
            dinner_s[rows, :] = d_inner
            dbi_ref[0] += column_sum(d_inner.astype(F32))
            dsec_s[rows, :] += dot_nt(d_inner, wi_ref[0])

        @pl.loop(0, model // ROWS)
        def _(index):
            rows = rows_of(index)
            gi_ref[0, rows, :] = dot_nn(low_t[rows, :], dinner_s[...]).astype(gi_ref.dtype)
            go_ref[0, rows, :] = dot_nn(back_t[rows, :], hidden_s[place]).astype(go_ref.dtype)

    @pl.when(step == 2 * count - 1)
    def _():
        @pl.loop(0, blocks)
        def _(index):
            rows = rows_of(index)
            unit, inverse = norm_parts(first_ref[rows, :])
            grads = dsec_s[rows, :]
            d_first = norm_back(grads, gain_one, unit, inverse)
            small_ref[3:4, :] += column_sum(d_first)
            small_ref[4:5, :] += column_sum(grads * unit)
            small_ref[5:6, :] += column_sum(grads)
            dfirst_ref[rows, :] = d_first
            dmix_ref[rows, :] = d_first.astype(BF16)


def attend_back_kernel(
    x_ref, a_ref, dmix_ref, dfirst_ref, q_ref, k_ref, v_ref, att_ref,
    dtok_ref, ga_ref, dbq_ref, dbv_ref,
    w_s, xt_s, dmixt_s, do_s, kt_s, dq_s, dk_s, dv_s, low_s,
):
    step = pl.program_id(0)
    length, model = x_ref.shape
    width = a_ref.shape[2] // 4
    heads = width // HEAD
    blocks = length // ROWS
    for slot in range(4):
        w_s[slot] = unpack(a_ref.at[0], slot, width)

    @pl.when(step == 0)
    def _():
        dtok_ref[...] = dfirst_ref[...]

        @pl.loop(0, blocks)
        def _(index):
            rows = rows_of(index)
            xt_s[:, rows] = x_ref[rows, :].T
            dmixt_s[:, rows] = dmix_ref[rows, :].T

    dk_s[...] = jnp.zeros_like(dk_s)
    dv_s[...] = jnp.zeros_like(dv_s)
    lanes = lane_index((ROWS, PAD))

    @pl.loop(0, blocks)
    def _(index):
        rows = rows_of(index)
        kt_s[:, rows] = k_ref[0, rows, :].T

    @pl.loop(0, blocks)
    def _(index):
        rows = rows_of(index)
        queries = q_ref[0, rows, :]
        d_att = dot_nn(dmix_ref[rows, :], w_s[3]).astype(BF16)
        product = d_att.astype(F32) * att_ref[0, rows, :].astype(F32)
        extended = d_att
        for head in range(heads):
            centre = jnp.sum(jnp.where(head_only(lanes, head), product, 0.0), axis=1, keepdims=True)
            for place, part in enumerate(three_parts(-centre)):
                here = lanes == width + DOCS + 3 * head + place
                extended = jnp.where(here, jnp.broadcast_to(part, (ROWS, PAD)), extended)
        chances_all = []
        d_scores_all = []
        d_att_all = []
        queries_all = []
        for head in range(heads):
            wide = head_and_extra(lanes, head, width)
            only = head_only(lanes, head)
            chances = jnp.exp2(dot_nt(k_ref[0], jnp.where(wide, queries, 0)) * LOG2E)
            d_chances = dot_nt(v_ref[0], jnp.where(wide, extended, 0))
            d_scores = (chances * d_chances).astype(BF16)
            chances_all.append(chances.astype(BF16))
            d_scores_all.append(d_scores)
            d_att_all.append(jnp.where(only, d_att, 0))
            queries_all.append(jnp.where(only, queries, 0))
            head_rows = slice(head * HEAD, (head + 1) * HEAD)
            dq_s[head_rows, rows] = dot_nn(kt_s[head_rows, :], d_scores)
        dv_s[...] += dot_nn(jnp.concatenate(chances_all, 1), jnp.concatenate(d_att_all, 0))
        dk_s[...] += dot_nn(jnp.concatenate(d_scores_all, 1), jnp.concatenate(queries_all, 0))

    dbq_ref[...] = jnp.zeros_like(dbq_ref)
    dbv_ref[...] = jnp.zeros_like(dbv_ref)

    @pl.loop(0, blocks)
    def _(index):
        rows = rows_of(index)
        d_query = (dq_s[:, rows].T * HEAD**-0.5).astype(BF16)
        d_query = jnp.where(lane_index(d_query.shape) < width, d_query, 0)
        d_key = dk_s[rows, :].astype(BF16)
        d_value = dv_s[rows, :].astype(BF16)
        low_s[0, rows, :] = d_query
        low_s[1, rows, :] = d_key
        low_s[2, rows, :] = d_value
        dbq_ref[0] += column_sum(d_query.astype(F32))
        dbv_ref[0] += column_sum(d_value.astype(F32))
        dtok_ref[rows, :] += (
            dot_nt(d_query, w_s[0]) + dot_nt(d_key, w_s[1]) + dot_nt(d_value, w_s[2])
        )

    @pl.loop(0, model // ROWS)
    def _(index):
        rows = rows_of(index)
        parts = [dot_nn(xt_s[rows, :], low_s[slot])[:, :width] for slot in range(3)]
        parts.append(dot_nn(dmixt_s[rows, :], att_ref[0])[:, :width])
        ga_ref[0, rows, :] = jnp.concatenate(parts, axis=1).astype(ga_ref.dtype)


VMEM_LIMIT = 60 * 1024 * 1024


def resident(shape):
    return pl.BlockSpec(shape, lambda step: (0,) * len(shape))


def stepped(shape):
    return pl.BlockSpec((1,) + shape[1:], lambda step: (step,) + (0,) * (len(shape) - 1))


def spec_list(pairs):
    return [stepped(shape) if moves else resident(shape) for shape, moves in pairs]


def attend_forward(x, a_all, bq, bv, qaug, kaug, vaug, b_mixer):
    length, model = x.shape
    groups = a_all.shape[0]
    block = (groups, length, PAD)
    return pl.pallas_call(
        attend_kernel,
        grid=(groups,),
        out_shape=[jax.ShapeDtypeStruct(block, BF16)] * 4 + [jax.ShapeDtypeStruct(x.shape, F32)],
        in_specs=spec_list(
            [
                (x.shape, 0), (a_all.shape, 1), (bq.shape, 1), (bv.shape, 1),
                (qaug.shape, 0), (kaug.shape, 0), (vaug.shape, 0), (b_mixer.shape, 0),
            ]
        ),
        out_specs=spec_list([(block, 1)] * 4 + [(x.shape, 0)]),
        scratch_shapes=[pltpu.VMEM((4, model, PAD), BF16)],
        compiler_params=pltpu.CompilerParams(vmem_limit_bytes=VMEM_LIMIT),
        name="attend_forward",
    )(x, a_all, bq, bv, qaug, kaug, vaug, b_mixer)


def dense_both(first_sum, wi, wo, bi, vectors, cotangent):
    length, model = first_sum.shape
    groups, _, hidden = wi.shape
    grad = (groups, model, hidden)
    forth = lambda shape: pl.BlockSpec(
        (1,) + shape[1:], lambda step: (lax.rem(step, groups),) + (0,) * (len(shape) - 1)
    )
    late = lambda shape: pl.BlockSpec(
        (1,) + shape[1:], lambda step: (jnp.maximum(step - groups, 0),) + (0,) * (len(shape) - 1)
    )
    return pl.pallas_call(
        dense_kernel,
        grid=(2 * groups,),
        out_shape=[
            jax.ShapeDtypeStruct((length, model), BF16),
            jax.ShapeDtypeStruct((length, model), F32),
            jax.ShapeDtypeStruct((length, model), BF16),
            jax.ShapeDtypeStruct(grad, BF16),
            jax.ShapeDtypeStruct(grad, BF16),
            jax.ShapeDtypeStruct((groups, 1, hidden), F32),
            jax.ShapeDtypeStruct((8, model), F32),
        ],
        in_specs=[
            pl.BlockSpec(memory_space=pl.ANY), forth(wi.shape), forth(wo.shape), forth(bi.shape),
            resident(vectors.shape), resident(cotangent.shape),
        ],
        out_specs=[
            resident((length, model)), resident((length, model)), resident((length, model)),
            late(grad), late(grad), late((groups, 1, hidden)), resident((8, model)),
        ],
        scratch_shapes=[
            pltpu.VMEM((length, model), F32),
            pltpu.VMEM((length, model), F32),
            pltpu.VMEM((length, model), F32),
            pltpu.VMEM((length, model), F32),
            pltpu.VMEM((groups, length, hidden), BF16),
            pltpu.VMEM((groups, length, hidden), BF16),
            pltpu.VMEM((length, model), BF16),
            pltpu.VMEM((model, length), BF16),
            pltpu.VMEM((model, length), BF16),
            pltpu.VMEM((length, hidden), BF16),
        ],
        compiler_params=pltpu.CompilerParams(vmem_limit_bytes=VMEM_LIMIT),
        name="dense_both",
    )(first_sum, wi, wo, bi, vectors, cotangent)


def attend_backward(x, a_all, d_mixed, d_first, q, k, v, attended):
    length, model = x.shape
    groups = a_all.shape[0]
    sums = (groups, 1, PAD)
    return pl.pallas_call(
        attend_back_kernel,
        grid=(groups,),
        out_shape=[
            jax.ShapeDtypeStruct(x.shape, F32),
            jax.ShapeDtypeStruct(a_all.shape, BF16),
            jax.ShapeDtypeStruct(sums, F32),
            jax.ShapeDtypeStruct(sums, F32),
        ],
        in_specs=spec_list(
            [
                (x.shape, 0), (a_all.shape, 1), (d_mixed.shape, 0), (d_first.shape, 0),
                (q.shape, 1), (k.shape, 1), (v.shape, 1), (attended.shape, 1),
            ]
        ),
        out_specs=spec_list([(x.shape, 0), (a_all.shape, 1), (sums, 1), (sums, 1)]),
        scratch_shapes=[
            pltpu.VMEM((4, model, PAD), BF16),
            pltpu.VMEM((model, length), BF16),
            pltpu.VMEM((model, length), BF16),
            pltpu.VMEM((length, PAD), BF16),
            pltpu.VMEM((PAD, length), BF16),
            pltpu.VMEM((PAD, length), F32),
            pltpu.VMEM((length, PAD), F32),
            pltpu.VMEM((length, PAD), F32),
            pltpu.VMEM((3, length, PAD), BF16),
        ],
        compiler_params=pltpu.CompilerParams(vmem_limit_bytes=VMEM_LIMIT),
        name="attend_backward",
    )(x, a_all, d_mixed, d_first, q, k, v, attended)


def augment(labels, width):
    length = labels.shape[0]
    lanes = lax.broadcasted_iota(jnp.int32, (length, PAD), 1)
    in_docs = (lanes >= width) & (lanes < width + DOCS)
    same = (lanes - width) == labels[:, None]
    qaug = jnp.where(in_docs & same, 1.0, 0.0).astype(BF16)
    spare = (lanes >= width + DOCS) & (lanes < width + DOCS + 3 * (width // HEAD))
    kaug = jnp.where(in_docs & ~same, -(2.0**100), jnp.where(spare, 1.0, 0.0)).astype(BF16)
    vaug = jnp.where((lanes[:1] == width) | spare[:1], 1.0, 0.0).astype(BF16)
    return qaug, kaug, vaug


def pad_groups(vector, groups, width):
    parts = vector.reshape(groups, 1, width)
    return jnp.pad(parts, ((0, 0), (0, 0), (0, PAD - width)))


def one_sequence(x, labels, a_all, wi, wo, bq, bv, bi, b_mixer, vectors, cotangent):
    groups = a_all.shape[0]
    width = a_all.shape[2] // 4
    qaug, kaug, vaug = augment(labels, width)
    q, k, v, attended, first_sum = attend_forward(
        x, a_all, pad_groups(bq, groups, width), pad_groups(bv, groups, width),
        qaug, kaug, vaug, b_mixer[None],
    )
    out, d_first, d_mixed, g_inner, g_outer, db_inner, small = dense_both(
        first_sum, wi, wo, bi.reshape(groups, 1, -1), vectors, cotangent
    )
    d_tokens, g_attend, dbq, dbv = attend_backward(
        x, a_all, d_mixed, d_first, q, k, v, attended
    )
    return (
        out, d_tokens, g_attend, g_inner, g_outer,
        dbq[:, 0, :width], dbv[:, 0, :width], db_inner[:, 0], small,
    )


def body(
    tokens, doc_ids, w_query, b_query, w_key, w_value, b_value, w_mixer, b_mixer, gain_one,
    bias_one, w_inner, b_inner, w_outer, b_outer, gain_two, bias_two, cotangent,
):
    groups = lax.axis_size("tensor")
    place = lax.axis_index("tensor")
    width = w_query.shape[1]
    hidden = w_inner.shape[1]
    length = doc_ids.shape[2]
    model = tokens.shape[3]

    def to_sequence(part):
        return lax.all_to_all(part, "tensor", 0, 2, tiled=True).reshape(length, model)

    def from_sequence(whole):
        return lax.all_to_all(whole.reshape(1, 1, length, model), "tensor", 2, 0, tiled=True)

    x = to_sequence(tokens)
    cot = to_sequence(cotangent)
    labels = lax.dynamic_index_in_dim(doc_ids[:, 0], place, 0, keepdims=False)
    shard_a = jnp.concatenate([w_query, w_key, w_value, w_mixer.T], axis=1)

    def gather(shard):
        whole = lax.all_gather(shard, ("tensor", "dp"), axis=0, tiled=True)
        return whole.reshape(groups, model, shard.shape[1])

    a_all = gather(shard_a)
    wi = gather(w_inner)
    wo = gather(w_outer.T)
    biases = lax.all_gather(jnp.concatenate([b_query, b_value, b_inner]), "tensor", axis=0)
    bq = biases[:, :width].reshape(-1)
    bv = biases[:, width : 2 * width].reshape(-1)
    bi = biases[:, 2 * width :].reshape(-1)
    vectors = jnp.stack([gain_one, bias_one, b_outer, gain_two, bias_two] + [b_outer] * 3)
    out, d_tokens, g_attend, g_inner, g_outer, dbq, dbv, dbi, small = one_sequence(
        x, labels, a_all, wi, wo, bq, bv, bi, b_mixer, vectors, cot
    )

    def scatter(grads):
        flat = grads.reshape(-1, grads.shape[2])
        return lax.psum_scatter(flat, ("tensor", "dp"), scatter_dimension=0, tiled=True)

    ga = scatter(g_attend).astype(F32)
    gi = scatter(g_inner).astype(F32)
    go = scatter(g_outer).astype(F32)
    summed = lax.psum(
        jnp.concatenate([dbq.reshape(-1), dbv.reshape(-1), dbi.reshape(-1), small.reshape(-1)]),
        ("dp", "tensor"),
    )
    mine = lambda start, size: lax.dynamic_slice_in_dim(summed, start + place * size, size)
    tail = summed[2 * model + dbi.size :].reshape(8, model)
    return (
        from_sequence(out),
        from_sequence(d_tokens),
        ga[:, :width],
        mine(0, width),
        ga[:, width : 2 * width],
        ga[:, 2 * width : 3 * width],
        mine(model, width),
        ga[:, 3 * width :].T,
        tail[3],
        tail[4],
        tail[5],
        gi,
        mine(2 * model, hidden),
        go.T,
        tail[0],
        tail[1],
        tail[2],
    )


def solution(mesh):
    split = P(None, "dp", "tensor", None)
    both, flipped, part = P("dp", "tensor"), P("tensor", "dp"), P("tensor")
    return jax.shard_map(
        body,
        mesh=mesh,
        in_specs=(
            split, P(None, "dp", None), both, part, both, both, part, flipped, P(), P(), P(),
            both, part, flipped, P(), P(), P(), split,
        ),
        out_specs=(
            split, split, both, part, both, both, part, flipped, P(), P(), P(), both, part,
            flipped, P(), P(), P(),
        ),
        check_vma=False,
    )
```

time: 1440 us -> 692 us (0.48)
  waiting for transfers between devices: 794 us -> 329 us
  matrix products: 282 us -> 0 us
  Pallas kernels: 0 us -> 175 us
  other arithmetic: 102 us -> 19.3 us
  blocking collectives: 168 us -> 101 us
  local copies, waits for them, and re-layouts: 61.9 us -> 35.5 us
    dot_general x96 -> x0, matrix products: 282 us -> none  [the longest x24 56.8 us: contract_cols(): lax.dot_general(left, right, (((1,), (1,)), ((), ())), preferred_element_...]
    reduce_scatter x18 -> x2, waiting for transfers between devices: 403 us -> 192 us  [scatter(): lax.psum_scatter(flat, ('tensor', 'dp'), scatter_dimension=0, tiled=True)]
    unnamed x44 -> x7, waiting for transfers between devices: 202 us -> 2.29 us
    pallas_call x0 -> x3, Pallas kernels: none -> 175 us  [the longest x1 74.7 us: attend_backward(): pl.pallas_call(attend_back_kernel, grid=(groups,), out_shape=[jax.ShapeDt...]
    all_gather x4 -> x1, blocking collectives: 126 us -> 22 us  [body(): lax.all_gather(jnp.concatenate([b_query, b_value, b_inner]), 'tensor', ax...]
    all_gather x18 -> x3, waiting for transfers between devices: 189 us -> 122 us  [gather(): whole = lax.all_gather(shard, ('tensor', 'dp'), axis=0, tiled=True)]
    reduce_sum x29 -> x0, other arithmetic: 52.7 us -> none  [the longest x4 13.4 us: normalize(): return centred * lax.rsqrt(spread + 1e-12) * weights + offsets]
    psum x1, blocking collectives: 41.6 us -> 79 us  [body(): lax.psum(jnp.concatenate([dbq.reshape(-1), dbv.reshape(-1), dbi.reshape(-...]
  transfers between devices with their start and end apart: 40 -> 10, of which waited for: 28 -> 6; matrix products, arithmetic and copies ran while one was open for 25% -> 7% of each run, Pallas kernels for 0% -> 6%
where the time goes in v1:
time: 692 us; the launch traced here: 691 us
  waiting for transfers between devices  329 us (48%)
  Pallas kernels  175 us (25%)
  blocking collectives  101 us (15%)
  local copies, waits for them, and re-layouts  35.5 us (5%)
  other arithmetic  19.3 us (3%)
  starting transfers between devices  15.8 us (2%)
  between operations  14.4 us (2%)
    reduce_scatter x2, waiting for transfers between devices, scatter(): lax.psum_scatter(flat, ('tensor', 'dp'), scatter_dimension=0, tiled=True)  192 us
    all_gather x3, waiting for transfers between devices, gather(): whole = lax.all_gather(shard, ('tensor', 'dp'), axis=0, tiled=True)  122 us
    psum x1, blocking collectives, body(): lax.psum(jnp.concatenate([dbq.reshape(-1), dbv.reshape(-1), dbi.reshape(-...  79 us
    pallas_call x1, Pallas kernels, attend_backward(): pl.pallas_call(attend_back_kernel, grid=(groups,), out_shape=[jax.ShapeDt...  74.7 us
    pallas_call x1, Pallas kernels, dense_both(): pl.pallas_call(dense_kernel, grid=(2 * groups,), out_shape=[jax.ShapeDtyp...  58.4 us
    pallas_call x1, Pallas kernels, attend_forward(): pl.pallas_call(attend_kernel, grid=(groups,), out_shape=[jax.ShapeDtypeSt...  42.1 us
    all_gather x1, blocking collectives, body(): lax.all_gather(jnp.concatenate([b_query, b_value, b_inner]), 'tensor', ax...  22 us
    unnamed x50, local copies, waits for them, and re-layouts  19.4 us
  transfers between devices with their start and end apart: 10, of which 6 were waited for; matrix products, arithmetic and copies ran while one was open for 7% of the time, Pallas kernels for 6%

profile of v1, /device:TPU:0, one launch (start us, length us, event | category | flops | bytes accessed | tf_op | source)
XLA Modules:
  0.0 690.7 jit_solution(10589702717902103831)
XLA Ops:
  7.3 0.9 copy.58
  8.2 1.6 pad_maximum_fusion
  11.4 4.4 all-to-all-start
  15.8 22.0 %all-gather.1 = f32[4,1,1152]{2,1,0:T(1,128)S(1)} all-gather(f32[1,1,1152]{2,1,0:T(1,128)S(1)} %reshape.149), channel_id=2, replica_groups=mesh['dp'=8,'tensor'=4] {'tensor'}, dimensions={0}, use_global_device_ids=true | all-gather | bytes 23040 | tf_op jit(solution)/shard_map/all_gather | solution.py:506
  37.9 3.6 all-to-all-start.1
  45.3 1.0 select_convert_fusion.1.qaug_ref
  46.4 1.1 select_convert_fusion.kaug_ref
  47.5 33.1 %all-gather.6.cloned.1.call-done = bf16[3072,768]{1,0:T(8,128)(2,1)} async-done(((bf16[96,768]{1,0:T(8,128)(2,1)}), bf16[3072,768]{1,0:T(8,128)(2,1)}) %all-gather.6.cloned.1.call-update) | async-done | bytes 4718608 | tf_op jit(solution)/shard_map/all_gather | solution.py:500
  80.6 42.1 %attend_forward.1 = (bf16[4,1024,256]{2,1,0:T(8,128)(2,1)}, bf16[4,1024,256]{2,1,0:T(8,128)(2,1)}, bf16[4,1024,256]{2,1,0:T(8,128)(2,1)}, bf16[4,1024,256]{2,1,0:T(8,128)(2,1)}, f32[1024,768]{1,0:T(8,128)}) custom-call(bf16[1024,768]{1,0:T(8,128)(2,1)} %bitcast.36, bf16[4,768,768]{2,1,0:T(8,128)(2,1)} %bitcast.34, f32[4,1,256]{2,1,0:T(1,128)} %pad.7.clone.bq_ref, ...), custom_call_target="tpu_custom_call" | custom-call | tf_op jit(solution)/shard_map/attend_forward/pallas_call | solution.py:340
  122.7 23.3 %all-gather.8.cloned.1.call-done = bf16[3072,768]{1,0:T(8,128)(2,1)} async-done(((bf16[96,768]{1,0:T(8,128)(2,1)}), bf16[3072,768]{1,0:T(8,128)(2,1)}) %all-gather.8.cloned.1.call-update) | async-done | bytes 4718608 | tf_op jit(solution)/shard_map/all_gather | solution.py:500
  146.1 65.4 %all-gather.10.cloned.1.call-done = bf16[3072,768]{1,0:T(8,128)(2,1)} async-done(((bf16[96,768]{1,0:T(8,128)(2,1)}), bf16[3072,768]{1,0:T(8,128)(2,1)}) %all-gather.10.cloned.1.call-update) | async-done | bytes 4718608 | tf_op jit(solution)/shard_map/all_gather | solution.py:500
  211.5 58.4 %dense_both.1 = (bf16[1024,768]{1,0:T(8,128)(2,1)}, f32[1024,768]{1,0:T(8,128)}, bf16[1024,768]{1,0:T(8,128)(2,1)}, bf16[4,768,768]{2,1,0:T(8,128)(2,1)}, bf16[4...) custom-call(f32[1024,768]{1,0:T(8,128)} %get-tuple-element.33.first_in, ...), custom_call_target="tpu_custom_call" | custom-call | tf_op jit(solution)/shard_map/dense_both/pallas_call | solution.py:367
  269.9 74.7 %attend_backward.1 = (f32[1024,768]{1,0:T(8,128)}, bf16[4,768,768]{2,1,0:T(8,128)(2,1)}, f32[4,1,256]{2,1,0:T(1,128)}, f32[4,1,256]{2,1,0:T(1,128)}) custom-call(bf16[1024,768]{1,0:T(8,128)(2,1)} %bitcast.37, bf16[4,768,768]{2,1,0:T(8,128)(2,1)} %bitcast.35, bf16[1024,768]{1,0:T(8,128)(2,1)} %get-tuple-element.35.dmix_ref, ...), custom_call_target="tpu_custom_call" | custom-call | tf_op jit(solution)/shard_map/attend_backward/pallas_call | solution.py:408
  345.8 3.8 copy.78
  350.2 11.6 %reduce.4 = bf16[1024,768]{1,0:T(8,128)(2,1)} reduce(bf16[1024,1,1,768]{3,2,1,0:T(2,128)(2,1)S(1)} %bitcast.39, bf16[]{:T(256)} %broadcast.83), dimensions={1,2}, to_apply=%bitcast.33.reduce_sub_computation | reduce | bytes 3145730
  361.8 3.8 reshape.156
  365.6 3.6 all-to-all-start.2
  369.2 6.9 copy.62
  376.1 13.2 %all-to-all-done.2 = bf16[4,2,98304]{2,1,0:T(2,128)(2,1)S(1)} async-done(((bf16[4,2,98304]{2,1,0:T(2,128)(2,1)}), bf16[4,2,98304]{2,1,0:T(2,128)(2,1)S(1)}, u32[]{:S(2)}, u32[]{:S(2)}) %all-to-all-start.2) | async-done | bytes 1572896 | tf_op jit(solution)/shard_map/all_to_all | solution.py:492
  389.2 1.1 copy-done.3
  390.4 3.9 all-to-all-start.3
  394.5 79.0 %psum.7 = f32[10752]{0:T(1024)S(1)} all-reduce(f32[10752]{0:T(1024)S(1)} %pad_maximum_fusion.1), channel_id=1, replica_groups=mesh['dp'=8,'tensor'=4] {'dp','tensor'}, use_global_device_ids=true, to_apply=%region_1.2 | all-reduce | flops 10752 | bytes 86016 | tf_op jit(solution)/shard_map/psum | solution.py:522
  474.9 4.5 reshape.157
  479.4 3.4 copy.72
  482.7 1.9 copy.65
  484.6 1.1 copy.70
  485.7 0.7 copy.66
  486.5 0.7 copy.67
  488.6 82.2 %reduce-scatter.8.cloned.1.call-done = bf16[96,768]{1,0:T(8,128)(2,1)} async-done(((bf16[3072,768]{1,0:T(8,128)(2,1)}), bf16[96,768]{1,0:T(8,128)(2,1)}) %reduce-scatter.8.cloned.1.call-update) | async-done | bytes 147472 | tf_op jit(solution)/shard_map/reduce_scatter | solution.py:517
  570.8 1.6 convert_bitcast_fusion
  572.4 109.8 %reduce-scatter.6.cloned.1.call-done = bf16[96,768]{1,0:T(8,128)(2,1)} async-done(((bf16[3072,768]{1,0:T(8,128)(2,1)}), bf16[96,768]{1,0:T(8,128)(2,1)}) %reduce-scatter.6.cloned.1.call-update) | async-done | bytes 147472 | tf_op jit(solution)/shard_map/reduce_scatter | solution.py:517
  682.3 1.6 convert_element_type.23
  (85 shorter events, 10.1 us)
Async XLA Ops:
  7.2 38.2 %copy-start = (s32[4,1,1024]{2,1,0:T(1,128)S(1)}, s32[4,1,1024]{2,1,0:T(1,128)}, u32[]{:S(2)}) copy-start(s32[4,1,1024]{2,1,0:T(1,128)} %param.19) | copy-start | bytes 49156
  7.2 8.5 %copy-start.16 = (f32[192]{0:T(256)S(1)}, f32[192]{0:T(256)}, u32[]{:S(2)}) copy-start(f32[192]{0:T(256)} %param.21) | copy-start | bytes 2308
  7.2 8.5 %copy-start.17 = (f32[192]{0:T(256)S(1)}, f32[192]{0:T(256)}, u32[]{:S(2)}) copy-start(f32[192]{0:T(256)} %param.24) | copy-start | bytes 2308
  7.2 8.5 %copy-start.7 = (f32[768]{0:T(1024)S(1)}, f32[768]{0:T(1024)}, u32[]{:S(2)}) copy-start(f32[768]{0:T(1024)} %param.30) | copy-start | bytes 9220
  7.2 73.3 %all-gather.6.cloned.1.call-start = ((), (), s32[]{:S(2)}) async-start(), calls=%async_computation.7 | async-start | bytes 4866048 | tf_op jit(solution)/shard_map/all_gather | solution.py:500
  9.8 136.2 %all-gather.8.cloned.1.call-start = ((), (), s32[]{:S(2)}) async-start(), calls=%async_computation.8 | async-start | bytes 4866048 | tf_op jit(solution)/shard_map/all_gather | solution.py:500
  10.6 200.9 %all-gather.10.cloned.1.call-start = ((), (), s32[]{:S(2)}) async-start(), calls=%async_computation.9 | async-start | bytes 4866048 | tf_op jit(solution)/shard_map/all_gather | solution.py:500
  11.3 31.5 %copy-start.8 = (f32[768]{0:T(1024)S(1)}, f32[768]{0:T(1024)}, u32[]{:S(2)}) copy-start(f32[768]{0:T(1024)} %param.26) | copy-start | bytes 9220
  11.3 32.7 %copy-start.9 = (f32[768]{0:T(1024)S(1)}, f32[768]{0:T(1024)}, u32[]{:S(2)}) copy-start(f32[768]{0:T(1024)} %param.27) | copy-start | bytes 9220
  11.3 32.7 %copy-start.10 = (f32[768]{0:T(1024)S(1)}, f32[768]{0:T(1024)}, u32[]{:S(2)}) copy-start(f32[768]{0:T(1024)} %param.28) | copy-start | bytes 9220
  11.3 32.7 %copy-start.11 = (f32[768]{0:T(1024)S(1)}, f32[768]{0:T(1024)}, u32[]{:S(2)}) copy-start(f32[768]{0:T(1024)} %param.32) | copy-start | bytes 9220
  11.4 32.7 %copy-start.12 = (f32[768]{0:T(1024)S(1)}, f32[768]{0:T(1024)}, u32[]{:S(2)}) copy-start(f32[768]{0:T(1024)} %param.33) | copy-start | bytes 9220
  11.4 32.7 %copy-start.13 = (f32[768]{0:T(1024)S(1)}, f32[768]{0:T(1024)}, u32[]{:S(2)}) copy-start(f32[768]{0:T(1024)} %param.34) | copy-start | bytes 9220
  11.4 26.5 %all-to-all-start = ((bf16[4,1,256,768]{3,2,1,0:T(8,128)(2,1)}), bf16[4,1,256,768]{3,2,1,0:T(8,128)(2,1)S(1)}, u32[]{:S(2)}, u32[]{:S(2)}) async-start(bf16[4,1,256,768]{3,2,1,0:T(8,128)(2,1)} %param.18), calls=%async_computation | async-start | bytes 3145728 | tf_op jit(solution)/shard_map/all_to_all | solution.py:489
  37.9 42.7 %copy-start.2 = (bf16[4,1,256,768]{3,2,1,0:T(8,128)(2,1)}, bf16[4,1,256,768]{3,2,1,0:T(8,128)(2,1)S(1)}, u32[]{:S(2)}) copy-start(bf16[4,1,256,768]{3,2,1,0:T(8,128)(2,1)S(1)} %all-to-all-done) | copy-start | bytes 4718596
  37.9 84.8 %all-to-all-start.1 = ((bf16[4,1,256,768]{3,2,1,0:T(8,128)(2,1)}), bf16[4,1,256,768]{3,2,1,0:T(8,128)(2,1)S(1)}, u32[]{:S(2)}, u32[]{:S(2)}) async-start(bf16[4,1,256,768]{3,2,1,0:T(8,128)(2,1)} %param.35), calls=%async_computation.1 | async-start | bytes 3145728 | tf_op jit(solution)/shard_map/all_to_all | solution.py:489
  41.5 443.1 %reduce-scatter.10.cloned.1.call-start = ((), (), s32[]{:S(2)}) async-start(), calls=%async_computation.12 | async-start | bytes 4866048
  122.7 88.8 %copy-start.4 = (bf16[4,1,256,768]{3,2,1,0:T(8,128)(2,1)}, bf16[4,1,256,768]{3,2,1,0:T(8,128)(2,1)S(1)}, u32[]{:S(2)}) copy-start(bf16[4,1,256,768]{3,2,1,0:T(8,128)(2,1)S(1)} %all-to-all-done.1) | copy-start | bytes 4718596
  344.7 226.1 %reduce-scatter.8.cloned.1.call-start = ((), (), s32[]{:S(2)}) async-start(), calls=%async_computation.11 | async-start | bytes 4866048 | tf_op jit(solution)/shard_map/reduce_scatter | solution.py:517
  345.2 337.0 %reduce-scatter.6.cloned.1.call-start = ((), (), s32[]{:S(2)}) async-start(), calls=%async_computation.10 | async-start | bytes 4866048 | tf_op jit(solution)/shard_map/reduce_scatter | solution.py:517
  365.6 23.6 %all-to-all-start.2 = ((bf16[4,2,98304]{2,1,0:T(2,128)(2,1)}), bf16[4,2,98304]{2,1,0:T(2,128)(2,1)S(1)}, u32[]{:S(2)}, u32[]{:S(2)}) async-start(bf16[4,2,98304]{2,1,0:T(2,128)(2,1)} %reshape.156), calls=%async_computation.2 | async-start | bytes 3145728 | tf_op jit(solution)/shard_map/all_to_all | solution.py:492
  376.0 18.3 %copy-start.14 = (f32[4,1,256]{2,1,0:T(1,128)S(1)}, f32[4,1,256]{2,1,0:T(1,128)}, u32[]{:S(2)}) copy-start(f32[4,1,256]{2,1,0:T(1,128)} %get-tuple-element.43) | copy-start | bytes 12292
  376.0 18.3 %copy-start.15 = (f32[4,1,256]{2,1,0:T(1,128)S(1)}, f32[4,1,256]{2,1,0:T(1,128)}, u32[]{:S(2)}) copy-start(f32[4,1,256]{2,1,0:T(1,128)} %get-tuple-element.44) | copy-start | bytes 12292
  376.0 18.5 %copy-start.5 = (f32[8,768]{1,0:T(8,128)S(1)}, f32[8,768]{1,0:T(8,128)}, u32[]{:S(2)}) copy-start(f32[8,768]{1,0:T(8,128)} %get-tuple-element.46) | copy-start | bytes 73732
  376.0 18.5 %copy-start.6 = (f32[4,1,768]{2,1,0:T(1,128)S(1)}, f32[4,1,768]{2,1,0:T(1,128)}, u32[]{:S(2)}) copy-start(f32[4,1,768]{2,1,0:T(1,128)} %get-tuple-element.45) | copy-start | bytes 36868
  389.2 1.1 copy-start.3
  390.4 92.4 %all-to-all-start.3 = ((f32[1,1,1024,768]{3,1,0,2:T(1,128)}), f32[1,1,1024,768]{3,1,0,2:T(1,128)S(1)}, u32[]{:S(2)}, u32[]{:S(2)}) async-start(f32[1,1,1024,768]{3,1,0,2:T(1,128)} %copy.62), calls=%async_computation.3 | async-start | bytes 6291456 | tf_op jit(solution)/shard_map/all_to_all | solution.py:492
  482.7 201.2 %copy-start.1 = (s32[4,1,1024]{2,1,0:T(1,128)S(1)}, s32[4,1,1024]{2,1,0:T(1,128)}, u32[]{:S(2)}) copy-start(s32[4,1,1024]{2,1,0:T(1,128)} %param.19) | copy-start | bytes 49156
Sparse Core Ops, SparseCore 0:
  11.6 68.9 all-gather.5
  83.5 62.5 all-gather.7
  149.0 62.4 all-gather.9
  344.8 113.5 reduce-scatter.9
  464.6 106.1 reduce-scatter.7
  576.1 106.0 reduce-scatter.5

commit v2 on v1

--- a/solution.py
+++ b/solution.py
@@ -59,56 +59,348 @@
     return jnp.concatenate([part, jnp.zeros((part.shape[0], PAD - width), part.dtype)], axis=1)
 
 
-def attend_kernel(
-    x_ref, a_ref, bq_ref, bv_ref, qaug_ref, kaug_ref, vaug_ref, bm_ref,
+def project(x_rows, rows, bq, bv, w_s, qaug_ref, kaug_ref, vaug_ref, q_ref, k_ref, v_ref):
+    queries = (dot_nn(x_rows, w_s[0]) + bq).astype(BF16)
+    q_ref[0, rows, :] = queries * jnp.asarray(HEAD**-0.5, BF16) + qaug_ref[rows, :]
+    keys = dot_nn(x_rows, w_s[1]).astype(BF16)
+    k_ref[0, rows, :] = keys + kaug_ref[rows, :]
+    values = (dot_nn(x_rows, w_s[2]) + bv).astype(BF16)
+    v_ref[0, rows, :] = values + vaug_ref[...]
+
+
+def attend_rows(rows, width, w_s, q_ref, k_ref, v_ref, att_ref, first_ref):
+    lanes = lane_index((ROWS, PAD))
+    queries = q_ref[0, rows, :]
+    attended = jnp.zeros((ROWS, PAD), F32)
+    extended = queries
+    for head in range(width // HEAD):
+        masked = jnp.where(head_and_extra(lanes, head, width), queries, 0)
+        scores = dot_nt(masked, k_ref[0])
+        highest = jnp.max(scores, axis=1, keepdims=True)
+        raw = jnp.exp2((scores - highest) * LOG2E).astype(BF16)
+        mixed = dot_nn(raw, v_ref[0])
+        total = mixed[:, width : width + 1]
+        attended = jnp.where(head_only(lanes, head), mixed / total, attended)
+        for spot, part in enumerate(three_parts(-(highest + jnp.log(total)))):
+            here = lanes == width + DOCS + 3 * head + spot
+            extended = jnp.where(here, jnp.broadcast_to(part, (ROWS, PAD)), extended)
+    q_ref[0, rows, :] = extended
+    attended = attended.astype(BF16)
+    att_ref[0, rows, :] = attended
+    first_ref[rows, :] += dot_nt(attended, w_s[3])
+
+
+def attend_plain_kernel(
+    x_ref, a_ref, bias_ref, qaug_ref, kaug_ref, vaug_ref, bm_ref,
     q_ref, k_ref, v_ref, att_ref, first_ref, w_s,
 ):
-    step = pl.program_id(0)
     length, model = x_ref.shape
     width = a_ref.shape[2] // 4
-    heads = width // HEAD
-    blocks = length // ROWS
     for slot in range(4):
         w_s[slot] = unpack(a_ref.at[0], slot, width)
+    biases = bias_ref[0]
+
+    @pl.when(pl.program_id(0) == 0)
+    def _():
+        first_ref[...] = x_ref[...].astype(F32) + bm_ref[...]
+
+    @pl.loop(0, length // ROWS)
+    def _(index):
+        rows = rows_of(index)
+        project(
+            x_ref[rows, :], rows, biases[:, :PAD], biases[:, PAD : 2 * PAD], w_s, qaug_ref,
+            kaug_ref, vaug_ref, q_ref, k_ref, v_ref,
+        )
+
+    @pl.loop(0, length // ROWS)
+    def _(index):
+        attend_rows(rows_of(index), width, w_s, q_ref, k_ref, v_ref, att_ref, first_ref)
+
+
+MESH = pl.DeviceIdType.MESH
+
+
+def partner(index, bits, size):
+    flipped = index
+    for bit in (1, 2, 4):
+        if bits & bit and bit < size:
+            flipped = flipped + bit - 2 * bit * lax.rem(lax.div(index, bit), 2)
+    return flipped
+
+
+class Wires:
+    def __init__(self, send, recv, place, row):
+        self.send, self.recv, self.place, self.row = send, recv, place, row
+
+    def to(self, tensor_bits, dp_bits):
+        return (partner(self.row, dp_bits, 8), partner(self.place, tensor_bits, 4))
+
+    def copy(self, number, source, target, tensor_bits=0, dp_bits=0):
+        return pltpu.make_async_remote_copy(
+            src_ref=source,
+            dst_ref=target,
+            send_sem=self.send.at[number],
+            recv_sem=self.recv.at[number],
+            device_id=self.to(tensor_bits, dp_bits),
+            device_id_type=MESH,
+        )
+
+
+def greet(wires, peers):
+    barrier = pltpu.get_barrier_semaphore()
+    for tensor_bits, dp_bits in peers:
+        pl.semaphore_signal(
+            barrier, inc=1, device_id=wires.to(tensor_bits, dp_bits), device_id_type=MESH
+        )
+    pl.semaphore_wait(barrier, len(peers))
+
+
+PEERS = ((1, 0), (2, 0), (3, 0), (0, 1), (0, 2), (0, 4), (0, 6))
+TOKENS, COTS, BIASES, KIND_A = 0, 3, 6, 9
+KIND_I = KIND_A + 17
+KIND_O = KIND_I + 17
+FORWARD_WIRES = KIND_O + 10
+
+
+class ShardGather:
+    def __init__(self, wires, base, shard, whole):
+        self.wires, self.base, self.shard, self.whole = wires, base, shard, whole
+
+    def at(self, slot, dp_bits):
+        return self.whole.at[slot, partner(self.wires.row, dp_bits, 8)]
+
+    def cross_x(self):
+        return self.wires.copy(self.base, self.shard, self.at(2, 0), 2, 0)
+
+    def along_z(self, slot, step, mine):
+        source = self.shard if slot == 0 else self.at(slot, 0)
+        number = self.base + 1 + 3 * (slot // 2) + step - 1
+        target = self.at(slot, 0) if mine else self.at(slot, 2 * step)
+        return self.wires.copy(number, source, target, 0, 2 * step)
+
+    def along_y(self, slot, step, mine):
+        source = self.shard if slot == 0 and step == 0 else self.at(slot, 2 * step)
+        number = self.base + 7 + 4 * (slot // 2) + step
+        target = self.at(slot, 2 * step) if mine else self.at(slot, 2 * step + 1)
+        return self.wires.copy(number, source, target, 0, 1)
+
+    def to_core(self, slot, mine):
+        number = self.base + 15 + slot // 2
+        target = self.whole.at[slot + 1]
+        return self.wires.copy(number, self.whole.at[slot], target, 1, 0)
+
+    def start_z(self, slot):
+        for step in (1, 2, 3):
+            self.along_z(slot, step, True).start()
+
+    def wait_z(self, slot):
+        for step in (1, 2, 3):
+            self.along_z(slot, step, False).wait_recv()
+
+    def pass_y(self, slot):
+        for step in (1, 2, 3):
+            self.along_y(slot, step, True).start()
+
+    def wait_y(self, slot):
+        for step in range(4):
+            self.along_y(slot, step, False).wait_recv()
+
+    def wait_sent(self, x_first=True):
+        for slot in (0, 2) if x_first else (0,):
+            for step in (1, 2, 3):
+                self.along_z(slot, step, True).wait_send()
+            for step in range(4):
+                self.along_y(slot, step, True).wait_send()
+        for slot in (0, 2):
+            self.to_core(slot, True).wait_send()
+
+
+class BlockGather(ShardGather):
+    def along_z(self, slot, step, mine):
+        target = self.at(0, 0) if mine else self.at(0, 2 * step)
+        return self.wires.copy(self.base + step - 1, self.shard, target, 0, 2 * step)
+
+    def along_y(self, slot, step, mine):
+        source = self.shard if step == 0 else self.at(0, 2 * step)
+        target = self.at(0, 2 * step) if mine else self.at(0, 2 * step + 1)
+        return self.wires.copy(self.base + 3 + step, source, target, 0, 1)
+
+    def cross_x(self):
+        return self.wires.copy(self.base + 7, self.whole.at[0], self.whole.at[2], 2, 0)
+
+    def to_core(self, slot, mine):
+        return self.wires.copy(
+            self.base + 8 + slot // 2, self.whole.at[slot], self.whole.at[slot + 1], 1, 0
+        )
+
+
+def attend_kernel(
+    tok_ref, cot_ref, sa_ref, si_ref, so_ref, bias_ref, qaug_ref, kaug_ref, vaug_ref, bm_ref,
+    q_ref, k_ref, v_ref, att_ref, first_ref, bi_ref, x_out, cot_out, a_out, wi_out, wo_out,
+    w_s, x_s, a_s, bias_s, send_sem, recv_sem, here_sem,
+):
+    step = pl.program_id(0)
+    place = lax.axis_index("tensor")
+    row = lax.axis_index("dp")
+    quarters, part, model = x_s.shape
+    length = quarters * part
+    width = sa_ref.shape[1] // 4
+    blocks = length // ROWS
+    share = sa_ref.shape[0]
+    wires = Wires(send_sem, recv_sem, place, row)
+    attn = ShardGather(wires, KIND_A, sa_ref, a_s)
+    inner = ShardGather(wires, KIND_I, si_ref, wi_out)
+    outer = BlockGather(wires, KIND_O, so_ref, wo_out)
+
+    def exchange(base, source, target, bits, mine):
+        other = partner(place, bits, 4)
+        return wires.copy(
+            base + bits - 1, source.at[other], target.at[place if mine else other], bits, 0
+        )
+
+    def bias_copy(bits, mine):
+        return wires.copy(BIASES + bits - 1, bias_ref, bias_s.at[bits], bits, 0)
+
+    local = [
+        pltpu.make_async_copy(tok_ref.at[place], x_s.at[place], here_sem.at[0]),
+        pltpu.make_async_copy(sa_ref, a_s.at[0, row], here_sem.at[1]),
+        pltpu.make_async_copy(si_ref, wi_out.at[0, row], here_sem.at[2]),
+        pltpu.make_async_copy(so_ref, wo_out.at[0, row], here_sem.at[3]),
+        pltpu.make_async_copy(cot_ref.at[place], cot_out.at[place], here_sem.at[4]),
+        pltpu.make_async_copy(bias_ref, bias_s.at[0], here_sem.at[5]),
+    ]
+    keep_x = pltpu.make_async_copy(x_s, x_out, here_sem.at[6])
+    keep_a = pltpu.make_async_copy(a_s, a_out, here_sem.at[7])
 
     @pl.when(step == 0)
     def _():
-        first_ref[...] = x_ref[...].astype(F32) + bm_ref[...]
+        greet(wires, PEERS)
+        attn.cross_x().start()
+        for bits in (1, 2, 3):
+            bias_copy(bits, True).start()
+        attn.start_z(0)
+        attn.along_y(0, 0, True).start()
+        for bits in (2, 3, 1):
+            exchange(TOKENS, tok_ref, x_s, bits, True).start()
+        for copy in local:
+            copy.start()
+        for copy in local:
+            copy.wait()
+        attn.cross_x().wait_recv()
+        attn.start_z(2)
+        attn.along_y(2, 0, True).start()
+        attn.wait_z(0)
+        attn.pass_y(0)
+        attn.wait_y(0)
+        attn.to_core(0, True).start()
+        for bits in (1, 2, 3):
+            exchange(TOKENS, tok_ref, x_s, bits, False).wait_recv()
+            bias_copy(bits, False).wait_recv()
+        keep_x.start()
+
+        @pl.loop(0, quarters)
+        def _(index):
+            rows = rows_of(index, part)
+            first_ref[rows, :] = x_s[index].astype(F32) + bm_ref[...]
+
+    @pl.when(step == 1)
+    def _():
+        attn.to_core(0, False).wait_recv()
+
+    @pl.when(step == 2)
+    def _():
+        attn.wait_y(2)
+        attn.to_core(2, True).start()
+
+    @pl.when(step == 3)
+    def _():
+        attn.to_core(2, False).wait_recv()
+        keep_a.start()
+
+    for dp_row in range(a_s.shape[1]):
+        packed = a_s[step, dp_row]
+        rest = jnp.zeros((share, PAD - width), packed.dtype)
+        for slot in range(4):
+            piece = packed[:, slot * width : (slot + 1) * width]
+            rows = slice(dp_row * share, (dp_row + 1) * share)
+            w_s[slot, rows, :] = jnp.concatenate([piece, rest], axis=1)
+    biases = bias_s[step]
+    bi_ref[0] = biases[:, 2 * PAD :]
+
+    @pl.loop(0, quarters)
+    def _(index):
+        rows = rows_of(index, part)
+        x_rows = x_s[index]
+        project(
+            x_rows, rows, biases[:, :PAD], biases[:, PAD : 2 * PAD], w_s, qaug_ref, kaug_ref,
+            vaug_ref, q_ref, k_ref, v_ref,
+        )
 
     @pl.loop(0, blocks)
     def _(index):
-        rows = rows_of(index)
-        x_rows = x_ref[rows, :]
-        queries = (dot_nn(x_rows, w_s[0]) + bq_ref[0]).astype(BF16)
-        q_ref[0, rows, :] = queries * jnp.asarray(HEAD**-0.5, BF16) + qaug_ref[rows, :]
-        keys = dot_nn(x_rows, w_s[1]).astype(BF16)
-        k_ref[0, rows, :] = keys + kaug_ref[rows, :]
-        values = (dot_nn(x_rows, w_s[2]) + bv_ref[0]).astype(BF16)
-        v_ref[0, rows, :] = values + vaug_ref[...]
-
-    @pl.loop(0, blocks)
-    def _(index):
-        rows = rows_of(index)
-        lanes = lane_index((ROWS, PAD))
-        queries = q_ref[0, rows, :]
-        attended = jnp.zeros((ROWS, PAD), F32)
-        extended = queries
-        for head in range(heads):
-            masked = jnp.where(head_and_extra(lanes, head, width), queries, 0)
-            scores = dot_nt(masked, k_ref[0])
-            highest = jnp.max(scores, axis=1, keepdims=True)
-            raw = jnp.exp2((scores - highest) * LOG2E).astype(BF16)
-            mixed = dot_nn(raw, v_ref[0])
-            total = mixed[:, width : width + 1]
-            attended = jnp.where(head_only(lanes, head), mixed / total, attended)
-            parts = three_parts(-(highest + jnp.log(total)))
-            for place, part in enumerate(parts):
-                here = lanes == width + DOCS + 3 * head + place
-                extended = jnp.where(here, jnp.broadcast_to(part, (ROWS, PAD)), extended)
-        q_ref[0, rows, :] = extended
-        attended = attended.astype(BF16)
-        att_ref[0, rows, :] = attended
-        first_ref[rows, :] += dot_nt(attended, w_s[3])
+        attend_rows(rows_of(index), width, w_s, q_ref, k_ref, v_ref, att_ref, first_ref)
+
+        @pl.when((step == 0) & (index == 1))
+        def _():
+            attn.wait_z(2)
+            attn.pass_y(2)
+            outer.start_z(0)
+            outer.along_y(0, 0, True).start()
+            inner.cross_x().start()
+            for bits in (2, 3, 1):
+                exchange(COTS, cot_ref, cot_out, bits, True).start()
+
+        @pl.when((step == 0) & (index == 3))
+        def _():
+            inner.cross_x().wait_recv()
+            inner.start_z(0)
+            inner.along_y(0, 0, True).start()
+            inner.start_z(2)
+            inner.along_y(2, 0, True).start()
+
+        @pl.when((step == 1) & (index == 2))
+        def _():
+            outer.wait_z(0)
+            outer.pass_y(0)
+
+        @pl.when((step == 2) & (index == 1))
+        def _():
+            outer.wait_y(0)
+            outer.cross_x().start()
+            outer.to_core(0, True).start()
+
+        @pl.when((step == 3) & (index == 0))
+        def _():
+            inner.wait_z(0)
+            inner.pass_y(0)
+
+        @pl.when((step == 3) & (index == 2))
+        def _():
+            inner.wait_z(2)
+            inner.pass_y(2)
+
+    @pl.when(step == 3)
+    def _():
+        inner.wait_y(0)
+        inner.to_core(0, True).start()
+        inner.wait_y(2)
+        inner.to_core(2, True).start()
+        outer.cross_x().wait_recv()
+        outer.to_core(2, True).start()
+        for bits in (1, 2, 3):
+            exchange(COTS, cot_ref, cot_out, bits, False).wait_recv()
+        for gather in (inner, outer):
+            for slot in (0, 2):
+                gather.to_core(slot, False).wait_recv()
+        for gather in (attn, inner, outer):
+            gather.cross_x().wait_send()
+            gather.wait_sent(gather is not outer)
+        for bits in (1, 2, 3):
+            exchange(TOKENS, tok_ref, x_s, bits, True).wait_send()
+            exchange(COTS, cot_ref, cot_out, bits, True).wait_send()
+            bias_copy(bits, True).wait_send()
+        keep_x.wait()
+        keep_a.wait()
 
 
 def gelu_parts(values):
@@ -333,25 +625,71 @@
     return [stepped(shape) if moves else resident(shape) for shape, moves in pairs]
 
 
-def attend_forward(x, a_all, bq, bv, qaug, kaug, vaug, b_mixer):
+def attend_forward(tokens, cotangent, shard_a, shard_i, shard_o, biases, qaug, kaug, vaug, b_mixer):
+    groups, part, model = tokens.shape
+    length = groups * part
+    share = shard_a.shape[0]
+    block = (groups, length, PAD)
+    whole = jax.ShapeDtypeStruct((groups, model // share, share, model), BF16)
+    hidden = shard_i.shape[1]
+    anywhere = pl.BlockSpec(memory_space=pl.ANY)
+    return pl.pallas_call(
+        attend_kernel,
+        grid=(groups,),
+        out_shape=[jax.ShapeDtypeStruct(block, BF16)] * 4
+        + [
+            jax.ShapeDtypeStruct((length, model), F32),
+            jax.ShapeDtypeStruct((groups, 1, hidden), F32),
+            jax.ShapeDtypeStruct(tokens.shape, BF16),
+            jax.ShapeDtypeStruct(tokens.shape, BF16),
+            whole,
+            whole,
+            whole,
+        ],
+        in_specs=[anywhere] * 5
+        + spec_list(
+            [
+                (biases.shape, 0), (qaug.shape, 0), (kaug.shape, 0), (vaug.shape, 0),
+                (b_mixer.shape, 0),
+            ]
+        ),
+        out_specs=spec_list([(block, 1)] * 4 + [((length, model), 0), ((groups, 1, hidden), 1)])
+        + [anywhere] * 5,
+        scratch_shapes=[
+            pltpu.VMEM((4, model, PAD), BF16),
+            pltpu.VMEM(tokens.shape, BF16),
+            pltpu.VMEM(whole.shape, BF16),
+            pltpu.VMEM((groups,) + biases.shape, F32),
+            pltpu.SemaphoreType.DMA((FORWARD_WIRES,)),
+            pltpu.SemaphoreType.DMA((FORWARD_WIRES,)),
+            pltpu.SemaphoreType.DMA((8,)),
+        ],
+        compiler_params=pltpu.CompilerParams(
+            vmem_limit_bytes=VMEM_LIMIT, collective_id=0, has_side_effects=True
+        ),
+        name="attend_forward",
+    )(tokens, cotangent, shard_a, shard_i, shard_o, biases, qaug, kaug, vaug, b_mixer)
+
+
+def attend_plain(x, a_all, biases, qaug, kaug, vaug, b_mixer):
     length, model = x.shape
     groups = a_all.shape[0]
     block = (groups, length, PAD)
     return pl.pallas_call(
-        attend_kernel,
+        attend_plain_kernel,
         grid=(groups,),
         out_shape=[jax.ShapeDtypeStruct(block, BF16)] * 4 + [jax.ShapeDtypeStruct(x.shape, F32)],
         in_specs=spec_list(
             [
-                (x.shape, 0), (a_all.shape, 1), (bq.shape, 1), (bv.shape, 1),
+                (x.shape, 0), (a_all.shape, 1), (biases.shape, 1),
                 (qaug.shape, 0), (kaug.shape, 0), (vaug.shape, 0), (b_mixer.shape, 0),
             ]
         ),
         out_specs=spec_list([(block, 1)] * 4 + [(x.shape, 0)]),
         scratch_shapes=[pltpu.VMEM((4, model, PAD), BF16)],
         compiler_params=pltpu.CompilerParams(vmem_limit_bytes=VMEM_LIMIT),
-        name="attend_forward",
-    )(x, a_all, bq, bv, qaug, kaug, vaug, b_mixer)
+        name="attend_plain",
+    )(x, a_all, biases, qaug, kaug, vaug, b_mixer)
 
 
 def dense_both(first_sum, wi, wo, bi, vectors, cotangent):
@@ -449,29 +787,12 @@
     return qaug, kaug, vaug
 
 
-def pad_groups(vector, groups, width):
-    parts = vector.reshape(groups, 1, width)
-    return jnp.pad(parts, ((0, 0), (0, 0), (0, PAD - width)))
-
-
-def one_sequence(x, labels, a_all, wi, wo, bq, bv, bi, b_mixer, vectors, cotangent):
-    groups = a_all.shape[0]
-    width = a_all.shape[2] // 4
-    qaug, kaug, vaug = augment(labels, width)
-    q, k, v, attended, first_sum = attend_forward(
-        x, a_all, pad_groups(bq, groups, width), pad_groups(bv, groups, width),
-        qaug, kaug, vaug, b_mixer[None],
+def after_attention(first_sum, a_all, wi, wo, bi, vectors, x, cot, saved):
+    out, d_first, d_mixed, g_inner, g_outer, db_inner, small = dense_both(
+        first_sum, wi, wo, bi, vectors, cot
     )
-    out, d_first, d_mixed, g_inner, g_outer, db_inner, small = dense_both(
-        first_sum, wi, wo, bi.reshape(groups, 1, -1), vectors, cotangent
-    )
-    d_tokens, g_attend, dbq, dbv = attend_backward(
-        x, a_all, d_mixed, d_first, q, k, v, attended
-    )
-    return (
-        out, d_tokens, g_attend, g_inner, g_outer,
-        dbq[:, 0, :width], dbv[:, 0, :width], db_inner[:, 0], small,
-    )
+    d_tokens, g_attend, dbq, dbv = attend_backward(x, a_all, d_mixed, d_first, *saved)
+    return out, d_tokens, g_attend, g_inner, g_outer, dbq, dbv, db_inner, small
 
 
 def body(
@@ -479,50 +800,64 @@
     bias_one, w_inner, b_inner, w_outer, b_outer, gain_two, bias_two, cotangent,
 ):
     groups = lax.axis_size("tensor")
+    rings = lax.axis_size("dp")
     place = lax.axis_index("tensor")
     width = w_query.shape[1]
     hidden = w_inner.shape[1]
     length = doc_ids.shape[2]
     model = tokens.shape[3]
-
-    def to_sequence(part):
-        return lax.all_to_all(part, "tensor", 0, 2, tiled=True).reshape(length, model)
+    near = groups == 4 and rings == 8
+
+    labels = lax.dynamic_index_in_dim(doc_ids[:, 0], place, 0, keepdims=False)
+    qaug, kaug, vaug = augment(labels, width)
+    shard_a = jnp.concatenate([w_query, w_key, w_value, w_mixer.T], axis=1)
+    shard_o = w_outer.T
+    spare = jnp.zeros((PAD - width,), F32)
+    biases = jnp.concatenate([b_query, spare, b_value, spare, b_inner])[None]
+    vectors = jnp.stack([gain_one, bias_one, b_outer, gain_two, bias_two] + [b_outer] * 3)
+    if near:
+        *saved, first_sum, bi, x, cot, a_all, wi, wo = attend_forward(
+            tokens[:, 0], cotangent[:, 0], shard_a, w_inner, shard_o, biases, qaug, kaug, vaug,
+            b_mixer[None],
+        )
+        a_all, wi, wo = (part.reshape(groups, model, model) for part in (a_all, wi, wo))
+        x, cot = (part.reshape(length, model) for part in (x, cot))
+        order = jnp.bitwise_xor(place, jnp.arange(groups))
+    else:
+
+        def gather(shard):
+            whole = lax.all_gather(shard, ("tensor", "dp"), axis=0, tiled=True)
+            return whole.reshape(groups, model, shard.shape[1])
+
+        def to_sequence(part):
+            return lax.all_to_all(part, "tensor", 0, 2, tiled=True).reshape(length, model)
+
+        x, cot = to_sequence(tokens), to_sequence(cotangent)
+        a_all, wi, wo = gather(shard_a), gather(w_inner), gather(shard_o)
+        every = lax.all_gather(biases, "tensor", axis=0)
+        *saved, first_sum = attend_plain(x, a_all, every, qaug, kaug, vaug, b_mixer[None])
+        bi = every[:, :, 2 * PAD :]
+        order = jnp.arange(groups)
+    out, d_tokens, *grads = after_attention(
+        first_sum, a_all, wi, wo, bi, vectors, x, cot, saved
+    )
+    g_attend, g_inner, g_outer, dbq, dbv, dbi, small = grads
 
     def from_sequence(whole):
         return lax.all_to_all(whole.reshape(1, 1, length, model), "tensor", 2, 0, tiled=True)
 
-    x = to_sequence(tokens)
-    cot = to_sequence(cotangent)
-    labels = lax.dynamic_index_in_dim(doc_ids[:, 0], place, 0, keepdims=False)
-    shard_a = jnp.concatenate([w_query, w_key, w_value, w_mixer.T], axis=1)
-
-    def gather(shard):
-        whole = lax.all_gather(shard, ("tensor", "dp"), axis=0, tiled=True)
-        return whole.reshape(groups, model, shard.shape[1])
-
-    a_all = gather(shard_a)
-    wi = gather(w_inner)
-    wo = gather(w_outer.T)
-    biases = lax.all_gather(jnp.concatenate([b_query, b_value, b_inner]), "tensor", axis=0)
-    bq = biases[:, :width].reshape(-1)
-    bv = biases[:, width : 2 * width].reshape(-1)
-    bi = biases[:, 2 * width :].reshape(-1)
-    vectors = jnp.stack([gain_one, bias_one, b_outer, gain_two, bias_two] + [b_outer] * 3)
-    out, d_tokens, g_attend, g_inner, g_outer, dbq, dbv, dbi, small = one_sequence(
-        x, labels, a_all, wi, wo, bq, bv, bi, b_mixer, vectors, cot
-    )
-
-    def scatter(grads):
-        flat = grads.reshape(-1, grads.shape[2])
+    def by_place(part):
+        return jnp.take(part, order, axis=0) if near else part
+
+    def scatter(part):
+        flat = by_place(part).reshape(-1, part.shape[2])
         return lax.psum_scatter(flat, ("tensor", "dp"), scatter_dimension=0, tiled=True)
 
     ga = scatter(g_attend).astype(F32)
     gi = scatter(g_inner).astype(F32)
     go = scatter(g_outer).astype(F32)
-    summed = lax.psum(
-        jnp.concatenate([dbq.reshape(-1), dbv.reshape(-1), dbi.reshape(-1), small.reshape(-1)]),
-        ("dp", "tensor"),
-    )
+    rows = [by_place(dbq[:, 0, :width]), by_place(dbv[:, 0, :width]), by_place(dbi[:, 0]), small]
+    summed = lax.psum(jnp.concatenate([part.reshape(-1) for part in rows]), ("dp", "tensor"))
     mine = lambda start, size: lax.dynamic_slice_in_dim(summed, start + place * size, size)
     tail = summed[2 * model + dbi.size :].reshape(8, model)
     return (

time: 692 us -> 643 us (0.929)
  waiting for transfers between devices: 329 us -> 209 us
  Pallas kernels: 175 us -> 247 us
  blocking collectives: 101 us -> 77.1 us
  local copies, waits for them, and re-layouts: 35.5 us -> 56.7 us
  other arithmetic: 19.3 us -> 30.7 us
  starting transfers between devices: 15.8 us -> 7.62 us
    all_gather x3 -> x0, waiting for transfers between devices: 122 us -> none  [gather(): whole = lax.all_gather(shard, ('tensor', 'dp'), axis=0, tiled=True)]
    pallas_call x1, Pallas kernels: 42.1 us -> 114 us  [attend_forward(): pl.pallas_call(attend_kernel, grid=(groups,), out_shape=[jax.ShapeDtypeSt...]
    all_gather x1 -> x0, blocking collectives: 22 us -> none  [body(): lax.all_gather(jnp.concatenate([b_query, b_value, b_inner]), 'tensor', ax...]
    gather x0 -> x6, local copies, waits for them, and re-layouts: none -> 17.8 us  [by_place(): return jnp.take(part, order, axis=0) if near else part]
    select_n x0 -> x5, other arithmetic: none -> 11.4 us  [by_place(): return jnp.take(part, order, axis=0) if near else part]
    all_to_all x2 -> x0, starting transfers between devices: 7.93 us -> none  [to_sequence(): lax.all_to_all(part, 'tensor', 0, 2, tiled=True).reshape(length, model)]
    unnamed x50 -> x27, local copies, waits for them, and re-layouts: 19.4 us -> 19.3 us
  transfers between devices with their start and end apart: 10 -> 5, of which waited for: 6 -> 3; matrix products, arithmetic and copies ran while one was open for 7% -> 7% of each run, Pallas kernels for 6% -> 0%
where the time goes in v2:
time: 643 us; the launch traced here: 642 us
  Pallas kernels  247 us (38%)
  waiting for transfers between devices  209 us (33%)
  blocking collectives  77.1 us (12%)
  local copies, waits for them, and re-layouts  56.7 us (9%)
  other arithmetic  30.7 us (5%)
  between operations  14 us (2%)
  starting transfers between devices  7.62 us (1%)
    reduce_scatter x2, waiting for transfers between devices, scatter(): lax.psum_scatter(flat, ('tensor', 'dp'), scatter_dimension=0, tiled=True)  194 us
    pallas_call x1, Pallas kernels, attend_forward(): pl.pallas_call(attend_kernel, grid=(groups,), out_shape=[jax.ShapeDtypeSt...  114 us
    psum x1, blocking collectives, body(): lax.psum(jnp.concatenate([part.reshape(-1) for part in rows]), ('dp', 'te...  77.1 us
    pallas_call x1, Pallas kernels, attend_backward(): pl.pallas_call(attend_back_kernel, grid=(groups,), out_shape=[jax.ShapeDt...  74.7 us
    pallas_call x1, Pallas kernels, dense_both(): pl.pallas_call(dense_kernel, grid=(2 * groups,), out_shape=[jax.ShapeDtyp...  58.1 us
    unnamed x27, local copies, waits for them, and re-layouts  19.3 us
    gather x6, local copies, waits for them, and re-layouts, by_place(): return jnp.take(part, order, axis=0) if near else part  17.8 us
    all_to_all x2, waiting for transfers between devices, from_sequence(): lax.all_to_all(whole.reshape(1, 1, length, model), 'tensor', 2, 0, tiled=...  13.2 us
  transfers between devices with their start and end apart: 5, of which 3 were waited for; matrix products, arithmetic and copies ran while one was open for 7% of the time, Pallas kernels for 0%

profile of v2, /device:TPU:0, one launch (start us, length us, event | category | flops | bytes accessed | tf_op | source)
XLA Modules:
  0.0 641.5 jit_solution(7718903989558413570)
XLA Ops:
  7.9 1.1 select_convert_fusion.1.qaug_ref
  9.0 1.1 select_convert_fusion.kaug_ref
  10.1 0.9 copy.51
  11.0 0.8 concatenate.10
  12.4 1.3 broadcast_in_dim.73.bm_ref
  17.1 1.6 pad_maximum_fusion.sa_ref
  19.3 113.8 %attend_forward.1 = (bf16[4,1024,256]{2,1,0:T(8,128)(2,1)}, bf16[4,1024,256]{2,1,0:T(8,128)(2,1)}, bf16[4,1024,256]{2,1,0:T(8,128)(2,1)}, bf16[4,1024,256]{2,1,0...) custom-call(bf16[4,256,768]{2,1,0:T(8,128)(2,1)} %bitcast.51, ...), custom_call_target="tpu_custom_call" | custom-call | tf_op jit(solution)/shard_map/attend_forward/pallas_call | solution.py:636
  133.1 58.1 %dense_both.1 = (bf16[1024,768]{1,0:T(8,128)(2,1)}, f32[1024,768]{1,0:T(8,128)}, bf16[1024,768]{1,0:T(8,128)(2,1)}, bf16[4,768,768]{2,1,0:T(8,128)(2,1)}, bf16[4...) custom-call(f32[1024,768]{1,0:T(8,128)} %get-tuple-element.41.first_in, ...), custom_call_target="tpu_custom_call" | custom-call | tf_op jit(solution)/shard_map/dense_both/pallas_call | solution.py:705
  191.2 74.7 %attend_backward.1 = (f32[1024,768]{1,0:T(8,128)}, bf16[4,768,768]{2,1,0:T(8,128)(2,1)}, f32[4,1,256]{2,1,0:T(1,128)}, f32[4,1,256]{2,1,0:T(1,128)}) custom-call(bf16[1024,768]{1,0:T(8,128)(2,1)} %bitcast.53, bf16[4,768,768]{2,1,0:T(8,128)(2,1)} %bitcast.47, bf16[1024,768]{1,0:T(8,128)(2,1)} %get-tuple-element.49.dmix_ref, ...), custom_call_target="tpu_custom_call" | custom-call | tf_op jit(solution)/shard_map/attend_backward/pallas_call | solution.py:746
  265.9 5.4 gather_fusion.1
  271.4 5.3 gather_fusion.5
  276.6 5.4 gather_fusion.4
  282.0 11.3 %broadcast_select_fusion = (bf16[4,768,768]{2,1,0:T(8,128)(2,1)}, bf16[4,768,768]{2,1,0:T(8,128)(2,1)}, bf16[4,768,768]{2,1,0:T(8,128)(2,1)}) fusion(bf16[4,768,768]{2,1,0:T(8,128)(2,1)} %gather_fusion.5, pred[4]{0:T(512)(128)(4,1)S(1)} %compare_and_fusion.1, bf16[4,768,768]{2,1,0:T(8,128)(2,1)} %gather_fusion.4, bf16[4,768,768]{2,1,0:T(8,128)(2,1)} %gather_fusion.1), kind=kLoop, calls=%fused_computation.6 | loop fusion | flops 7077888 | bytes 28311556 | tf_op jit(solution)/shard_map/jit(_take)/select_n | solution.py:850
  294.8 3.8 copy.73
  299.2 11.6 %reduce = bf16[1024,768]{1,0:T(8,128)(2,1)} reduce(bf16[1024,1,1,768]{3,2,1,0:T(2,128)(2,1)S(1)} %bitcast.45, bf16[]{:T(256)} %broadcast.196), dimensions={1,2}, to_apply=%bitcast.38.reduce_sub_computation | reduce | bytes 3145730
  310.8 3.7 reshape.249
  314.5 3.6 all-to-all-start
  318.1 6.8 %copy.53 = f32[1,1,1024,768]{3,1,0,2:T(1,128)} copy(f32[1,1,1024,768]{3,2,1,0:T(8,128)} %bitcast.50) | data formatting | bytes 6291456 | tf_op jit(solution)/shard_map/reshape | solution.py:847
  324.9 13.2 %all-to-all-done = bf16[4,2,98304]{2,1,0:T(2,128)(2,1)S(1)} async-done(((bf16[4,2,98304]{2,1,0:T(2,128)(2,1)}), bf16[4,2,98304]{2,1,0:T(2,128)(2,1)S(1)}, u32[]{:S(2)}, u32[]{:S(2)}) %all-to-all-start) | async-done | bytes 1572896 | tf_op jit(solution)/shard_map/all_to_all | solution.py:847
  338.1 1.1 copy-done.2
  339.3 3.9 all-to-all-start.1
  345.3 77.1 %psum.7 = f32[10752]{0:T(1024)S(1)} all-reduce(f32[10752]{0:T(1024)S(1)} %pad_maximum_fusion.1), channel_id=1, replica_groups=mesh['dp'=8,'tensor'=4] {'dp','tensor'}, use_global_device_ids=true, to_apply=%region_1.4 | all-reduce | flops 10752 | bytes 86016 | tf_op jit(solution)/shard_map/psum | solution.py:860
  423.8 4.5 reshape.250
  428.2 3.4 copy.62
  431.6 1.9 copy.56
  433.5 1.1 copy.61
  434.6 0.7 copy.57
  435.3 0.7 copy.58
  437.4 84.3 %reduce-scatter.8.cloned.1.call-done = bf16[96,768]{1,0:T(8,128)(2,1)} async-done(((bf16[3072,768]{1,0:T(8,128)(2,1)}), bf16[96,768]{1,0:T(8,128)(2,1)}) %reduce-scatter.8.cloned.1.call-update) | async-done | bytes 147472 | tf_op jit(solution)/shard_map/reduce_scatter | solution.py:854
  521.8 1.6 convert_bitcast_fusion
  523.4 109.9 %reduce-scatter.6.cloned.1.call-done = bf16[96,768]{1,0:T(8,128)(2,1)} async-done(((bf16[3072,768]{1,0:T(8,128)(2,1)}), bf16[96,768]{1,0:T(8,128)(2,1)}) %reduce-scatter.6.cloned.1.call-update) | async-done | bytes 147472 | tf_op jit(solution)/shard_map/reduce_scatter | solution.py:854
  633.3 1.6 convert_element_type.20
  (59 shorter events, 12.2 us)
Async XLA Ops:
  7.2 0.7 copy-start
  7.2 426.3 %reduce-scatter.10.cloned.1.call-start = ((), (), s32[]{:S(2)}) async-start(), calls=%async_computation.7 | async-start | bytes 4866048
  293.3 228.4 %reduce-scatter.8.cloned.1.call-start = ((), (), s32[]{:S(2)}) async-start(), calls=%async_computation.6 | async-start | bytes 4866048 | tf_op jit(solution)/shard_map/reduce_scatter | solution.py:854
  294.1 339.2 %reduce-scatter.6.cloned.1.call-start = ((), (), s32[]{:S(2)}) async-start(), calls=%async_computation.5 | async-start | bytes 4866048 | tf_op jit(solution)/shard_map/reduce_scatter | solution.py:854
  314.5 23.6 %all-to-all-start = ((bf16[4,2,98304]{2,1,0:T(2,128)(2,1)}), bf16[4,2,98304]{2,1,0:T(2,128)(2,1)S(1)}, u32[]{:S(2)}, u32[]{:S(2)}) async-start(bf16[4,2,98304]{2,1,0:T(2,128)(2,1)} %reshape.249), calls=%async_computation | async-start | bytes 3145728 | tf_op jit(solution)/shard_map/all_to_all | solution.py:847
  324.9 18.3 %copy-start.6 = (f32[4,1,256]{2,1,0:T(1,128)S(1)}, f32[4,1,256]{2,1,0:T(1,128)}, u32[]{:S(2)}) copy-start(f32[4,1,256]{2,1,0:T(1,128)} %get-tuple-element.57) | copy-start | bytes 12292
  324.9 18.9 %copy-start.5 = (f32[4,1,256]{2,1,0:T(1,128)S(1)}, f32[4,1,256]{2,1,0:T(1,128)}, u32[]{:S(2)}) copy-start(f32[4,1,256]{2,1,0:T(1,128)} %get-tuple-element.58) | copy-start | bytes 12292
  324.9 19.7 %copy-start.4 = (f32[4,1,768]{2,1,0:T(1,128)S(1)}, f32[4,1,768]{2,1,0:T(1,128)}, u32[]{:S(2)}) copy-start(f32[4,1,768]{2,1,0:T(1,128)} %get-tuple-element.59) | copy-start | bytes 36868
  324.9 20.4 %copy-start.3 = (f32[8,768]{1,0:T(8,128)S(1)}, f32[8,768]{1,0:T(8,128)}, u32[]{:S(2)}) copy-start(f32[8,768]{1,0:T(8,128)} %get-tuple-element.60) | copy-start | bytes 73732
  338.1 1.1 copy-start.2
  339.3 92.3 %all-to-all-start.1 = ((f32[1,1,1024,768]{3,1,0,2:T(1,128)}), f32[1,1,1024,768]{3,1,0,2:T(1,128)S(1)}, u32[]{:S(2)}, u32[]{:S(2)}) async-start(f32[1,1,1024,768]{3,1,0,2:T(1,128)} %copy.53), calls=%async_computation.1 | async-start | bytes 6291456 | tf_op jit(solution)/shard_map/all_to_all | solution.py:847
  431.6 203.4 %copy-start.1 = (s32[4,1,1024]{2,1,0:T(1,128)S(1)}, s32[4,1,1024]{2,1,0:T(1,128)}, u32[]{:S(2)}) copy-start(s32[4,1,1024]{2,1,0:T(1,128)} %param.23) | copy-start | bytes 49156
Sparse Core Ops, SparseCore 0:
  293.5 115.7 reduce-scatter.9
  415.6 106.1 reduce-scatter.7
  527.2 106.0 reduce-scatter.5

commit v3 on v2

--- a/solution.py
+++ b/solution.py
@@ -520,20 +520,75 @@
             dmix_ref[rows, :] = d_first.astype(BF16)
 
 
+def back_rows(rows, width, w_s, dmix_rows, q_ref, k_ref, v_ref, att_ref, kt_s, dq_s, dk_s, dv_s):
+    lanes = lane_index((ROWS, PAD))
+    queries = q_ref[0, rows, :]
+    d_att = dot_nn(dmix_rows, w_s[3]).astype(BF16)
+    product = d_att.astype(F32) * att_ref[0, rows, :].astype(F32)
+    heads = range(width // HEAD)
+    extended = d_att
+    for head in heads:
+        centre = jnp.sum(jnp.where(head_only(lanes, head), product, 0.0), axis=1, keepdims=True)
+        for spot, part in enumerate(three_parts(-centre)):
+            here = lanes == width + DOCS + 3 * head + spot
+            extended = jnp.where(here, jnp.broadcast_to(part, (ROWS, PAD)), extended)
+    chances_all = []
+    d_scores_all = []
+    d_att_all = []
+    queries_all = []
+    for head in heads:
+        wide = head_and_extra(lanes, head, width)
+        only = head_only(lanes, head)
+        chances = jnp.exp2(dot_nt(k_ref[0], jnp.where(wide, queries, 0)) * LOG2E)
+        d_chances = dot_nt(v_ref[0], jnp.where(wide, extended, 0))
+        d_scores = (chances * d_chances).astype(BF16)
+        chances_all.append(chances.astype(BF16))
+        d_scores_all.append(d_scores)
+        d_att_all.append(jnp.where(only, d_att, 0))
+        queries_all.append(jnp.where(only, queries, 0))
+        head_rows = slice(head * HEAD, (head + 1) * HEAD)
+        dq_s[head_rows, rows] = dot_nn(kt_s[head_rows, :], d_scores)
+    dv_s[...] += dot_nn(jnp.concatenate(chances_all, 1), jnp.concatenate(d_att_all, 0))
+    dk_s[...] += dot_nn(jnp.concatenate(d_scores_all, 1), jnp.concatenate(queries_all, 0))
+
+
+def back_low(rows, width, dq_s, dk_s, dv_s, low_s):
+    d_query = (dq_s[:, rows].T * HEAD**-0.5).astype(BF16)
+    d_query = jnp.where(lane_index(d_query.shape) < width, d_query, 0)
+    d_value = dv_s[rows, :].astype(BF16)
+    low_s[0, rows, :] = d_query
+    low_s[1, rows, :] = dk_s[rows, :].astype(BF16)
+    low_s[2, rows, :] = d_value
+    return column_sum(d_query.astype(F32)), column_sum(d_value.astype(F32))
+
+
+def back_tokens(rows, w_s, low_s):
+    return sum(dot_nt(low_s[slot, rows, :], w_s[slot]) for slot in range(3))
+
+
+def back_weights(rows, width, slots, xt_s, dmixt_s, low_s, att_ref):
+    parts = []
+    for slot in slots:
+        if slot < 3:
+            part = dot_nn(xt_s[rows, :], low_s[slot])
+        else:
+            part = dot_nn(dmixt_s[rows, :], att_ref[0])
+        parts.append(part[:, :width])
+    return jnp.concatenate(parts, axis=1).astype(BF16)
+
+
 def attend_back_kernel(
     x_ref, a_ref, dmix_ref, dfirst_ref, q_ref, k_ref, v_ref, att_ref,
     dtok_ref, ga_ref, dbq_ref, dbv_ref,
-    w_s, xt_s, dmixt_s, do_s, kt_s, dq_s, dk_s, dv_s, low_s,
+    w_s, xt_s, dmixt_s, kt_s, dq_s, dk_s, dv_s, low_s,
 ):
-    step = pl.program_id(0)
     length, model = x_ref.shape
     width = a_ref.shape[2] // 4
-    heads = width // HEAD
     blocks = length // ROWS
     for slot in range(4):
         w_s[slot] = unpack(a_ref.at[0], slot, width)
 
-    @pl.when(step == 0)
+    @pl.when(pl.program_id(0) == 0)
     def _():
         dtok_ref[...] = dfirst_ref[...]
 
@@ -543,9 +598,8 @@
             xt_s[:, rows] = x_ref[rows, :].T
             dmixt_s[:, rows] = dmix_ref[rows, :].T
 
-    dk_s[...] = jnp.zeros_like(dk_s)
-    dv_s[...] = jnp.zeros_like(dv_s)
-    lanes = lane_index((ROWS, PAD))
+    for sums in (dk_s, dv_s, dbq_ref, dbv_ref):
+        sums[...] = jnp.zeros_like(sums)
 
     @pl.loop(0, blocks)
     def _(index):
@@ -555,59 +609,363 @@
     @pl.loop(0, blocks)
     def _(index):
         rows = rows_of(index)
-        queries = q_ref[0, rows, :]
-        d_att = dot_nn(dmix_ref[rows, :], w_s[3]).astype(BF16)
-        product = d_att.astype(F32) * att_ref[0, rows, :].astype(F32)
-        extended = d_att
-        for head in range(heads):
-            centre = jnp.sum(jnp.where(head_only(lanes, head), product, 0.0), axis=1, keepdims=True)
-            for place, part in enumerate(three_parts(-centre)):
-                here = lanes == width + DOCS + 3 * head + place
-                extended = jnp.where(here, jnp.broadcast_to(part, (ROWS, PAD)), extended)
-        chances_all = []
-        d_scores_all = []
-        d_att_all = []
-        queries_all = []
-        for head in range(heads):
-            wide = head_and_extra(lanes, head, width)
-            only = head_only(lanes, head)
-            chances = jnp.exp2(dot_nt(k_ref[0], jnp.where(wide, queries, 0)) * LOG2E)
-            d_chances = dot_nt(v_ref[0], jnp.where(wide, extended, 0))
-            d_scores = (chances * d_chances).astype(BF16)
-            chances_all.append(chances.astype(BF16))
-            d_scores_all.append(d_scores)
-            d_att_all.append(jnp.where(only, d_att, 0))
-            queries_all.append(jnp.where(only, queries, 0))
-            head_rows = slice(head * HEAD, (head + 1) * HEAD)
-            dq_s[head_rows, rows] = dot_nn(kt_s[head_rows, :], d_scores)
-        dv_s[...] += dot_nn(jnp.concatenate(chances_all, 1), jnp.concatenate(d_att_all, 0))
-        dk_s[...] += dot_nn(jnp.concatenate(d_scores_all, 1), jnp.concatenate(queries_all, 0))
-
-    dbq_ref[...] = jnp.zeros_like(dbq_ref)
-    dbv_ref[...] = jnp.zeros_like(dbv_ref)
+        dmix_rows = dmix_ref[rows, :]
+        back_rows(
+            rows, width, w_s, dmix_rows, q_ref, k_ref, v_ref, att_ref, kt_s, dq_s, dk_s, dv_s
+        )
 
     @pl.loop(0, blocks)
     def _(index):
         rows = rows_of(index)
-        d_query = (dq_s[:, rows].T * HEAD**-0.5).astype(BF16)
-        d_query = jnp.where(lane_index(d_query.shape) < width, d_query, 0)
-        d_key = dk_s[rows, :].astype(BF16)
-        d_value = dv_s[rows, :].astype(BF16)
-        low_s[0, rows, :] = d_query
-        low_s[1, rows, :] = d_key
-        low_s[2, rows, :] = d_value
-        dbq_ref[0] += column_sum(d_query.astype(F32))
-        dbv_ref[0] += column_sum(d_value.astype(F32))
-        dtok_ref[rows, :] += (
-            dot_nt(d_query, w_s[0]) + dot_nt(d_key, w_s[1]) + dot_nt(d_value, w_s[2])
-        )
+        for_query, for_value = back_low(rows, width, dq_s, dk_s, dv_s, low_s)
+        dbq_ref[0] += for_query
+        dbv_ref[0] += for_value
+        dtok_ref[rows, :] += back_tokens(rows, w_s, low_s)
 
     @pl.loop(0, model // ROWS)
     def _(index):
         rows = rows_of(index)
-        parts = [dot_nn(xt_s[rows, :], low_s[slot])[:, :width] for slot in range(3)]
-        parts.append(dot_nn(dmixt_s[rows, :], att_ref[0])[:, :width])
-        ga_ref[0, rows, :] = jnp.concatenate(parts, axis=1).astype(ga_ref.dtype)
+        ga_ref[0, rows, :] = back_weights(rows, width, range(4), xt_s, dmixt_s, low_s, att_ref)
+
+
+def add_into(target, source):
+    target[...] = (target[...].astype(F32) + source[...].astype(F32)).astype(target.dtype)
+
+
+class Reduce:
+    COUNT = 11
+
+    def __init__(self, wires, base, held, core, by_y, by_z, by_x):
+        self.wires, self.base, self.held, self.core = wires, base, held, core
+        self.by_y, self.by_z, self.by_x = by_y, by_z, by_x
+        self.z, self.y = lax.div(wires.row, 2), lax.rem(wires.row, 2)
+
+    def core_copy(self, j, source):
+        return self.wires.copy(self.base + j, source, self.core.at[j], 1, 0)
+
+    def add_core(self, j):
+        self.core_copy(j, self.held.at[j]).wait_recv()
+        for z in range(4):
+            for y in range(2):
+                add_into(self.held.at[j, z, y], self.core.at[j, z, y])
+
+    def y_copy(self, j):
+        source = self.held.at[j, :, 1 - self.y]
+        return self.wires.copy(self.base + 2 + j, source, self.by_y.at[j], 0, 1)
+
+    def add_y(self, j):
+        self.y_copy(j).wait_recv()
+        for z in range(4):
+            add_into(self.held.at[j, z, self.y], self.by_y.at[j, z])
+
+    def z_copy(self, j, step):
+        source = self.held.at[j, lax.div(partner(self.wires.row, 2 * step, 8), 2), self.y]
+        number = self.base + 4 + 3 * j + step - 1
+        return self.wires.copy(number, source, self.by_z.at[j, step - 1], 0, 2 * step)
+
+    def start_z(self, j):
+        for step in (1, 2, 3):
+            self.z_copy(j, step).start()
+
+    def total_z(self, j):
+        total = self.held[j, self.z, self.y].astype(F32)
+        for step in (1, 2, 3):
+            self.z_copy(j, step).wait_recv()
+            total = total + self.by_z[j, step - 1].astype(F32)
+        return total
+
+    def x_copy(self):
+        source = self.held.at[1, self.z, self.y]
+        return self.wires.copy(self.base + 10, source, self.by_x, 2, 0)
+
+    def send_x(self):
+        self.held[1, self.z, self.y] = self.total_z(1).astype(BF16)
+        self.x_copy().start()
+
+    def whole_x_copy(self):
+        return self.wires.copy(self.base + 10, self.held.at[1], self.by_x, 2, 0)
+
+    def add_whole_x(self):
+        self.whole_x_copy().wait_recv()
+        for z in range(4):
+            for y in range(2):
+                add_into(self.held.at[0, z, y], self.by_x.at[z, y])
+
+    def wait_sent(self, j_all):
+        for j in j_all:
+            self.y_copy(j).wait_send()
+            for step in (1, 2, 3):
+                self.z_copy(j, step).wait_send()
+
+
+OUTPUTS, TOKEN_GRADS, SUMS, LATE_SUMS = 0, 3, 6, 11
+RED_I = 16
+RED_O = RED_I + Reduce.COUNT
+RED_A = RED_O + Reduce.COUNT
+BACKWARD_WIRES = RED_A + 2 * Reduce.COUNT
+HOPS = ((1, 0), (2, 0), (0, 1), (0, 2), (0, 4))
+
+
+def slot_at(step):
+    return jnp.where(step < 2, 3 - 2 * step, 6 - 2 * step)
+
+
+def attend_reduce_kernel(
+    x_ref, a_ref, dmix_ref, dfirst_ref, q_ref, k_ref, v_ref, att_ref, gi_ref, go_ref, out_ref,
+    dbi_ref, small_ref,
+    out_res, dtok_res, ga_one, ga_two, gi_res, go_res, sum_res, late_res,
+    w_s, xt_s, dmixt_s, kt_s, dq_s, dk_s, dv_s, low_s, dmix_s, dtok_s, dlow_s, sums_s, late_s,
+    sums_r, late_r,
+    held_i, core_i, y_i, z_i, x_i, held_o, core_o, y_o, z_o, x_o,
+    send_a, held_a, core_a, y_a, z_a, x_a,
+    send_sem, recv_sem, here_sem,
+):
+    step = pl.program_id(0)
+    place = lax.axis_index("tensor")
+    row = lax.axis_index("dp")
+    length, model = dmix_s.shape
+    quarters, part, _ = dlow_s.shape
+    width = a_ref.shape[2] // 4
+    blocks = length // ROWS
+    wires = Wires(send_sem, recv_sem, place, row)
+    inner = Reduce(wires, RED_I, held_i, core_i, y_i, z_i, x_i)
+    outer = Reduce(wires, RED_O, held_o, core_o, y_o, z_o, x_o)
+    attn = [
+        Reduce(
+            wires, RED_A + half * Reduce.COUNT, held_a.at[half], core_a.at[half], y_a.at[half],
+            z_a.at[half], x_a.at[half],
+        )
+        for half in range(2)
+    ]
+
+    def exchange(base, source, target, bits, mine):
+        other = partner(place, bits, 4)
+        return wires.copy(
+            base + bits - 1, source.at[other], target.at[place if mine else other], bits, 0
+        )
+
+    def hop(base, kept, got, number):
+        bits = HOPS[number]
+        return wires.copy(base + number, kept.at[number], got.at[number], *bits)
+
+    def add_hop(base, kept, got, number):
+        hop(base, kept, got, number).wait_recv()
+        kept[number + 1] = kept[number] + got[number]
+
+    def next_hop(base, kept, got, number):
+        add_hop(base, kept, got, number)
+        if number + 1 < len(HOPS):
+            hop(base, kept, got, number + 1).start()
+
+    loads = [
+        pltpu.make_async_copy(gi_ref.at[0], held_i.at[0], here_sem.at[0]),
+        pltpu.make_async_copy(gi_ref.at[2], held_i.at[1], here_sem.at[1]),
+        pltpu.make_async_copy(go_ref.at[0], held_o.at[0], here_sem.at[2]),
+        pltpu.make_async_copy(go_ref.at[2], held_o.at[1], here_sem.at[3]),
+        pltpu.make_async_copy(dmix_ref, dmix_s, here_sem.at[4]),
+        pltpu.make_async_copy(dfirst_ref, dtok_s, here_sem.at[5]),
+    ]
+    keep_out = pltpu.make_async_copy(out_ref.at[place], out_res.at[place], here_sem.at[6])
+    keep_dtok = pltpu.make_async_copy(dlow_s.at[place], dtok_res.at[place], here_sem.at[7])
+    load_x = pltpu.make_async_copy(x_ref, dlow_s, here_sem.at[8])
+
+    def core_sends(kind, source):
+        return [kind.core_copy(0, source.at[1]), kind.core_copy(1, source.at[3])]
+
+    @pl.when(step == 0)
+    def _():
+        for copy in loads:
+            copy.start()
+        load_x.start()
+        sums_s[0] = jnp.zeros_like(sums_s[0])
+        late_s[0] = jnp.zeros_like(late_s[0])
+        for bits in range(4):
+            sums_s[0, pl.ds(partner(place, bits, 4), 1), :] = dbi_ref[bits]
+        sums_s[0, 8:16, :] = small_ref[...]
+        greet(wires, PEERS)
+        for copy in core_sends(inner, gi_ref) + core_sends(outer, go_ref):
+            copy.start()
+        hop(SUMS, sums_s, sums_r, 0).start()
+        for copy in loads:
+            copy.wait()
+        load_x.wait()
+
+        @pl.loop(0, quarters)
+        def _(index):
+            rows = rows_of(index, part)
+            xt_s[:, rows] = dlow_s[index].T
+            dmixt_s[:, rows] = dmix_s[rows, :].T
+
+        for j in (1, 0):
+            inner.add_core(j)
+            inner.y_copy(j).start()
+        outer.add_core(1)
+        outer.whole_x_copy().start()
+        outer.add_core(0)
+        next_hop(SUMS, sums_s, sums_r, 0)
+
+    @pl.when(step == 3)
+    def _():
+        for reduce in attn:
+            reduce.add_core(1)
+            reduce.y_copy(1).start()
+
+    for slot in range(4):
+        w_s[slot] = unpack(a_ref.at[0], slot, width)
+    for sums in (dk_s, dv_s):
+        sums[...] = jnp.zeros_like(sums)
+
+    @pl.loop(0, blocks)
+    def _(index):
+        rows = rows_of(index)
+        kt_s[:, rows] = k_ref[0, rows, :].T
+
+    @pl.loop(0, blocks)
+    def _(index):
+        rows = rows_of(index)
+        dmix_rows = dmix_s[rows, :]
+        back_rows(
+            rows, width, w_s, dmix_rows, q_ref, k_ref, v_ref, att_ref, kt_s, dq_s, dk_s, dv_s
+        )
+
+        for number in range(1, 4):
+
+            @pl.when((step == 0) & (index == number))
+            def _(number=number):
+                next_hop(SUMS, sums_s, sums_r, number)
+
+        @pl.when((step == 1) & (index == 0))
+        def _():
+            add_hop(SUMS, sums_s, sums_r, 4)
+
+        @pl.when((step == 1) & (index == 2))
+        def _():
+            for j in (1, 0):
+                inner.add_y(j)
+                inner.start_z(j)
+
+        @pl.when((step == 1) & (index == 3))
+        def _():
+            outer.add_whole_x()
+            outer.y_copy(0).start()
+            for bits in (2, 3, 1):
+                exchange(OUTPUTS, out_ref, out_res, bits, True).start()
+            keep_out.start()
+
+        @pl.when((step == 2) & (index == 2))
+        def _():
+            outer.add_y(0)
+            outer.start_z(0)
+
+        @pl.when((step == 3) & (index == 1))
+        def _():
+            inner.send_x()
+
+        @pl.when((step == 3) & (index == 3))
+        def _():
+            for reduce in attn:
+                reduce.add_y(1)
+                reduce.start_z(1)
+
+    @pl.loop(0, blocks)
+    def _(index):
+        rows = rows_of(index)
+        for_query, for_value = back_low(rows, width, dq_s, dk_s, dv_s, low_s)
+        for number, bits in enumerate((3, 1, 2, 0)):
+
+            @pl.when(step == number)
+            def _(bits=bits):
+                late_s[0, pl.ds(partner(place, bits, 4), 1), :] += for_query
+                late_s[0, pl.ds(4 + partner(place, bits, 4), 1), :] += for_value
+
+    share = held_i.shape[3]
+    for half in range(2):
+
+        @pl.loop(0, model // (2 * share))
+        def _(z):
+            rows = pl.ds(pl.multiple_of(z * 2 * share, 2 * share), 2 * share)
+            slots = (0, 1) if half == 0 else (2, 3)
+            grads = back_weights(rows, width, slots, xt_s, dmixt_s, low_s, att_ref)
+            for y in range(2):
+                piece = grads[y * share : (y + 1) * share]
+
+                @pl.when(step < 2)
+                def _(y=y, piece=piece):
+                    send_a[half, step, z, y] = piece
+
+                @pl.when(step >= 2)
+                def _(y=y, piece=piece):
+                    held_a[half, 3 - step, z, y] = piece
+
+        for number, j in ((0, 1), (1, 0)):
+
+            @pl.when(step == number)
+            def _(number=number, j=j):
+                attn[half].core_copy(j, send_a.at[half, number]).start()
+
+        @pl.when(step == 3)
+        def _():
+            attn[half].add_core(0)
+            attn[half].y_copy(0).start()
+
+    @pl.when(step == 3)
+    def _():
+        hop(LATE_SUMS, late_s, late_r, 0).start()
+
+    @pl.loop(0, quarters)
+    def _(index):
+        rows = rows_of(index, part)
+        dtok_s[rows, :] += back_tokens(rows, w_s, low_s)
+
+        @pl.when(step == 3)
+        def _():
+            dlow_s[index] = dtok_s[rows, :].astype(BF16)
+
+    @pl.when(step == 3)
+    def _():
+        for bits in (2, 3, 1):
+            exchange(TOKEN_GRADS, dlow_s, dtok_res, bits, True).start()
+        keep_dtok.start()
+        next_hop(LATE_SUMS, late_s, late_r, 0)
+        go_res[...] = outer.total_z(0)
+        inner.x_copy().wait_recv()
+        gi_res[...] = inner.total_z(0) + x_i[...].astype(F32)
+        next_hop(LATE_SUMS, late_s, late_r, 1)
+        for reduce in attn:
+            reduce.send_x()
+        next_hop(LATE_SUMS, late_s, late_r, 2)
+        for reduce in attn:
+            reduce.add_y(0)
+            reduce.start_z(0)
+        next_hop(LATE_SUMS, late_s, late_r, 3)
+        add_hop(LATE_SUMS, late_s, late_r, 4)
+        sum_res[...] = sums_s[5]
+        late_res[...] = late_s[5]
+        for half, result in enumerate((ga_one, ga_two)):
+            attn[half].x_copy().wait_recv()
+            result[...] = attn[half].total_z(0) + x_a[half].astype(F32)
+        for bits in (1, 2, 3):
+            for base, source, target in (
+                (OUTPUTS, out_ref, out_res), (TOKEN_GRADS, dlow_s, dtok_res),
+            ):
+                exchange(base, source, target, bits, False).wait_recv()
+                exchange(base, source, target, bits, True).wait_send()
+        keep_out.wait()
+        keep_dtok.wait()
+        for number in range(len(HOPS)):
+            hop(SUMS, sums_s, sums_r, number).wait_send()
+            hop(LATE_SUMS, late_s, late_r, number).wait_send()
+        for copy in core_sends(inner, gi_ref) + core_sends(outer, go_ref):
+            copy.wait_send()
+        inner.wait_sent((0, 1))
+        inner.x_copy().wait_send()
+        outer.wait_sent((0,))
+        outer.whole_x_copy().wait_send()
+        for half, reduce in enumerate(attn):
+            for number, j in ((0, 1), (1, 0)):
+                reduce.core_copy(j, send_a.at[half, number]).wait_send()
+            reduce.wait_sent((0, 1))
+            reduce.x_copy().wait_send()
 
 
 VMEM_LIMIT = 60 * 1024 * 1024
@@ -763,7 +1121,6 @@
             pltpu.VMEM((4, model, PAD), BF16),
             pltpu.VMEM((model, length), BF16),
             pltpu.VMEM((model, length), BF16),
-            pltpu.VMEM((length, PAD), BF16),
             pltpu.VMEM((PAD, length), BF16),
             pltpu.VMEM((PAD, length), F32),
             pltpu.VMEM((length, PAD), F32),
@@ -773,6 +1130,61 @@
         compiler_params=pltpu.CompilerParams(vmem_limit_bytes=VMEM_LIMIT),
         name="attend_backward",
     )(x, a_all, d_mixed, d_first, q, k, v, attended)
+
+
+def attend_reduce(x, a_all, d_mixed, d_first, q, k, v, attended, g_inner, g_outer, out, dbi, small):
+    quarters, part, model = x.shape
+    length = quarters * part
+    share = model // 8
+    half = model // 2
+    block = (4, 2, share, model)
+    anywhere = pl.BlockSpec(memory_space=pl.ANY)
+
+    def ordered(shape):
+        return pl.BlockSpec(
+            (1,) + shape[1:], lambda step: (slot_at(step),) + (0,) * (len(shape) - 1)
+        )
+
+    def vmem(*shape, kind=BF16):
+        return pltpu.VMEM(shape, kind)
+
+    final = [
+        ((share, half), F32), ((share, half), F32), ((share, model), F32), ((share, model), F32),
+        ((16, model), F32), ((8, PAD), F32),
+    ]
+    return pl.pallas_call(
+        attend_reduce_kernel,
+        grid=(4,),
+        out_shape=[jax.ShapeDtypeStruct(x.shape, BF16)] * 2
+        + [jax.ShapeDtypeStruct(*each) for each in final],
+        in_specs=[anywhere, ordered(a_all.shape), anywhere, anywhere]
+        + [ordered(q.shape)] * 4
+        + [anywhere] * 3
+        + [resident(dbi.shape), resident(small.shape)],
+        out_specs=[anywhere] * 2 + [resident(each[0]) for each in final],
+        scratch_shapes=[
+            vmem(4, model, PAD), vmem(model, length), vmem(model, length), vmem(PAD, length),
+            vmem(PAD, length, kind=F32), vmem(length, PAD, kind=F32),
+            vmem(length, PAD, kind=F32), vmem(3, length, PAD), vmem(length, model),
+            vmem(length, model, kind=F32), vmem(quarters, part, model),
+            vmem(6, 16, model, kind=F32), vmem(6, 8, PAD, kind=F32),
+            vmem(5, 16, model, kind=F32), vmem(5, 8, PAD, kind=F32),
+            vmem(2, *block), vmem(2, *block), vmem(2, 4, share, model),
+            vmem(2, 3, share, model), vmem(share, model),
+            vmem(2, *block), vmem(2, *block), vmem(1, 4, share, model),
+            vmem(1, 3, share, model), vmem(*block),
+            vmem(2, 2, 4, 2, share, half), vmem(2, 2, 4, 2, share, half),
+            vmem(2, 2, 4, 2, share, half), vmem(2, 2, 4, share, half),
+            vmem(2, 2, 3, share, half), vmem(2, share, half),
+            pltpu.SemaphoreType.DMA((BACKWARD_WIRES,)),
+            pltpu.SemaphoreType.DMA((BACKWARD_WIRES,)),
+            pltpu.SemaphoreType.DMA((9,)),
+        ],
+        compiler_params=pltpu.CompilerParams(
+            vmem_limit_bytes=VMEM_LIMIT, collective_id=1, has_side_effects=True
+        ),
+        name="attend_reduce",
+    )(x, a_all, d_mixed, d_first, q, k, v, attended, g_inner, g_outer, out, dbi, small)
 
 
 def augment(labels, width):
@@ -785,14 +1197,6 @@
     kaug = jnp.where(in_docs & ~same, -(2.0**100), jnp.where(spare, 1.0, 0.0)).astype(BF16)
     vaug = jnp.where((lanes[:1] == width) | spare[:1], 1.0, 0.0).astype(BF16)
     return qaug, kaug, vaug
-
-
-def after_attention(first_sum, a_all, wi, wo, bi, vectors, x, cot, saved):
-    out, d_first, d_mixed, g_inner, g_outer, db_inner, small = dense_both(
-        first_sum, wi, wo, bi, vectors, cot
-    )
-    d_tokens, g_attend, dbq, dbv = attend_backward(x, a_all, d_mixed, d_first, *saved)
-    return out, d_tokens, g_attend, g_inner, g_outer, dbq, dbv, db_inner, small
 
 
 def body(
@@ -821,8 +1225,20 @@
             b_mixer[None],
         )
         a_all, wi, wo = (part.reshape(groups, model, model) for part in (a_all, wi, wo))
-        x, cot = (part.reshape(length, model) for part in (x, cot))
-        order = jnp.bitwise_xor(place, jnp.arange(groups))
+        out, d_first, d_mixed, g_inner, g_outer, dbi, small = dense_both(
+            first_sum, wi, wo, bi, vectors, cot.reshape(length, model)
+        )
+        pieces = (groups, 4, 2, model // rings, model)
+        out, d_tokens, ga_one, ga_two, gi, go, tail, late = attend_reduce(
+            x, a_all, d_mixed, d_first, *saved, g_inner.reshape(pieces), g_outer.reshape(pieces),
+            out.reshape(x.shape), dbi, small,
+        )
+        ga = jnp.concatenate([ga_one, ga_two], axis=1)
+        own = lambda whole, start: lax.dynamic_index_in_dim(whole, start + place, 0, False)
+        dbq, dbv = own(late, 0)[:width], own(late, groups)[:width]
+        dbi = own(tail, 0)
+        tail = tail[2 * groups :]
+        out, d_tokens = out[:, None], d_tokens[:, None].astype(F32)
     else:
 
         def gather(shard):
@@ -831,49 +1247,44 @@
 
         def to_sequence(part):
             return lax.all_to_all(part, "tensor", 0, 2, tiled=True).reshape(length, model)
+
+        def from_sequence(whole):
+            return lax.all_to_all(whole.reshape(1, 1, length, model), "tensor", 2, 0, tiled=True)
+
+        def scatter(part):
+            flat = part.reshape(-1, part.shape[2])
+            total = lax.psum_scatter(flat, ("tensor", "dp"), scatter_dimension=0, tiled=True)
+            return total.astype(F32)
 
         x, cot = to_sequence(tokens), to_sequence(cotangent)
         a_all, wi, wo = gather(shard_a), gather(w_inner), gather(shard_o)
         every = lax.all_gather(biases, "tensor", axis=0)
         *saved, first_sum = attend_plain(x, a_all, every, qaug, kaug, vaug, b_mixer[None])
-        bi = every[:, :, 2 * PAD :]
-        order = jnp.arange(groups)
-    out, d_tokens, *grads = after_attention(
-        first_sum, a_all, wi, wo, bi, vectors, x, cot, saved
-    )
-    g_attend, g_inner, g_outer, dbq, dbv, dbi, small = grads
-
-    def from_sequence(whole):
-        return lax.all_to_all(whole.reshape(1, 1, length, model), "tensor", 2, 0, tiled=True)
-
-    def by_place(part):
-        return jnp.take(part, order, axis=0) if near else part
-
-    def scatter(part):
-        flat = by_place(part).reshape(-1, part.shape[2])
-        return lax.psum_scatter(flat, ("tensor", "dp"), scatter_dimension=0, tiled=True)
-
-    ga = scatter(g_attend).astype(F32)
-    gi = scatter(g_inner).astype(F32)
-    go = scatter(g_outer).astype(F32)
-    rows = [by_place(dbq[:, 0, :width]), by_place(dbv[:, 0, :width]), by_place(dbi[:, 0]), small]
-    summed = lax.psum(jnp.concatenate([part.reshape(-1) for part in rows]), ("dp", "tensor"))
-    mine = lambda start, size: lax.dynamic_slice_in_dim(summed, start + place * size, size)
-    tail = summed[2 * model + dbi.size :].reshape(8, model)
+        out, d_first, d_mixed, g_inner, g_outer, dbi, small = dense_both(
+            first_sum, wi, wo, every[:, :, 2 * PAD :], vectors, cot
+        )
+        d_tokens, g_attend, dbq, dbv = attend_backward(x, a_all, d_mixed, d_first, *saved)
+        ga, gi, go = scatter(g_attend), scatter(g_inner), scatter(g_outer)
+        rows = [dbq[:, 0, :width], dbv[:, 0, :width], dbi[:, 0], small]
+        summed = lax.psum(jnp.concatenate([part.reshape(-1) for part in rows]), ("dp", "tensor"))
+        own = lambda start, size: lax.dynamic_slice_in_dim(summed, start + place * size, size)
+        dbq, dbv, dbi = own(0, width), own(model, width), own(2 * model, hidden)
+        tail = summed[-small.size :].reshape(small.shape)
+        out, d_tokens = from_sequence(out), from_sequence(d_tokens)
     return (
-        from_sequence(out),
-        from_sequence(d_tokens),
+        out,
+        d_tokens,
         ga[:, :width],
-        mine(0, width),
+        dbq,
         ga[:, width : 2 * width],
         ga[:, 2 * width : 3 * width],
-        mine(model, width),
+        dbv,
         ga[:, 3 * width :].T,
         tail[3],
         tail[4],
         tail[5],
         gi,
-        mine(2 * model, hidden),
+        dbi,
         go.T,
         tail[0],
         tail[1],

time: 643 us -> 348 us (0.54)
  waiting for transfers between devices: 209 us -> 0 us
  blocking collectives: 77.1 us -> 0 us
  Pallas kernels: 247 us -> 323 us
  local copies, waits for them, and re-layouts: 56.7 us -> 15.9 us
  other arithmetic: 30.7 us -> 7.78 us
  between operations: 14 us -> 0.73 us
  starting transfers between devices: 7.62 us -> 0 us
    reduce_scatter x2 -> x0, waiting for transfers between devices: 194 us -> none  [scatter(): lax.psum_scatter(flat, ('tensor', 'dp'), scatter_dimension=0, tiled=True)]
    psum x1 -> x0, blocking collectives: 77.1 us -> none  [body(): lax.psum(jnp.concatenate([part.reshape(-1) for part in rows]), ('dp', 'te...]
    pallas_call x1, Pallas kernels: 74.7 us -> 151 us  [attend_reduce(): pl.pallas_call(attend_reduce_kernel, grid=(4,), out_shape=[jax.ShapeDtype...]
    gather x6 -> x0, local copies, waits for them, and re-layouts: 17.8 us -> none  [by_place(): return jnp.take(part, order, axis=0) if near else part]
    unnamed x27 -> x13, local copies, waits for them, and re-layouts: 19.3 us -> 4.22 us
    all_to_all x2 -> x0, waiting for transfers between devices: 13.2 us -> none  [from_sequence(): lax.all_to_all(whole.reshape(1, 1, length, model), 'tensor', 2, 0, tiled=...]
    select_n x5 -> x0, other arithmetic: 11.4 us -> none  [by_place(): return jnp.take(part, order, axis=0) if near else part]
    reshape x5 -> x0, local copies, waits for them, and re-layouts: 10.8 us -> none  [the longest x2 10.7 us: from_sequence(): whole.reshape(1, 1, length, model)]
  transfers between devices with their start and end apart: 5 -> 0, of which waited for: 3 -> 0; matrix products, arithmetic and copies ran while one was open for 7% -> 0% of each run, Pallas kernels for 0% -> 0%
where the time goes in v3:
time: 348 us; the launch traced here: 347 us
  Pallas kernels  323 us (93%)
  local copies, waits for them, and re-layouts  15.9 us (5%)
  other arithmetic  7.78 us (2%)
    pallas_call x1, Pallas kernels, attend_reduce(): pl.pallas_call(attend_reduce_kernel, grid=(4,), out_shape=[jax.ShapeDtype...  151 us
    pallas_call x1, Pallas kernels, attend_forward(): pl.pallas_call(attend_kernel, grid=(groups,), out_shape=[jax.ShapeDtypeSt...  114 us
    pallas_call x1, Pallas kernels, dense_both(): pl.pallas_call(dense_kernel, grid=(2 * groups,), out_shape=[jax.ShapeDtyp...  58.2 us

profile of v3, /device:TPU:0, one launch (start us, length us, event | category | flops | bytes accessed | tf_op | source)
XLA Modules:
  0.0 347.4 jit_solution(4362104716387562689)
XLA Ops:
  0.7 0.0 copy-start
  0.7 0.6 fusion.1.vaug_ref
  1.3 1.3 broadcast_in_dim.49.bm_ref
  2.5 0.7 stack.21
  3.2 0.7 stack.22
  3.9 0.7 stack.23
  4.6 0.7 stack.24
  5.3 0.7 stack.25
  6.0 0.0 copy-done
  6.0 0.8 concatenate.7
  6.8 0.6 broadcast_in_dim.41.bias_ref
  7.4 0.6 stack.26.vec_ref
  8.1 0.9 copy.35
  8.9 1.6 pad_maximum_fusion.sa_ref
  10.6 1.1 select_convert_fusion.kaug_ref
  11.6 1.0 select_convert_fusion.1.qaug_ref
  12.7 113.8 %attend_forward.1 = (bf16[4,1024,256]{2,1,0:T(8,128)(2,1)}, bf16[4,1024,256]{2,1,0:T(8,128)(2,1)}, bf16[4,1024,256]{2,1,0:T(8,128)(2,1)}, bf16[4,1024,256]{2,1,0...) custom-call(bf16[4,256,768]{2,1,0:T(8,128)(2,1)} %bitcast.32, ...), custom_call_target="tpu_custom_call" | custom-call | tf_op jit(solution)/shard_map/attend_forward/pallas_call | solution.py:994
  126.5 58.2 %dense_both.1 = (bf16[1024,768]{1,0:T(8,128)(2,1)}, f32[1024,768]{1,0:T(8,128)}, bf16[1024,768]{1,0:T(8,128)(2,1)}, bf16[4,768,768]{2,1,0:T(8,128)(2,1)}, bf16[4...) custom-call(f32[1024,768]{1,0:T(8,128)} %get-tuple-element.45.first_in, ...), custom_call_target="tpu_custom_call" | custom-call | tf_op jit(solution)/shard_map/dense_both/pallas_call | solution.py:1063
  184.7 151.1 %attend_reduce.1 = (bf16[4,256,768]{2,1,0:T(8,128)(2,1)}, bf16[4,256,768]{2,1,0:T(8,128)(2,1)}, f32[96,384]{1,0:T(8,128)}, f32[96,384]{1,0:T(8,128)}, f32[96,768...) custom-call(bf16[4,256,768]{2,1,0:T(8,128)(2,1)} %get-tuple-element.43.x_ref, ...), custom_call_target="tpu_custom_call" | custom-call | tf_op jit(solution)/shard_map/attend_reduce/pallas_call | solution.py:1155
  335.8 1.4 constant_dynamic-slice_fusion
  337.1 1.8 slice_reduce_fusion
  338.9 1.8 slice_bitcast_fusion
  340.7 0.7 copy.38
  341.4 0.0 copy-start.1
  341.4 3.5 bitcast_convert_fusion
  344.9 0.0 copy-done.1
  344.9 0.0 copy-start.3
  344.9 1.1 copy.42
  346.0 0.0 copy-done.3
  346.0 0.7 copy.43
  346.7 0.0 copy-done.2
  346.7 0.7 copy.44
  (6 shorter events, 0.0 us)
Async XLA Ops:
  0.7 5.3 %copy-start = (s32[4,1,1024]{2,1,0:T(1,128)S(1)}, s32[4,1,1024]{2,1,0:T(1,128)}, u32[]{:S(2)}) copy-start(s32[4,1,1024]{2,1,0:T(1,128)} %param.19) | copy-start | bytes 49156
  341.4 3.5 copy-start.1
  344.9 1.1 copy-start.3
  344.9 1.9 copy-start.2

commit v4 on v3

--- a/solution.py
+++ b/solution.py
@@ -61,32 +61,32 @@
 
 def project(x_rows, rows, bq, bv, w_s, qaug_ref, kaug_ref, vaug_ref, q_ref, k_ref, v_ref):
     queries = (dot_nn(x_rows, w_s[0]) + bq).astype(BF16)
-    q_ref[0, rows, :] = queries * jnp.asarray(HEAD**-0.5, BF16) + qaug_ref[rows, :]
+    q_ref[rows, :] = queries * jnp.asarray(HEAD**-0.5, BF16) + qaug_ref[rows, :]
     keys = dot_nn(x_rows, w_s[1]).astype(BF16)
-    k_ref[0, rows, :] = keys + kaug_ref[rows, :]
+    k_ref[rows, :] = keys + kaug_ref[rows, :]
     values = (dot_nn(x_rows, w_s[2]) + bv).astype(BF16)
-    v_ref[0, rows, :] = values + vaug_ref[...]
+    v_ref[rows, :] = values + vaug_ref[...]
 
 
 def attend_rows(rows, width, w_s, q_ref, k_ref, v_ref, att_ref, first_ref):
     lanes = lane_index((ROWS, PAD))
-    queries = q_ref[0, rows, :]
+    queries = q_ref[rows, :]
     attended = jnp.zeros((ROWS, PAD), F32)
     extended = queries
     for head in range(width // HEAD):
         masked = jnp.where(head_and_extra(lanes, head, width), queries, 0)
-        scores = dot_nt(masked, k_ref[0])
+        scores = dot_nt(masked, k_ref[...])
         highest = jnp.max(scores, axis=1, keepdims=True)
         raw = jnp.exp2((scores - highest) * LOG2E).astype(BF16)
-        mixed = dot_nn(raw, v_ref[0])
+        mixed = dot_nn(raw, v_ref[...])
         total = mixed[:, width : width + 1]
         attended = jnp.where(head_only(lanes, head), mixed / total, attended)
         for spot, part in enumerate(three_parts(-(highest + jnp.log(total)))):
             here = lanes == width + DOCS + 3 * head + spot
             extended = jnp.where(here, jnp.broadcast_to(part, (ROWS, PAD)), extended)
-    q_ref[0, rows, :] = extended
+    q_ref[rows, :] = extended
     attended = attended.astype(BF16)
-    att_ref[0, rows, :] = attended
+    att_ref[rows, :] = attended
     first_ref[rows, :] += dot_nt(attended, w_s[3])
 
 
@@ -109,12 +109,13 @@
         rows = rows_of(index)
         project(
             x_ref[rows, :], rows, biases[:, :PAD], biases[:, PAD : 2 * PAD], w_s, qaug_ref,
-            kaug_ref, vaug_ref, q_ref, k_ref, v_ref,
+            kaug_ref, vaug_ref, q_ref.at[0], k_ref.at[0], v_ref.at[0],
         )
 
     @pl.loop(0, length // ROWS)
     def _(index):
-        attend_rows(rows_of(index), width, w_s, q_ref, k_ref, v_ref, att_ref, first_ref)
+        refs = (ref.at[0] for ref in (q_ref, k_ref, v_ref, att_ref))
+        attend_rows(rows_of(index), width, w_s, *refs, first_ref)
 
 
 MESH = pl.DeviceIdType.MESH
@@ -234,10 +235,36 @@
         )
 
 
-def attend_kernel(
+def gelu_parts(values):
+    phi = jnp.exp2(values * values * (-0.5 * LOG2E)) * 0.3989422804014327
+    total = 0.5 + 0.5 * lax.erf(values * 0.7071067811865476)
+    return values * total, total + values * phi
+
+
+def norm_parts(values):
+    average = jnp.mean(values, axis=-1, keepdims=True)
+    centred = values - average
+    spread = jnp.mean(centred * centred, axis=-1, keepdims=True)
+    inverse = lax.rsqrt(spread + EPS)
+    return centred * inverse, inverse
+
+
+def norm_back(grads, gain, unit, inverse):
+    scaled = grads * gain
+    average = jnp.mean(scaled, axis=-1, keepdims=True)
+    along = jnp.mean(scaled * unit, axis=-1, keepdims=True)
+    return (scaled - average - unit * along) * inverse
+
+
+def column_sum(values):
+    return jnp.sum(values, axis=0, keepdims=True)
+
+
+def forward_kernel(
     tok_ref, cot_ref, sa_ref, si_ref, so_ref, bias_ref, qaug_ref, kaug_ref, vaug_ref, bm_ref,
-    q_ref, k_ref, v_ref, att_ref, first_ref, bi_ref, x_out, cot_out, a_out, wi_out, wo_out,
-    w_s, x_s, a_s, bias_s, send_sem, recv_sem, here_sem,
+    vec_ref,
+    acts_ref, att_ref, slope_ref, first_out, second_out, low_out, x_out, cot_out, wia_out, wo_out,
+    w_s, x_s, a_s, i_s, o_s, bias_s, first_s, second_s, low_s, send_sem, recv_sem, here_sem,
 ):
     step = pl.program_id(0)
     place = lax.axis_index("tensor")
@@ -249,8 +276,10 @@
     share = sa_ref.shape[0]
     wires = Wires(send_sem, recv_sem, place, row)
     attn = ShardGather(wires, KIND_A, sa_ref, a_s)
-    inner = ShardGather(wires, KIND_I, si_ref, wi_out)
-    outer = BlockGather(wires, KIND_O, so_ref, wo_out)
+    inner = ShardGather(wires, KIND_I, si_ref, i_s)
+    outer = BlockGather(wires, KIND_O, so_ref, o_s)
+    gain_one, bias_one, b_outer = (vec_ref[i : i + 1, :] for i in range(3))
+    q_ref, k_ref, v_ref = (acts_ref.at[0, :, i * PAD : (i + 1) * PAD] for i in range(3))
 
     def exchange(base, source, target, bits, mine):
         other = partner(place, bits, 4)
@@ -264,13 +293,18 @@
     local = [
         pltpu.make_async_copy(tok_ref.at[place], x_s.at[place], here_sem.at[0]),
         pltpu.make_async_copy(sa_ref, a_s.at[0, row], here_sem.at[1]),
-        pltpu.make_async_copy(si_ref, wi_out.at[0, row], here_sem.at[2]),
-        pltpu.make_async_copy(so_ref, wo_out.at[0, row], here_sem.at[3]),
-        pltpu.make_async_copy(cot_ref.at[place], cot_out.at[place], here_sem.at[4]),
-        pltpu.make_async_copy(bias_ref, bias_s.at[0], here_sem.at[5]),
+        pltpu.make_async_copy(si_ref, i_s.at[0, row], here_sem.at[2]),
+        pltpu.make_async_copy(so_ref, o_s.at[0, row], here_sem.at[3]),
+        pltpu.make_async_copy(bias_ref, bias_s.at[0], here_sem.at[4]),
     ]
+    own_cot = pltpu.make_async_copy(cot_ref.at[place], cot_out.at[place], here_sem.at[5])
     keep_x = pltpu.make_async_copy(x_s, x_out, here_sem.at[6])
-    keep_a = pltpu.make_async_copy(a_s, a_out, here_sem.at[7])
+    keep_a = pltpu.make_async_copy(a_s, wia_out.at[1], here_sem.at[7])
+    keep_i = pltpu.make_async_copy(i_s, wia_out.at[0], here_sem.at[8])
+    keep_o = pltpu.make_async_copy(o_s, wo_out, here_sem.at[9])
+    keep_first = pltpu.make_async_copy(first_s, first_out, here_sem.at[10])
+    keep_low = pltpu.make_async_copy(low_s, low_out, here_sem.at[11])
+    keep_second = pltpu.make_async_copy(second_s, second_out, here_sem.at[12])
 
     @pl.when(step == 0)
     def _():
@@ -284,6 +318,7 @@
             exchange(TOKENS, tok_ref, x_s, bits, True).start()
         for copy in local:
             copy.start()
+        own_cot.start()
         for copy in local:
             copy.wait()
         attn.cross_x().wait_recv()
@@ -293,6 +328,7 @@
         attn.pass_y(0)
         attn.wait_y(0)
         attn.to_core(0, True).start()
+        inner.cross_x().start()
         for bits in (1, 2, 3):
             exchange(TOKENS, tok_ref, x_s, bits, False).wait_recv()
             bias_copy(bits, False).wait_recv()
@@ -301,7 +337,7 @@
         @pl.loop(0, quarters)
         def _(index):
             rows = rows_of(index, part)
-            first_ref[rows, :] = x_s[index].astype(F32) + bm_ref[...]
+            first_s[rows, :] = x_s[index].astype(F32) + bm_ref[...]
 
     @pl.when(step == 1)
     def _():
@@ -317,81 +353,135 @@
         attn.to_core(2, False).wait_recv()
         keep_a.start()
 
-    for dp_row in range(a_s.shape[1]):
-        packed = a_s[step, dp_row]
-        rest = jnp.zeros((share, PAD - width), packed.dtype)
-        for slot in range(4):
-            piece = packed[:, slot * width : (slot + 1) * width]
-            rows = slice(dp_row * share, (dp_row + 1) * share)
-            w_s[slot, rows, :] = jnp.concatenate([piece, rest], axis=1)
-    biases = bias_s[step]
-    bi_ref[0] = biases[:, 2 * PAD :]
-
-    @pl.loop(0, quarters)
-    def _(index):
-        rows = rows_of(index, part)
-        x_rows = x_s[index]
-        project(
-            x_rows, rows, biases[:, :PAD], biases[:, PAD : 2 * PAD], w_s, qaug_ref, kaug_ref,
-            vaug_ref, q_ref, k_ref, v_ref,
-        )
-
-    @pl.loop(0, blocks)
-    def _(index):
-        attend_rows(rows_of(index), width, w_s, q_ref, k_ref, v_ref, att_ref, first_ref)
-
-        @pl.when((step == 0) & (index == 1))
-        def _():
-            attn.wait_z(2)
-            attn.pass_y(2)
-            outer.start_z(0)
-            outer.along_y(0, 0, True).start()
-            inner.cross_x().start()
-            for bits in (2, 3, 1):
-                exchange(COTS, cot_ref, cot_out, bits, True).start()
-
-        @pl.when((step == 0) & (index == 3))
-        def _():
-            inner.cross_x().wait_recv()
-            inner.start_z(0)
-            inner.along_y(0, 0, True).start()
-            inner.start_z(2)
-            inner.along_y(2, 0, True).start()
-
-        @pl.when((step == 1) & (index == 2))
-        def _():
-            outer.wait_z(0)
-            outer.pass_y(0)
-
-        @pl.when((step == 2) & (index == 1))
-        def _():
-            outer.wait_y(0)
-            outer.cross_x().start()
-            outer.to_core(0, True).start()
-
-        @pl.when((step == 3) & (index == 0))
-        def _():
-            inner.wait_z(0)
-            inner.pass_y(0)
-
-        @pl.when((step == 3) & (index == 2))
-        def _():
-            inner.wait_z(2)
-            inner.pass_y(2)
-
-    @pl.when(step == 3)
-    def _():
-        inner.wait_y(0)
-        inner.to_core(0, True).start()
+    @pl.when(step < 4)
+    def _():
+        for dp_row in range(a_s.shape[1]):
+            packed = a_s[step, dp_row]
+            rest = jnp.zeros((share, PAD - width), packed.dtype)
+            for slot in range(4):
+                piece = packed[:, slot * width : (slot + 1) * width]
+                rows = slice(dp_row * share, (dp_row + 1) * share)
+                w_s[slot, rows, :] = jnp.concatenate([piece, rest], axis=1)
+        biases = bias_s[step]
+
+        @pl.loop(0, quarters)
+        def _(index):
+            rows = rows_of(index, part)
+            x_rows = x_s[index]
+            project(
+                x_rows, rows, biases[:, :PAD], biases[:, PAD : 2 * PAD], w_s, qaug_ref, kaug_ref,
+                vaug_ref, q_ref, k_ref, v_ref,
+            )
+
+        @pl.loop(0, blocks)
+        def _(index):
+            attend_rows(
+                rows_of(index), width, w_s, q_ref, k_ref, v_ref, att_ref.at[0], first_s
+            )
+
+            @pl.when((step == 0) & (index == 0))
+            def _():
+                outer.start_z(0)
+                outer.along_y(0, 0, True).start()
+                for bits in (2, 3, 1):
+                    exchange(COTS, cot_ref, cot_out, bits, True).start()
+
+            @pl.when((step == 0) & (index == 1))
+            def _():
+                attn.wait_z(2)
+                attn.pass_y(2)
+
+            @pl.when((step == 0) & (index == 3))
+            def _():
+                inner.start_z(0)
+                inner.along_y(0, 0, True).start()
+
+            @pl.when((step == 1) & (index == 1))
+            def _():
+                outer.wait_z(0)
+                outer.pass_y(0)
+
+            @pl.when((step == 1) & (index == 2))
+            def _():
+                inner.cross_x().wait_recv()
+                inner.start_z(2)
+                inner.along_y(2, 0, True).start()
+
+            @pl.when((step == 2) & (index == 2))
+            def _():
+                inner.wait_z(0)
+                inner.pass_y(0)
+
+            @pl.when((step == 2) & (index == 3))
+            def _():
+                outer.wait_y(0)
+                outer.cross_x().start()
+                outer.to_core(0, True).start()
+
+            @pl.when((step == 3) & (index == 1))
+            def _():
+                inner.wait_y(0)
+                inner.to_core(0, True).start()
+
+            @pl.when((step == 3) & (index == 3))
+            def _():
+                inner.wait_z(2)
+                inner.pass_y(2)
+
+    @pl.when(step == 4)
+    def _():
+        keep_first.start()
+
+        @pl.loop(0, blocks)
+        def _(index):
+            rows = rows_of(index)
+            unit, _inverse = norm_parts(first_s[rows, :])
+            normed = unit * gain_one + bias_one
+            low_s[rows, :] = normed.astype(BF16)
+            second_s[rows, :] = normed + b_outer
+
+        keep_low.start()
+
+    @pl.when(step == 5)
+    def _():
+        inner.to_core(0, False).wait_recv()
+        outer.to_core(0, False).wait_recv()
+
+    @pl.when(step == 6)
+    def _():
         inner.wait_y(2)
         inner.to_core(2, True).start()
         outer.cross_x().wait_recv()
         outer.to_core(2, True).start()
+
+    @pl.when(step == 7)
+    def _():
+        inner.to_core(2, False).wait_recv()
+        outer.to_core(2, False).wait_recv()
+        keep_i.start()
+        keep_o.start()
+
+    @pl.when(step >= 4)
+    def _():
+        slot = step - 4
+        w_inner = i_s[slot].reshape(model, model)
+        w_outer = o_s[slot].reshape(model, model)
+        b_inner = bias_s[slot][:, 2 * PAD :]
+
+        @pl.loop(0, blocks)
+        def _(index):
+            rows = rows_of(index)
+            value, slope = gelu_parts(dot_nn(low_s[rows, :], w_inner) + b_inner)
+            hidden = value.astype(BF16)
+            acts_ref[0, rows, :] = hidden
+            slope_ref[0, rows, :] = slope.astype(BF16)
+            second_s[rows, :] += dot_nt(hidden, w_outer)
+
+    @pl.when(step == 7)
+    def _():
+        keep_second.start()
         for bits in (1, 2, 3):
             exchange(COTS, cot_ref, cot_out, bits, False).wait_recv()
-        for gather in (inner, outer):
-            for slot in (0, 2):
-                gather.to_core(slot, False).wait_recv()
         for gather in (attn, inner, outer):
             gather.cross_x().wait_send()
             gather.wait_sent(gather is not outer)
@@ -399,33 +489,10 @@
             exchange(TOKENS, tok_ref, x_s, bits, True).wait_send()
             exchange(COTS, cot_ref, cot_out, bits, True).wait_send()
             bias_copy(bits, True).wait_send()
-        keep_x.wait()
-        keep_a.wait()
-
-
-def gelu_parts(values):
-    phi = jnp.exp2(values * values * (-0.5 * LOG2E)) * 0.3989422804014327
-    total = 0.5 + 0.5 * lax.erf(values * 0.7071067811865476)
-    return values * total, total + values * phi
-
-
-def norm_parts(values):
-    average = jnp.mean(values, axis=-1, keepdims=True)
-    centred = values - average
-    spread = jnp.mean(centred * centred, axis=-1, keepdims=True)
-    inverse = lax.rsqrt(spread + EPS)
-    return centred * inverse, inverse
-
-
-def norm_back(grads, gain, unit, inverse):
-    scaled = grads * gain
-    average = jnp.mean(scaled, axis=-1, keepdims=True)
-    along = jnp.mean(scaled * unit, axis=-1, keepdims=True)
-    return (scaled - average - unit * along) * inverse
-
-
-def column_sum(values):
-    return jnp.sum(values, axis=0, keepdims=True)
+        for copy in (
+            own_cot, keep_x, keep_a, keep_i, keep_o, keep_first, keep_low, keep_second,
+        ):
+            copy.wait()
 
 
 def dense_kernel(
@@ -522,9 +589,9 @@
 
 def back_rows(rows, width, w_s, dmix_rows, q_ref, k_ref, v_ref, att_ref, kt_s, dq_s, dk_s, dv_s):
     lanes = lane_index((ROWS, PAD))
-    queries = q_ref[0, rows, :]
+    queries = q_ref[rows, :]
     d_att = dot_nn(dmix_rows, w_s[3]).astype(BF16)
-    product = d_att.astype(F32) * att_ref[0, rows, :].astype(F32)
+    product = d_att.astype(F32) * att_ref[rows, :].astype(F32)
     heads = range(width // HEAD)
     extended = d_att
     for head in heads:
@@ -539,8 +606,8 @@
     for head in heads:
         wide = head_and_extra(lanes, head, width)
         only = head_only(lanes, head)
-        chances = jnp.exp2(dot_nt(k_ref[0], jnp.where(wide, queries, 0)) * LOG2E)
-        d_chances = dot_nt(v_ref[0], jnp.where(wide, extended, 0))
+        chances = jnp.exp2(dot_nt(k_ref[...], jnp.where(wide, queries, 0)) * LOG2E)
+        d_chances = dot_nt(v_ref[...], jnp.where(wide, extended, 0))
         d_scores = (chances * d_chances).astype(BF16)
         chances_all.append(chances.astype(BF16))
         d_scores_all.append(d_scores)
@@ -556,23 +623,23 @@
     d_query = (dq_s[:, rows].T * HEAD**-0.5).astype(BF16)
     d_query = jnp.where(lane_index(d_query.shape) < width, d_query, 0)
     d_value = dv_s[rows, :].astype(BF16)
-    low_s[0, rows, :] = d_query
-    low_s[1, rows, :] = dk_s[rows, :].astype(BF16)
-    low_s[2, rows, :] = d_value
+    low_s[rows, :PAD] = d_query
+    low_s[rows, PAD : 2 * PAD] = dk_s[rows, :].astype(BF16)
+    low_s[rows, 2 * PAD :] = d_value
     return column_sum(d_query.astype(F32)), column_sum(d_value.astype(F32))
 
 
 def back_tokens(rows, w_s, low_s):
-    return sum(dot_nt(low_s[slot, rows, :], w_s[slot]) for slot in range(3))
+    return sum(dot_nt(low_s[rows, slot * PAD : (slot + 1) * PAD], w_s[slot]) for slot in range(3))
 
 
 def back_weights(rows, width, slots, xt_s, dmixt_s, low_s, att_ref):
     parts = []
     for slot in slots:
         if slot < 3:
-            part = dot_nn(xt_s[rows, :], low_s[slot])
+            part = dot_nn(xt_s[rows, :], low_s[:, slot * PAD : (slot + 1) * PAD])
         else:
-            part = dot_nn(dmixt_s[rows, :], att_ref[0])
+            part = dot_nn(dmixt_s[rows, :], att_ref[...])
         parts.append(part[:, :width])
     return jnp.concatenate(parts, axis=1).astype(BF16)
 
@@ -610,9 +677,8 @@
     def _(index):
         rows = rows_of(index)
         dmix_rows = dmix_ref[rows, :]
-        back_rows(
-            rows, width, w_s, dmix_rows, q_ref, k_ref, v_ref, att_ref, kt_s, dq_s, dk_s, dv_s
-        )
+        refs = (ref.at[0] for ref in (q_ref, k_ref, v_ref, att_ref))
+        back_rows(rows, width, w_s, dmix_rows, *refs, kt_s, dq_s, dk_s, dv_s)
 
     @pl.loop(0, blocks)
     def _(index):
@@ -625,7 +691,9 @@
     @pl.loop(0, model // ROWS)
     def _(index):
         rows = rows_of(index)
-        ga_ref[0, rows, :] = back_weights(rows, width, range(4), xt_s, dmixt_s, low_s, att_ref)
+        ga_ref[0, rows, :] = back_weights(
+            rows, width, range(4), xt_s, dmixt_s, low_s, att_ref.at[0]
+        )
 
 
 def add_into(target, source):
@@ -635,52 +703,68 @@
 class Reduce:
     COUNT = 11
 
-    def __init__(self, wires, base, held, core, by_y, by_z, by_x):
+    def __init__(self, wires, base, held, core, by_y, by_z, by_x, cols=slice(None)):
         self.wires, self.base, self.held, self.core = wires, base, held, core
         self.by_y, self.by_z, self.by_x = by_y, by_z, by_x
+        self.cols = cols
         self.z, self.y = lax.div(wires.row, 2), lax.rem(wires.row, 2)
 
+    def part(self, ref, *index):
+        return ref.at[index + (slice(None), self.cols)]
+
     def core_copy(self, j, source):
-        return self.wires.copy(self.base + j, source, self.core.at[j], 1, 0)
+        everything = (slice(None), slice(None))
+        return self.wires.copy(
+            self.base + j, self.part(source, *everything), self.part(self.core, j, *everything), 1, 0
+        )
 
     def add_core(self, j):
         self.core_copy(j, self.held.at[j]).wait_recv()
         for z in range(4):
             for y in range(2):
-                add_into(self.held.at[j, z, y], self.core.at[j, z, y])
+                add_into(self.part(self.held, j, z, y), self.part(self.core, j, z, y))
 
     def y_copy(self, j):
-        source = self.held.at[j, :, 1 - self.y]
-        return self.wires.copy(self.base + 2 + j, source, self.by_y.at[j], 0, 1)
+        source = self.part(self.held, j, slice(None), 1 - self.y)
+        return self.wires.copy(
+            self.base + 2 + j, source, self.part(self.by_y, j, slice(None)), 0, 1
+        )
 
     def add_y(self, j):
         self.y_copy(j).wait_recv()
         for z in range(4):
-            add_into(self.held.at[j, z, self.y], self.by_y.at[j, z])
+            add_into(self.part(self.held, j, z, self.y), self.part(self.by_y, j, z))
 
     def z_copy(self, j, step):
-        source = self.held.at[j, lax.div(partner(self.wires.row, 2 * step, 8), 2), self.y]
+        other = lax.div(partner(self.wires.row, 2 * step, 8), 2)
         number = self.base + 4 + 3 * j + step - 1
-        return self.wires.copy(number, source, self.by_z.at[j, step - 1], 0, 2 * step)
+        return self.wires.copy(
+            number, self.part(self.held, j, other, self.y), self.part(self.by_z, j, step - 1),
+            0, 2 * step,
+        )
 
     def start_z(self, j):
         for step in (1, 2, 3):
             self.z_copy(j, step).start()
 
     def total_z(self, j):
-        total = self.held[j, self.z, self.y].astype(F32)
+        total = self.part(self.held, j, self.z, self.y)[...].astype(F32)
         for step in (1, 2, 3):
             self.z_copy(j, step).wait_recv()
-            total = total + self.by_z[j, step - 1].astype(F32)
+            total = total + self.part(self.by_z, j, step - 1)[...].astype(F32)
         return total
 
     def x_copy(self):
-        source = self.held.at[1, self.z, self.y]
-        return self.wires.copy(self.base + 10, source, self.by_x, 2, 0)
+        source = self.part(self.held, 1, self.z, self.y)
+        return self.wires.copy(self.base + 10, source, self.part(self.by_x), 2, 0)
 
     def send_x(self):
-        self.held[1, self.z, self.y] = self.total_z(1).astype(BF16)
+        self.part(self.held, 1, self.z, self.y)[...] = self.total_z(1).astype(BF16)
         self.x_copy().start()
+
+    def total(self):
+        self.x_copy().wait_recv()
+        return self.total_z(0) + self.part(self.by_x)[...].astype(F32)
 
     def whole_x_copy(self):
         return self.wires.copy(self.base + 10, self.held.at[1], self.by_x, 2, 0)
@@ -710,33 +794,35 @@
     return jnp.where(step < 2, 3 - 2 * step, 6 - 2 * step)
 
 
-def attend_reduce_kernel(
-    x_ref, a_ref, dmix_ref, dfirst_ref, q_ref, k_ref, v_ref, att_ref, gi_ref, go_ref, out_ref,
-    dbi_ref, small_ref,
-    out_res, dtok_res, ga_one, ga_two, gi_res, go_res, sum_res, late_res,
-    w_s, xt_s, dmixt_s, kt_s, dq_s, dk_s, dv_s, low_s, dmix_s, dtok_s, dlow_s, sums_s, late_s,
-    sums_r, late_r,
-    held_i, core_i, y_i, z_i, x_i, held_o, core_o, y_o, z_o, x_o,
-    send_a, held_a, core_a, y_a, z_a, x_a,
+def backward_kernel(
+    acts_ref, att_ref, slope_ref, wia_ref, wo_ref, vec_ref, second_ref, first_ref, low_ref, x_ref,
+    cot_ref,
+    out_res, dtok_res, ga_res, gi_res, go_res, sum_res, late_res,
+    low_t, back_t, dmix_s, low_s, flow_s, out_s, grad_s, first_s, w_s, kt_s, dq_s, dk_s, dv_s,
+    sums_s, late_s, sums_r, late_r,
+    send_i, held_i, core_i, y_i, z_i, x_i, send_o, held_o, core_o, y_o, z_o, x_o,
+    held_a, core_a, y_a, z_a, x_a,
     send_sem, recv_sem, here_sem,
 ):
     step = pl.program_id(0)
     place = lax.axis_index("tensor")
     row = lax.axis_index("dp")
     length, model = dmix_s.shape
-    quarters, part, _ = dlow_s.shape
-    width = a_ref.shape[2] // 4
+    quarters, part, _ = flow_s.shape
+    width = wia_ref.shape[2] // 4
     blocks = length // ROWS
+    share = held_i.shape[3]
     wires = Wires(send_sem, recv_sem, place, row)
     inner = Reduce(wires, RED_I, held_i, core_i, y_i, z_i, x_i)
     outer = Reduce(wires, RED_O, held_o, core_o, y_o, z_o, x_o)
+    halves = (slice(0, model // 2), slice(model // 2, model))
+    send_a = send_i
     attn = [
-        Reduce(
-            wires, RED_A + half * Reduce.COUNT, held_a.at[half], core_a.at[half], y_a.at[half],
-            z_a.at[half], x_a.at[half],
-        )
-        for half in range(2)
+        Reduce(wires, RED_A + half * Reduce.COUNT, held_a, core_a, y_a, z_a, x_a, cols)
+        for half, cols in enumerate(halves)
     ]
+    gain_one, gain_two, bias_two = (vec_ref[i : i + 1, :] for i in (0, 3, 4))
+    q_ref, k_ref, v_ref = (acts_ref.at[0, :, i * PAD : (i + 1) * PAD] for i in range(3))
 
     def exchange(base, source, target, bits, mine):
         other = partner(place, bits, 4)
@@ -748,205 +834,283 @@
         bits = HOPS[number]
         return wires.copy(base + number, kept.at[number], got.at[number], *bits)
 
-    def add_hop(base, kept, got, number):
+    def next_hop(base, kept, got, number):
         hop(base, kept, got, number).wait_recv()
         kept[number + 1] = kept[number] + got[number]
-
-    def next_hop(base, kept, got, number):
-        add_hop(base, kept, got, number)
         if number + 1 < len(HOPS):
             hop(base, kept, got, number + 1).start()
 
-    loads = [
-        pltpu.make_async_copy(gi_ref.at[0], held_i.at[0], here_sem.at[0]),
-        pltpu.make_async_copy(gi_ref.at[2], held_i.at[1], here_sem.at[1]),
-        pltpu.make_async_copy(go_ref.at[0], held_o.at[0], here_sem.at[2]),
-        pltpu.make_async_copy(go_ref.at[2], held_o.at[1], here_sem.at[3]),
-        pltpu.make_async_copy(dmix_ref, dmix_s, here_sem.at[4]),
-        pltpu.make_async_copy(dfirst_ref, dtok_s, here_sem.at[5]),
-    ]
-    keep_out = pltpu.make_async_copy(out_ref.at[place], out_res.at[place], here_sem.at[6])
-    keep_dtok = pltpu.make_async_copy(dlow_s.at[place], dtok_res.at[place], here_sem.at[7])
-    load_x = pltpu.make_async_copy(x_ref, dlow_s, here_sem.at[8])
-
-    def core_sends(kind, source):
-        return [kind.core_copy(0, source.at[1]), kind.core_copy(1, source.at[3])]
+    load_second = pltpu.make_async_copy(second_ref, grad_s, here_sem.at[0])
+    load_cot = pltpu.make_async_copy(cot_ref, flow_s, here_sem.at[1])
+    load_low = pltpu.make_async_copy(low_ref, low_s, here_sem.at[2])
+    load_x = pltpu.make_async_copy(x_ref, flow_s, here_sem.at[3])
+    keep_out = pltpu.make_async_copy(out_s.at[place], out_res.at[place], here_sem.at[4])
+    keep_dtok = pltpu.make_async_copy(flow_s.at[place], dtok_res.at[place], here_sem.at[5])
+
+    def load_first(index):
+        return pltpu.make_async_copy(
+            first_ref.at[rows_of(index)], first_s.at[index % 2], here_sem.at[6 + index % 2]
+        )
+
+    order = (3, 1, 2, 0)
 
     @pl.when(step == 0)
     def _():
-        for copy in loads:
-            copy.start()
-        load_x.start()
+        load_second.start()
+        load_cot.start()
+        load_low.start()
         sums_s[0] = jnp.zeros_like(sums_s[0])
         late_s[0] = jnp.zeros_like(late_s[0])
-        for bits in range(4):
-            sums_s[0, pl.ds(partner(place, bits, 4), 1), :] = dbi_ref[bits]
-        sums_s[0, 8:16, :] = small_ref[...]
         greet(wires, PEERS)
-        for copy in core_sends(inner, gi_ref) + core_sends(outer, go_ref):
-            copy.start()
-        hop(SUMS, sums_s, sums_r, 0).start()
-        for copy in loads:
-            copy.wait()
-        load_x.wait()
+        load_second.wait()
+        load_cot.wait()
+        load_low.wait()
 
         @pl.loop(0, quarters)
         def _(index):
             rows = rows_of(index, part)
-            xt_s[:, rows] = dlow_s[index].T
-            dmixt_s[:, rows] = dmix_s[rows, :].T
-
-        for j in (1, 0):
-            inner.add_core(j)
-            inner.y_copy(j).start()
+            low_t[:, rows] = low_s[rows, :].T
+            unit, inverse = norm_parts(grad_s[rows, :])
+            out_s[index] = (unit * gain_two + bias_two).astype(BF16)
+            grads = flow_s[index].astype(F32)
+            d_second = norm_back(grads, gain_two, unit, inverse)
+            sums_s[0, 8:9, :] += column_sum(d_second)
+            sums_s[0, 9:10, :] += column_sum(grads * unit)
+            sums_s[0, 10:11, :] += column_sum(grads)
+            grad_s[rows, :] = d_second
+            lower = d_second.astype(BF16)
+            dmix_s[rows, :] = lower
+            back_t[:, rows] = lower.T
+
+        for bits in (2, 3, 1):
+            exchange(OUTPUTS, out_s, out_res, bits, True).start()
+        keep_out.start()
+        load_x.start()
+
+    @pl.when(step < 4)
+    def _():
+        @pl.loop(0, blocks)
+        def _(index):
+            rows = rows_of(index)
+            d_hidden = dot_nn(dmix_s[rows, :], wo_ref[0])
+            d_inner = (d_hidden * slope_ref[0, rows, :].astype(F32)).astype(BF16)
+            low_s[rows, :] = d_inner
+            for_inner = column_sum(d_inner.astype(F32))
+            for number, bits in enumerate(order):
+
+                @pl.when(step == number)
+                def _(bits=bits):
+                    sums_s[0, pl.ds(partner(place, bits, 4), 1), :] += for_inner
+
+            grad_s[rows, :] += dot_nt(d_inner, wia_ref[0])
+
+        @pl.loop(0, model // (2 * share))
+        def _(z):
+            rows = pl.ds(pl.multiple_of(z * 2 * share, 2 * share), 2 * share)
+            for transposed, right, sent, held in (
+                (back_t, acts_ref.at[0], send_o, held_o), (low_t, low_s, send_i, held_i),
+            ):
+                grads = dot_nn(transposed[rows, :], right[...]).astype(BF16)
+                for y in range(2):
+                    piece = grads[y * share : (y + 1) * share]
+
+                    @pl.when(step < 2)
+                    def _(y=y, piece=piece, sent=sent):
+                        sent[step, z, y] = piece
+
+                    @pl.when(step >= 2)
+                    def _(y=y, piece=piece, held=held):
+                        held[3 - step, z, y] = piece
+
+    for number, j in ((0, 1), (1, 0)):
+
+        @pl.when(step == number)
+        def _(number=number, j=j):
+            outer.core_copy(j, send_o.at[number]).start()
+            inner.core_copy(j, send_i.at[number]).start()
+
+    @pl.when(step == 2)
+    def _():
+        load_first(0).start()
+        load_first(1).start()
         outer.add_core(1)
         outer.whole_x_copy().start()
+        inner.add_core(1)
+        inner.y_copy(1).start()
+
+    @pl.when(step == 3)
+    def _():
+        inner.add_core(0)
+        inner.y_copy(0).start()
         outer.add_core(0)
-        next_hop(SUMS, sums_s, sums_r, 0)
-
-    @pl.when(step == 3)
+        load_x.wait()
+        for index in range(blocks):
+            rows = slice(index * ROWS, (index + 1) * ROWS)
+            load_first(index).wait()
+            unit, inverse = norm_parts(first_s[index % 2])
+            if index + 2 < blocks:
+                load_first(index + 2).start()
+            grads = grad_s[rows, :]
+            d_first = norm_back(grads, gain_one, unit, inverse)
+            sums_s[0, 11:12, :] += column_sum(d_first)
+            sums_s[0, 12:13, :] += column_sum(grads * unit)
+            sums_s[0, 13:14, :] += column_sum(grads)
+            grad_s[rows, :] = d_first
+            lower = d_first.astype(BF16)
+            dmix_s[rows, :] = lower
+            back_t[:, rows] = lower.T
+            low_t[:, rows] = flow_s[index].T
+        hop(SUMS, sums_s, sums_r, 0).start()
+
+    @pl.when(step == 4)
+    def _():
+        for number, j in ((0, 1), (1, 0)):
+            inner.core_copy(j, send_i.at[number]).wait_send()
+
+    @pl.when(step == 7)
     def _():
         for reduce in attn:
             reduce.add_core(1)
             reduce.y_copy(1).start()
 
-    for slot in range(4):
-        w_s[slot] = unpack(a_ref.at[0], slot, width)
-    for sums in (dk_s, dv_s):
-        sums[...] = jnp.zeros_like(sums)
-
-    @pl.loop(0, blocks)
-    def _(index):
-        rows = rows_of(index)
-        kt_s[:, rows] = k_ref[0, rows, :].T
-
-    @pl.loop(0, blocks)
-    def _(index):
-        rows = rows_of(index)
-        dmix_rows = dmix_s[rows, :]
-        back_rows(
-            rows, width, w_s, dmix_rows, q_ref, k_ref, v_ref, att_ref, kt_s, dq_s, dk_s, dv_s
-        )
-
-        for number in range(1, 4):
-
-            @pl.when((step == 0) & (index == number))
-            def _(number=number):
-                next_hop(SUMS, sums_s, sums_r, number)
-
-        @pl.when((step == 1) & (index == 0))
+    @pl.when(step >= 4)
+    def _():
+        for slot in range(4):
+            w_s[slot] = unpack(wia_ref.at[0], slot, width)
+        for sums in (dk_s, dv_s):
+            sums[...] = jnp.zeros_like(sums)
+
+        @pl.loop(0, blocks)
+        def _(index):
+            rows = rows_of(index)
+            kt_s[:, rows] = k_ref[rows, :].T
+
+        @pl.loop(0, blocks)
+        def _(index):
+            rows = rows_of(index)
+            back_rows(
+                rows, width, w_s, dmix_s[rows, :], q_ref, k_ref, v_ref, att_ref.at[0], kt_s,
+                dq_s, dk_s, dv_s,
+            )
+
+            @pl.when((step == 4) & (index == 0))
+            def _():
+                next_hop(SUMS, sums_s, sums_r, 0)
+                inner.add_y(1)
+                inner.start_z(1)
+
+            @pl.when((step == 4) & (index == 1))
+            def _():
+                next_hop(SUMS, sums_s, sums_r, 1)
+
+            @pl.when((step == 4) & (index == 3))
+            def _():
+                next_hop(SUMS, sums_s, sums_r, 2)
+                inner.add_y(0)
+                inner.start_z(0)
+                outer.add_whole_x()
+                outer.y_copy(0).start()
+
+            @pl.when((step == 5) & (index == 0))
+            def _():
+                next_hop(SUMS, sums_s, sums_r, 3)
+
+            @pl.when((step == 5) & (index == 1))
+            def _():
+                next_hop(SUMS, sums_s, sums_r, 4)
+                inner.send_x()
+
+            @pl.when((step == 5) & (index == 3))
+            def _():
+                outer.add_y(0)
+                outer.start_z(0)
+
+            @pl.when((step == 6) & (index == 1))
+            def _():
+                gi_res[...] = inner.total()
+
+            @pl.when((step == 6) & (index == 3))
+            def _():
+                go_res[...] = outer.total_z(0)
+
+            @pl.when((step == 7) & (index == 3))
+            def _():
+                for reduce in attn:
+                    reduce.add_y(1)
+                    reduce.start_z(1)
+
+        @pl.loop(0, blocks)
+        def _(index):
+            rows = rows_of(index)
+            for_query, for_value = back_low(rows, width, dq_s, dk_s, dv_s, low_s)
+            for number, bits in enumerate(order):
+
+                @pl.when(step == 4 + number)
+                def _(bits=bits):
+                    late_s[0, pl.ds(partner(place, bits, 4), 1), :] += for_query
+                    late_s[0, pl.ds(4 + partner(place, bits, 4), 1), :] += for_value
+
+        for half, cols in enumerate(halves):
+
+            @pl.loop(0, model // (2 * share))
+            def _(z):
+                rows = pl.ds(pl.multiple_of(z * 2 * share, 2 * share), 2 * share)
+                slots = (0, 1) if half == 0 else (2, 3)
+                grads = back_weights(rows, width, slots, low_t, back_t, low_s, att_ref.at[0])
+                for y in range(2):
+                    piece = grads[y * share : (y + 1) * share]
+
+                    @pl.when(step < 6)
+                    def _(y=y, piece=piece):
+                        send_a[step - 4, z, y, :, cols] = piece
+
+                    @pl.when(step >= 6)
+                    def _(y=y, piece=piece):
+                        held_a[7 - step, z, y, :, cols] = piece
+
+            for number, j in ((0, 1), (1, 0)):
+
+                @pl.when(step == 4 + number)
+                def _(number=number, j=j):
+                    attn[half].core_copy(j, send_a.at[number]).start()
+
+            @pl.when(step == 7)
+            def _():
+                attn[half].add_core(0)
+                attn[half].y_copy(0).start()
+
+        @pl.when(step == 7)
         def _():
-            add_hop(SUMS, sums_s, sums_r, 4)
-
-        @pl.when((step == 1) & (index == 2))
-        def _():
-            for j in (1, 0):
-                inner.add_y(j)
-                inner.start_z(j)
-
-        @pl.when((step == 1) & (index == 3))
-        def _():
-            outer.add_whole_x()
-            outer.y_copy(0).start()
-            for bits in (2, 3, 1):
-                exchange(OUTPUTS, out_ref, out_res, bits, True).start()
-            keep_out.start()
-
-        @pl.when((step == 2) & (index == 2))
-        def _():
-            outer.add_y(0)
-            outer.start_z(0)
-
-        @pl.when((step == 3) & (index == 1))
-        def _():
-            inner.send_x()
-
-        @pl.when((step == 3) & (index == 3))
-        def _():
-            for reduce in attn:
-                reduce.add_y(1)
-                reduce.start_z(1)
-
-    @pl.loop(0, blocks)
-    def _(index):
-        rows = rows_of(index)
-        for_query, for_value = back_low(rows, width, dq_s, dk_s, dv_s, low_s)
-        for number, bits in enumerate((3, 1, 2, 0)):
-
-            @pl.when(step == number)
-            def _(bits=bits):
-                late_s[0, pl.ds(partner(place, bits, 4), 1), :] += for_query
-                late_s[0, pl.ds(4 + partner(place, bits, 4), 1), :] += for_value
-
-    share = held_i.shape[3]
-    for half in range(2):
-
-        @pl.loop(0, model // (2 * share))
-        def _(z):
-            rows = pl.ds(pl.multiple_of(z * 2 * share, 2 * share), 2 * share)
-            slots = (0, 1) if half == 0 else (2, 3)
-            grads = back_weights(rows, width, slots, xt_s, dmixt_s, low_s, att_ref)
-            for y in range(2):
-                piece = grads[y * share : (y + 1) * share]
-
-                @pl.when(step < 2)
-                def _(y=y, piece=piece):
-                    send_a[half, step, z, y] = piece
-
-                @pl.when(step >= 2)
-                def _(y=y, piece=piece):
-                    held_a[half, 3 - step, z, y] = piece
-
-        for number, j in ((0, 1), (1, 0)):
-
-            @pl.when(step == number)
-            def _(number=number, j=j):
-                attn[half].core_copy(j, send_a.at[half, number]).start()
-
-        @pl.when(step == 3)
-        def _():
-            attn[half].add_core(0)
-            attn[half].y_copy(0).start()
-
-    @pl.when(step == 3)
-    def _():
-        hop(LATE_SUMS, late_s, late_r, 0).start()
-
-    @pl.loop(0, quarters)
-    def _(index):
-        rows = rows_of(index, part)
-        dtok_s[rows, :] += back_tokens(rows, w_s, low_s)
-
-        @pl.when(step == 3)
-        def _():
-            dlow_s[index] = dtok_s[rows, :].astype(BF16)
-
-    @pl.when(step == 3)
+            hop(LATE_SUMS, late_s, late_r, 0).start()
+
+        @pl.loop(0, quarters)
+        def _(index):
+            rows = rows_of(index, part)
+            grad_s[rows, :] += back_tokens(rows, w_s, low_s)
+
+            @pl.when(step == 7)
+            def _():
+                flow_s[index] = grad_s[rows, :].astype(BF16)
+
+    @pl.when(step == 7)
     def _():
         for bits in (2, 3, 1):
-            exchange(TOKEN_GRADS, dlow_s, dtok_res, bits, True).start()
+            exchange(TOKEN_GRADS, flow_s, dtok_res, bits, True).start()
         keep_dtok.start()
         next_hop(LATE_SUMS, late_s, late_r, 0)
-        go_res[...] = outer.total_z(0)
-        inner.x_copy().wait_recv()
-        gi_res[...] = inner.total_z(0) + x_i[...].astype(F32)
-        next_hop(LATE_SUMS, late_s, late_r, 1)
         for reduce in attn:
             reduce.send_x()
-        next_hop(LATE_SUMS, late_s, late_r, 2)
-        for reduce in attn:
             reduce.add_y(0)
             reduce.start_z(0)
-        next_hop(LATE_SUMS, late_s, late_r, 3)
-        add_hop(LATE_SUMS, late_s, late_r, 4)
+        for number in range(1, len(HOPS)):
+            next_hop(LATE_SUMS, late_s, late_r, number)
         sum_res[...] = sums_s[5]
         late_res[...] = late_s[5]
-        for half, result in enumerate((ga_one, ga_two)):
-            attn[half].x_copy().wait_recv()
-            result[...] = attn[half].total_z(0) + x_a[half].astype(F32)
+        for reduce, cols in zip(attn, halves):
+            ga_res[:, cols] = reduce.total()
         for bits in (1, 2, 3):
             for base, source, target in (
-                (OUTPUTS, out_ref, out_res), (TOKEN_GRADS, dlow_s, dtok_res),
+                (OUTPUTS, out_s, out_res), (TOKEN_GRADS, flow_s, dtok_res),
             ):
                 exchange(base, source, target, bits, False).wait_recv()
                 exchange(base, source, target, bits, True).wait_send()
@@ -955,20 +1119,20 @@
         for number in range(len(HOPS)):
             hop(SUMS, sums_s, sums_r, number).wait_send()
             hop(LATE_SUMS, late_s, late_r, number).wait_send()
-        for copy in core_sends(inner, gi_ref) + core_sends(outer, go_ref):
-            copy.wait_send()
+        for number, j in ((0, 1), (1, 0)):
+            outer.core_copy(j, send_o.at[number]).wait_send()
+            for reduce in attn:
+                reduce.core_copy(j, send_a.at[number]).wait_send()
         inner.wait_sent((0, 1))
         inner.x_copy().wait_send()
         outer.wait_sent((0,))
         outer.whole_x_copy().wait_send()
-        for half, reduce in enumerate(attn):
-            for number, j in ((0, 1), (1, 0)):
-                reduce.core_copy(j, send_a.at[half, number]).wait_send()
+        for reduce in attn:
             reduce.wait_sent((0, 1))
             reduce.x_copy().wait_send()
 
 
-VMEM_LIMIT = 60 * 1024 * 1024
+VMEM_LIMIT = 62 * 1024 * 1024
 
 
 def resident(shape):
@@ -983,50 +1147,64 @@
     return [stepped(shape) if moves else resident(shape) for shape, moves in pairs]
 
 
-def attend_forward(tokens, cotangent, shard_a, shard_i, shard_o, biases, qaug, kaug, vaug, b_mixer):
+def near_forward(tokens, cotangent, shard_a, shard_i, shard_o, biases, augs, b_mixer, vectors):
     groups, part, model = tokens.shape
     length = groups * part
     share = shard_a.shape[0]
-    block = (groups, length, PAD)
-    whole = jax.ShapeDtypeStruct((groups, model // share, share, model), BF16)
-    hidden = shard_i.shape[1]
+    whole = (groups, model // share, share, model)
+    attended = (groups, length, PAD)
+    slopes = (groups, length, model)
+    flat = (length, model)
     anywhere = pl.BlockSpec(memory_space=pl.ANY)
+
+    def early(shape):
+        return pl.BlockSpec(
+            (1,) + shape[1:], lambda step: (jnp.minimum(step, 3),) + (0,) * (len(shape) - 1)
+        )
+
+    def late(shape):
+        return pl.BlockSpec(
+            (1,) + shape[1:], lambda step: (jnp.maximum(step - 4, 0),) + (0,) * (len(shape) - 1)
+        )
+
+    kept = [biases, *augs, b_mixer, vectors]
     return pl.pallas_call(
-        attend_kernel,
-        grid=(groups,),
-        out_shape=[jax.ShapeDtypeStruct(block, BF16)] * 4
-        + [
-            jax.ShapeDtypeStruct((length, model), F32),
-            jax.ShapeDtypeStruct((groups, 1, hidden), F32),
+        forward_kernel,
+        grid=(2 * groups,),
+        out_shape=[
+            jax.ShapeDtypeStruct((2 * groups, length, model), BF16),
+            jax.ShapeDtypeStruct(attended, BF16),
+            jax.ShapeDtypeStruct(slopes, BF16),
+            jax.ShapeDtypeStruct(flat, F32),
+            jax.ShapeDtypeStruct(flat, F32),
+            jax.ShapeDtypeStruct(flat, BF16),
             jax.ShapeDtypeStruct(tokens.shape, BF16),
             jax.ShapeDtypeStruct(tokens.shape, BF16),
-            whole,
-            whole,
-            whole,
+            jax.ShapeDtypeStruct((2,) + whole, BF16),
+            jax.ShapeDtypeStruct(whole, BF16),
         ],
-        in_specs=[anywhere] * 5
-        + spec_list(
-            [
-                (biases.shape, 0), (qaug.shape, 0), (kaug.shape, 0), (vaug.shape, 0),
-                (b_mixer.shape, 0),
-            ]
-        ),
-        out_specs=spec_list([(block, 1)] * 4 + [((length, model), 0), ((groups, 1, hidden), 1)])
-        + [anywhere] * 5,
+        in_specs=[anywhere] * 5 + [resident(each.shape) for each in kept],
+        out_specs=[stepped((2 * groups, length, model)), early(attended), late(slopes)]
+        + [anywhere] * 7,
         scratch_shapes=[
             pltpu.VMEM((4, model, PAD), BF16),
             pltpu.VMEM(tokens.shape, BF16),
-            pltpu.VMEM(whole.shape, BF16),
+            pltpu.VMEM(whole, BF16),
+            pltpu.VMEM(whole, BF16),
+            pltpu.VMEM(whole, BF16),
             pltpu.VMEM((groups,) + biases.shape, F32),
+            pltpu.VMEM(flat, F32),
+            pltpu.VMEM(flat, F32),
+            pltpu.VMEM(flat, BF16),
             pltpu.SemaphoreType.DMA((FORWARD_WIRES,)),
             pltpu.SemaphoreType.DMA((FORWARD_WIRES,)),
-            pltpu.SemaphoreType.DMA((8,)),
+            pltpu.SemaphoreType.DMA((13,)),
         ],
         compiler_params=pltpu.CompilerParams(
             vmem_limit_bytes=VMEM_LIMIT, collective_id=0, has_side_effects=True
         ),
-        name="attend_forward",
-    )(tokens, cotangent, shard_a, shard_i, shard_o, biases, qaug, kaug, vaug, b_mixer)
+        name="near_forward",
+    )(tokens, cotangent, shard_a, shard_i, shard_o, *kept)
 
 
 def attend_plain(x, a_all, biases, qaug, kaug, vaug, b_mixer):
@@ -1125,66 +1303,79 @@
             pltpu.VMEM((PAD, length), F32),
             pltpu.VMEM((length, PAD), F32),
             pltpu.VMEM((length, PAD), F32),
-            pltpu.VMEM((3, length, PAD), BF16),
+            pltpu.VMEM((length, 3 * PAD), BF16),
         ],
         compiler_params=pltpu.CompilerParams(vmem_limit_bytes=VMEM_LIMIT),
         name="attend_backward",
     )(x, a_all, d_mixed, d_first, q, k, v, attended)
 
 
-def attend_reduce(x, a_all, d_mixed, d_first, q, k, v, attended, g_inner, g_outer, out, dbi, small):
+def near_backward(acts, attended, slopes, w_ia, w_o, vectors, second, first, low, x, cotangent):
     quarters, part, model = x.shape
     length = quarters * part
     share = model // 8
-    half = model // 2
     block = (4, 2, share, model)
     anywhere = pl.BlockSpec(memory_space=pl.ANY)
 
-    def ordered(shape):
+    def ordered(shape, place):
         return pl.BlockSpec(
-            (1,) + shape[1:], lambda step: (slot_at(step),) + (0,) * (len(shape) - 1)
-        )
+            (1,) + shape[1:], lambda step: (place(step),) + (0,) * (len(shape) - 1)
+        )
+
+    def acts_at(step):
+        return jnp.where(step < 4, 4 + slot_at(step), slot_at(step - 4))
+
+    def weights_at(step):
+        return jnp.where(step < 4, slot_at(step), 4 + slot_at(step - 4))
+
+    def first_half(step):
+        return slot_at(jnp.minimum(step, 3))
+
+    def last_half(step):
+        return slot_at(jnp.maximum(step - 4, 0))
 
     def vmem(*shape, kind=BF16):
         return pltpu.VMEM(shape, kind)
 
     final = [
-        ((share, half), F32), ((share, half), F32), ((share, model), F32), ((share, model), F32),
-        ((16, model), F32), ((8, PAD), F32),
+        ((share, model), F32), ((share, model), F32), ((share, model), F32), ((16, model), F32),
+        ((8, PAD), F32),
     ]
     return pl.pallas_call(
-        attend_reduce_kernel,
-        grid=(4,),
+        backward_kernel,
+        grid=(8,),
         out_shape=[jax.ShapeDtypeStruct(x.shape, BF16)] * 2
         + [jax.ShapeDtypeStruct(*each) for each in final],
-        in_specs=[anywhere, ordered(a_all.shape), anywhere, anywhere]
-        + [ordered(q.shape)] * 4
-        + [anywhere] * 3
-        + [resident(dbi.shape), resident(small.shape)],
+        in_specs=[
+            ordered(acts.shape, acts_at), ordered(attended.shape, last_half),
+            ordered(slopes.shape, first_half), ordered(w_ia.shape, weights_at),
+            ordered(w_o.shape, first_half), resident(vectors.shape),
+        ]
+        + [anywhere] * 5,
         out_specs=[anywhere] * 2 + [resident(each[0]) for each in final],
         scratch_shapes=[
-            vmem(4, model, PAD), vmem(model, length), vmem(model, length), vmem(PAD, length),
-            vmem(PAD, length, kind=F32), vmem(length, PAD, kind=F32),
-            vmem(length, PAD, kind=F32), vmem(3, length, PAD), vmem(length, model),
-            vmem(length, model, kind=F32), vmem(quarters, part, model),
+            vmem(model, length), vmem(model, length), vmem(length, model), vmem(length, 3 * PAD),
+            vmem(*x.shape), vmem(*x.shape), vmem(length, model, kind=F32),
+            vmem(2, ROWS, model, kind=F32),
+            vmem(4, model, PAD), vmem(PAD, length), vmem(PAD, length, kind=F32),
+            vmem(length, PAD, kind=F32), vmem(length, PAD, kind=F32),
             vmem(6, 16, model, kind=F32), vmem(6, 8, PAD, kind=F32),
             vmem(5, 16, model, kind=F32), vmem(5, 8, PAD, kind=F32),
+            vmem(2, *block), vmem(2, *block), vmem(2, *block), vmem(2, 4, share, model),
+            vmem(2, 3, share, model), vmem(share, model),
+            vmem(2, *block), vmem(2, *block), vmem(2, *block), vmem(1, 4, share, model),
+            vmem(1, 3, share, model), vmem(*block),
             vmem(2, *block), vmem(2, *block), vmem(2, 4, share, model),
             vmem(2, 3, share, model), vmem(share, model),
-            vmem(2, *block), vmem(2, *block), vmem(1, 4, share, model),
-            vmem(1, 3, share, model), vmem(*block),
-            vmem(2, 2, 4, 2, share, half), vmem(2, 2, 4, 2, share, half),
-            vmem(2, 2, 4, 2, share, half), vmem(2, 2, 4, share, half),
-            vmem(2, 2, 3, share, half), vmem(2, share, half),
             pltpu.SemaphoreType.DMA((BACKWARD_WIRES,)),
             pltpu.SemaphoreType.DMA((BACKWARD_WIRES,)),
-            pltpu.SemaphoreType.DMA((9,)),
+            pltpu.SemaphoreType.DMA((8,)),
         ],
         compiler_params=pltpu.CompilerParams(
             vmem_limit_bytes=VMEM_LIMIT, collective_id=1, has_side_effects=True
         ),
-        name="attend_reduce",
-    )(x, a_all, d_mixed, d_first, q, k, v, attended, g_inner, g_outer, out, dbi, small)
+        name="near_backward",
+    )(acts, attended, slopes, w_ia, w_o, vectors, second, first, low, x, cotangent)
 
 
 def augment(labels, width):
@@ -1220,20 +1411,14 @@
     biases = jnp.concatenate([b_query, spare, b_value, spare, b_inner])[None]
     vectors = jnp.stack([gain_one, bias_one, b_outer, gain_two, bias_two] + [b_outer] * 3)
     if near:
-        *saved, first_sum, bi, x, cot, a_all, wi, wo = attend_forward(
-            tokens[:, 0], cotangent[:, 0], shard_a, w_inner, shard_o, biases, qaug, kaug, vaug,
-            b_mixer[None],
-        )
-        a_all, wi, wo = (part.reshape(groups, model, model) for part in (a_all, wi, wo))
-        out, d_first, d_mixed, g_inner, g_outer, dbi, small = dense_both(
-            first_sum, wi, wo, bi, vectors, cot.reshape(length, model)
-        )
-        pieces = (groups, 4, 2, model // rings, model)
-        out, d_tokens, ga_one, ga_two, gi, go, tail, late = attend_reduce(
-            x, a_all, d_mixed, d_first, *saved, g_inner.reshape(pieces), g_outer.reshape(pieces),
-            out.reshape(x.shape), dbi, small,
-        )
-        ga = jnp.concatenate([ga_one, ga_two], axis=1)
+        acts, attended, slopes, first, second, low, x, cot, w_ia, w_o = near_forward(
+            tokens[:, 0], cotangent[:, 0], shard_a, w_inner, shard_o, biases, (qaug, kaug, vaug),
+            b_mixer[None], vectors,
+        )
+        out, d_tokens, ga, gi, go, tail, late = near_backward(
+            acts, attended, slopes, w_ia.reshape(2 * groups, model, model),
+            w_o.reshape(groups, model, model), vectors, second, first, low, x, cot,
+        )
         own = lambda whole, start: lax.dynamic_index_in_dim(whole, start + place, 0, False)
         dbq, dbv = own(late, 0)[:width], own(late, groups)[:width]
         dbi = own(tail, 0)

time: 348 us -> 312 us (0.90)
  Pallas kernels: 323 us -> 286 us
    pallas_call x3 -> x2, Pallas kernels: 323 us -> 286 us  [the longest x1 183 us: near_backward(): pl.pallas_call(backward_kernel, grid=(8,), out_shape=[jax.ShapeDtypeStruc...]
where the time goes in v4:
time: 312 us; the launch traced here: 311 us
  Pallas kernels  286 us (92%)
  local copies, waits for them, and re-layouts  15.9 us (5%)
  other arithmetic  7.78 us (2%)
    pallas_call x1, Pallas kernels, near_backward(): pl.pallas_call(backward_kernel, grid=(8,), out_shape=[jax.ShapeDtypeStruc...  183 us
    pallas_call x1, Pallas kernels, near_forward(): pl.pallas_call(forward_kernel, grid=(2 * groups,), out_shape=[jax.ShapeDt...  104 us

profile of v4, /device:TPU:0, one launch (start us, length us, event | category | flops | bytes accessed | tf_op | source)
XLA Modules:
  0.0 310.9 jit_solution(9707055161628280220)
XLA Ops:
  0.7 0.0 copy-start
  0.7 0.6 fusion.1.vaug_ref
  1.3 1.3 broadcast_in_dim.49.bm_ref
  2.5 0.7 stack.21
  3.2 0.7 stack.22
  3.9 0.7 stack.23
  4.6 0.7 stack.24
  5.3 0.7 stack.25
  6.0 0.0 copy-done
  6.0 0.8 concatenate.7
  6.8 0.6 broadcast_in_dim.41.bias_ref
  7.4 0.6 stack.26.vec_ref
  8.1 0.9 copy.35
  8.9 1.6 pad_maximum_fusion.sa_ref
  10.6 1.1 select_convert_fusion.kaug_ref
  11.6 1.0 select_convert_fusion.1.qaug_ref
  12.7 103.8 %near_forward.1 = (bf16[8,1024,768]{2,1,0:T(8,128)(2,1)}, bf16[4,1024,256]{2,1,0:T(8,128)(2,1)}, bf16[4,1024,768]{2,1,0:T(8,128)(2,1)}, f32[1024,768]{1,0:T(8,12...) custom-call(bf16[4,256,768]{2,1,0:T(8,128)(2,1)} %bitcast.23, ...), custom_call_target="tpu_custom_call" | custom-call | tf_op jit(solution)/shard_map/near_forward/pallas_call | solution.py:1171
  116.5 182.7 %near_backward.1 = (bf16[4,256,768]{2,1,0:T(8,128)(2,1)}, bf16[4,256,768]{2,1,0:T(8,128)(2,1)}, f32[96,768]{1,0:T(8,128)}, f32[96,768]{1,0:T(8,128)}, f32[96,768...) custom-call(bf16[8,1024,768]{2,1,0:T(8,128)(2,1)} %get-tuple-element.34.acts_ref, ...), custom_call_target="tpu_custom_call" | custom-call | tf_op jit(solution)/shard_map/near_backward/pallas_call | solution.py:1344
  299.2 1.4 constant_dynamic-slice_fusion
  300.5 1.8 slice_reduce_fusion
  302.3 1.8 slice_bitcast_fusion
  304.1 0.7 copy.38
  304.9 0.0 copy-start.1
  304.9 3.5 %bitcast_convert_fusion = f32[4,1,256,768]{3,2,1,0:T(8,128)} fusion(bf16[4,256,768]{2,1,0:T(8,128)(2,1)} %get-tuple-element.45), kind=kLoop, calls=%fused_computation | loop fusion | flops 786432 | bytes 4718592
  308.3 0.0 copy-done.1
  308.3 0.0 copy-start.3
  308.3 0.0 copy-start.2
  308.3 1.1 copy.42
  309.5 0.0 copy-done.3
  309.5 0.7 copy.43
  310.2 0.0 copy-done.2
  310.2 0.7 copy.44
  (5 shorter events, 0.0 us)
Async XLA Ops:
  0.7 5.3 %copy-start = (s32[4,1,1024]{2,1,0:T(1,128)S(1)}, s32[4,1,1024]{2,1,0:T(1,128)}, u32[]{:S(2)}) copy-start(s32[4,1,1024]{2,1,0:T(1,128)} %param.19) | copy-start | bytes 49156
  304.9 3.5 %copy-start.1 = (bf16[4,256,768]{2,1,0:T(8,128)(2,1)S(1)}, bf16[4,256,768]{2,1,0:T(8,128)(2,1)}, u32[]{:S(2)}) copy-start(bf16[4,256,768]{2,1,0:T(8,128)(2,1)} %get-tuple-element.44) | copy-start | bytes 4718596
  308.3 1.1 copy-start.3
  308.3 1.9 copy-start.2

commit v5 on v4

--- a/solution.py
+++ b/solution.py
@@ -260,26 +260,86 @@
     return jnp.sum(values, axis=0, keepdims=True)
 
 
+WIDE = 512
+SEG = 16
+
+
+def head_rows(head):
+    return slice(head * HEAD, (head + 1) * HEAD)
+
+
+def extra_rows(head, width):
+    return slice(width + head * SEG, width + (head + 1) * SEG)
+
+
+def place_head(part, extra, head, width):
+    count = part.shape[1]
+    zeros = lambda rows: [jnp.zeros((rows, count), part.dtype)] if rows else []
+    pieces = zeros(head * HEAD) + [part] + zeros(width - (head + 1) * HEAD)
+    pieces += zeros(head * SEG) + [extra] + zeros(PAD - width - (head + 1) * SEG)
+    return jnp.concatenate(pieces, axis=0)
+
+
+def parts_rows(values, before):
+    parts = [part for part in three_parts(values)]
+    rest = jnp.zeros((SEG - DOCS - 3, values.shape[1]), BF16)
+    return jnp.concatenate([before] + parts + [rest], axis=0)
+
+
+def attend_block(cols, width, key_ref, vt_s, side_ref):
+    outs = []
+    for head in range(width // HEAD):
+        docs = side_ref[extra_rows(head, width), cols]
+        queries = place_head(side_ref[head_rows(head), cols], docs, head, width)
+        scores = dot_nn(key_ref[...], queries)
+        highest = jnp.max(scores, axis=0, keepdims=True)
+        raw = jnp.exp2((scores - highest) * LOG2E).astype(BF16)
+        mixed = dot_nn(vt_s[head], raw)
+        total = mixed[HEAD : HEAD + 1]
+        outs.append((mixed[:HEAD] / total).astype(BF16))
+        logs = -(highest + jnp.log(total))
+        side_ref[extra_rows(head, width), cols] = parts_rows(logs, docs[:DOCS])
+    return jnp.concatenate(outs, axis=0)
+
+
+def attend_block_back(cols, width, key_ref, value_ref, side_ref, do_s, kt_s, all_t, dk_t, dv_t):
+    for head in range(width // HEAD):
+        queries = side_ref[head_rows(head), cols]
+        d_att = do_s[head_rows(head), cols]
+        extra = extra_rows(head, width)
+        chances = jnp.exp2(
+            dot_nn(key_ref[...], place_head(queries, side_ref[extra, cols], head, width)) * LOG2E
+        )
+        d_chances = dot_nn(value_ref[...], place_head(d_att, do_s[extra, cols], head, width))
+        d_scores = (chances * d_chances).astype(BF16)
+        d_query = dot_nn(kt_s[head_rows(head), :], d_scores) * HEAD**-0.5
+        all_t[head_rows(head), cols] = d_query.astype(BF16)
+        dk_t[head_rows(head), :] += dot_nt(queries, d_scores)
+        dv_t[head_rows(head), :] += dot_nt(d_att, chances.astype(BF16))
+
+
 def forward_kernel(
-    tok_ref, cot_ref, sa_ref, si_ref, so_ref, bias_ref, qaug_ref, kaug_ref, vaug_ref, bm_ref,
-    vec_ref,
-    acts_ref, att_ref, slope_ref, first_out, second_out, low_out, x_out, cot_out, wia_out, wo_out,
-    w_s, x_s, a_s, i_s, o_s, bias_s, first_s, second_s, low_s, send_sem, recv_sem, here_sem,
+    tok_ref, cot_ref, si_ref, wq_ref, wk_ref, wv_ref, wm_ref, wo_ref, doc_ref, vec_ref,
+    acts_ref, side_ref, slope_ref, first_out, second_out, low_out, xt_out, cot_out, wia_out,
+    wo_out,
+    sa_s, so_s, w_s, wm_s, x_s, xt_s, a_s, i_s, o_s, bias_s, kaug_s, qdoc_s, vt_s, mix_s,
+    first_s, second_s, low_s, send_sem, recv_sem, here_sem,
 ):
     step = pl.program_id(0)
     place = lax.axis_index("tensor")
     row = lax.axis_index("dp")
     quarters, part, model = x_s.shape
     length = quarters * part
-    width = sa_ref.shape[1] // 4
+    share, width = wq_ref.shape
+    heads = width // HEAD
     blocks = length // ROWS
-    share = sa_ref.shape[0]
+    wides = length // WIDE
     wires = Wires(send_sem, recv_sem, place, row)
-    attn = ShardGather(wires, KIND_A, sa_ref, a_s)
+    attn = ShardGather(wires, KIND_A, sa_s, a_s)
     inner = ShardGather(wires, KIND_I, si_ref, i_s)
-    outer = BlockGather(wires, KIND_O, so_ref, o_s)
-    gain_one, bias_one, b_outer = (vec_ref[i : i + 1, :] for i in range(3))
-    q_ref, k_ref, v_ref = (acts_ref.at[0, :, i * PAD : (i + 1) * PAD] for i in range(3))
+    outer = BlockGather(wires, KIND_O, so_s, o_s)
+    b_mixer, gain_one, bias_one, b_outer = (vec_ref[i : i + 1, :] for i in range(4))
+    key_ref, value_ref = (acts_ref.at[0, :, i * PAD : (i + 1) * PAD] for i in range(2))
 
     def exchange(base, source, target, bits, mine):
         other = partner(place, bits, 4)
@@ -288,17 +348,17 @@
         )
 
     def bias_copy(bits, mine):
-        return wires.copy(BIASES + bits - 1, bias_ref, bias_s.at[bits], bits, 0)
+        return wires.copy(BIASES + bits - 1, vec_ref, bias_s.at[bits], bits, 0)
 
     local = [
         pltpu.make_async_copy(tok_ref.at[place], x_s.at[place], here_sem.at[0]),
-        pltpu.make_async_copy(sa_ref, a_s.at[0, row], here_sem.at[1]),
+        pltpu.make_async_copy(sa_s, a_s.at[0, row], here_sem.at[1]),
         pltpu.make_async_copy(si_ref, i_s.at[0, row], here_sem.at[2]),
-        pltpu.make_async_copy(so_ref, o_s.at[0, row], here_sem.at[3]),
-        pltpu.make_async_copy(bias_ref, bias_s.at[0], here_sem.at[4]),
+        pltpu.make_async_copy(so_s, o_s.at[0, row], here_sem.at[3]),
+        pltpu.make_async_copy(vec_ref, bias_s.at[0], here_sem.at[4]),
     ]
     own_cot = pltpu.make_async_copy(cot_ref.at[place], cot_out.at[place], here_sem.at[5])
-    keep_x = pltpu.make_async_copy(x_s, x_out, here_sem.at[6])
+    keep_x = pltpu.make_async_copy(xt_s, xt_out, here_sem.at[6])
     keep_a = pltpu.make_async_copy(a_s, wia_out.at[1], here_sem.at[7])
     keep_i = pltpu.make_async_copy(i_s, wia_out.at[0], here_sem.at[8])
     keep_o = pltpu.make_async_copy(o_s, wo_out, here_sem.at[9])
@@ -308,6 +368,9 @@
 
     @pl.when(step == 0)
     def _():
+        sa_s[...] = jnp.concatenate(
+            [wq_ref[...], wk_ref[...], wv_ref[...], wm_ref[...].T], axis=1
+        )
         greet(wires, PEERS)
         attn.cross_x().start()
         for bits in (1, 2, 3):
@@ -316,9 +379,24 @@
         attn.along_y(0, 0, True).start()
         for bits in (2, 3, 1):
             exchange(TOKENS, tok_ref, x_s, bits, True).start()
+        so_s[...] = wo_ref[...].T
         for copy in local:
             copy.start()
         own_cot.start()
+        labels = doc_ref[place]
+        docs = lax.broadcasted_iota(jnp.int32, (DOCS, length), 0)
+        same = docs == labels
+        ones = jnp.ones((3, length), F32)
+        rest = jnp.zeros((SEG - DOCS - 3, length), F32)
+        qdoc_s[...] = jnp.concatenate(
+            [jnp.where(same, 1.0, 0.0), jnp.zeros((SEG - DOCS, length), F32)], axis=0
+        ).astype(BF16)
+        one_head = jnp.concatenate([jnp.where(same, 0.0, -(2.0**100)), ones, rest], axis=0)
+        tall = jnp.zeros((width - PAD // 2, length), F32)
+        last = jnp.zeros((PAD - width - heads * SEG, length), F32)
+        kaug_s[...] = jnp.concatenate([tall] + [one_head] * heads + [last], axis=0).astype(BF16).T
+        for head in range(heads):
+            vt_s[head, HEAD:, :] = jnp.ones((SEG, length), BF16)
         for copy in local:
             copy.wait()
         attn.cross_x().wait_recv()
@@ -332,12 +410,19 @@
         for bits in (1, 2, 3):
             exchange(TOKENS, tok_ref, x_s, bits, False).wait_recv()
             bias_copy(bits, False).wait_recv()
+
+        @pl.loop(0, quarters)
+        def _(index):
+            rows = rows_of(index, part)
+            first_s[rows, :] = x_s[index].astype(F32) + b_mixer
+
+    @pl.when(step == 1)
+    def _():
+        @pl.loop(0, quarters)
+        def _(index):
+            xt_s[:, rows_of(index, part)] = x_s[index].T
+
         keep_x.start()
-
-        @pl.loop(0, quarters)
-        def _(index):
-            rows = rows_of(index, part)
-            first_s[rows, :] = x_s[index].astype(F32) + bm_ref[...]
 
     @pl.when(step == 1)
     def _():
@@ -358,26 +443,50 @@
         for dp_row in range(a_s.shape[1]):
             packed = a_s[step, dp_row]
             rest = jnp.zeros((share, PAD - width), packed.dtype)
+            rows = slice(dp_row * share, (dp_row + 1) * share)
             for slot in range(4):
                 piece = packed[:, slot * width : (slot + 1) * width]
-                rows = slice(dp_row * share, (dp_row + 1) * share)
-                w_s[slot, rows, :] = jnp.concatenate([piece, rest], axis=1)
-        biases = bias_s[step]
-
-        @pl.loop(0, quarters)
-        def _(index):
-            rows = rows_of(index, part)
-            x_rows = x_s[index]
-            project(
-                x_rows, rows, biases[:, :PAD], biases[:, PAD : 2 * PAD], w_s, qaug_ref, kaug_ref,
-                vaug_ref, q_ref, k_ref, v_ref,
-            )
+                piece = jnp.concatenate([piece, rest], axis=1)
+                if slot < 3:
+                    w_s[rows, slot * PAD : (slot + 1) * PAD] = piece
+                else:
+                    wm_s[rows, :] = piece
+        bias = bias_s[step][7:8]
+        lanes = lax.broadcasted_iota(jnp.int32, (1, PAD), 1) - width
+        spare = (lanes >= 0) & (lanes < heads * SEG) & (lax.rem(lanes + SEG, SEG) >= DOCS)
+        vaug = jnp.where(spare & (lax.rem(lanes + SEG, SEG) < DOCS + 3), 1.0, 0.0).astype(BF16)
+
+        @pl.loop(0, wides)
+        def _(index):
+            rows = rows_of(index, WIDE)
+            x_rows = x_s[pl.ds(index * (WIDE // part), WIDE // part)].reshape(WIDE, model)
+            result = dot_nn(x_rows, w_s[...])
+            queries = (result[:, :PAD] + bias[:, :PAD]).astype(BF16)
+            queries = (queries * jnp.asarray(HEAD**-0.5, BF16)).T
+            side_ref[0, :width, rows] = queries[:width]
+            side_ref[0, PAD + width :, rows] = jnp.zeros((PAD - width, WIDE), BF16)
+            keys = result[:, PAD : 2 * PAD].astype(BF16)
+            key_ref[rows, : PAD // 2] = keys[:, : PAD // 2]
+            key_ref[rows, PAD // 2 :] = keys[:, PAD // 2 :] + kaug_s[rows, :]
+            values = (result[:, 2 * PAD :] + bias[:, PAD : 2 * PAD]).astype(BF16)
+            value_ref[rows, :] = values + vaug
+            values_t = values.T
+            for head in range(heads):
+                vt_s[head, :HEAD, rows] = values_t[head_rows(head)]
+
+        for head in range(heads):
+            side_ref[0, extra_rows(head, width), :] = qdoc_s[...]
+        side_ref[0, width + heads * SEG : PAD, :] = jnp.zeros(
+            (PAD - width - heads * SEG, length), BF16
+        )
 
         @pl.loop(0, blocks)
         def _(index):
-            attend_rows(
-                rows_of(index), width, w_s, q_ref, k_ref, v_ref, att_ref.at[0], first_s
-            )
+            cols = rows_of(index)
+            attended = attend_block(cols, width, key_ref, vt_s, side_ref.at[0])
+            side_ref[0, PAD : PAD + width, cols] = attended
+            rest = jnp.zeros((PAD - width, ROWS), BF16)
+            mix_s[cols, :] = jnp.concatenate([attended, rest], axis=0).T
 
             @pl.when((step == 0) & (index == 0))
             def _():
@@ -427,6 +536,11 @@
             def _():
                 inner.wait_z(2)
                 inner.pass_y(2)
+
+        @pl.loop(0, wides)
+        def _(index):
+            rows = rows_of(index, WIDE)
+            first_s[rows, :] += dot_nt(mix_s[rows, :], wm_s[...])
 
     @pl.when(step == 4)
     def _():
@@ -466,11 +580,11 @@
         slot = step - 4
         w_inner = i_s[slot].reshape(model, model)
         w_outer = o_s[slot].reshape(model, model)
-        b_inner = bias_s[slot][:, 2 * PAD :]
-
-        @pl.loop(0, blocks)
-        def _(index):
-            rows = rows_of(index)
+        b_inner = bias_s[slot][6:7]
+
+        @pl.loop(0, wides)
+        def _(index):
+            rows = rows_of(index, WIDE)
             value, slope = gelu_parts(dot_nn(low_s[rows, :], w_inner) + b_inner)
             hidden = value.astype(BF16)
             acts_ref[0, rows, :] = hidden
@@ -795,11 +909,11 @@
 
 
 def backward_kernel(
-    acts_ref, att_ref, slope_ref, wia_ref, wo_ref, vec_ref, second_ref, first_ref, low_ref, x_ref,
+    acts_ref, side_ref, slope_ref, wia_ref, wo_ref, vec_ref, second_ref, first_ref, low_ref, xt_ref,
     cot_ref,
     out_res, dtok_res, ga_res, gi_res, go_res, sum_res, late_res,
-    low_t, back_t, dmix_s, low_s, flow_s, out_s, grad_s, first_s, w_s, kt_s, dq_s, dk_s, dv_s,
-    sums_s, late_s, sums_r, late_r,
+    low_t, back_t, dmix_s, low_s, flow_s, out_s, grad_s, first_s, wmt_s, do_s, kt_s, all_t, dk_t,
+    dv_t, sums_s, late_s, sums_r, late_r,
     send_i, held_i, core_i, y_i, z_i, x_i, send_o, held_o, core_o, y_o, z_o, x_o,
     held_a, core_a, y_a, z_a, x_a,
     send_sem, recv_sem, here_sem,
@@ -810,7 +924,9 @@
     length, model = dmix_s.shape
     quarters, part, _ = flow_s.shape
     width = wia_ref.shape[2] // 4
+    heads = width // HEAD
     blocks = length // ROWS
+    wides = length // WIDE
     share = held_i.shape[3]
     wires = Wires(send_sem, recv_sem, place, row)
     inner = Reduce(wires, RED_I, held_i, core_i, y_i, z_i, x_i)
@@ -821,8 +937,9 @@
         Reduce(wires, RED_A + half * Reduce.COUNT, held_a, core_a, y_a, z_a, x_a, cols)
         for half, cols in enumerate(halves)
     ]
-    gain_one, gain_two, bias_two = (vec_ref[i : i + 1, :] for i in (0, 3, 4))
-    q_ref, k_ref, v_ref = (acts_ref.at[0, :, i * PAD : (i + 1) * PAD] for i in range(3))
+    gain_one, gain_two, bias_two = (vec_ref[i : i + 1, :] for i in (1, 4, 5))
+    key_ref, value_ref = (acts_ref.at[0, :, i * PAD : (i + 1) * PAD] for i in range(2))
+    att_ref = side_ref.at[0, PAD : PAD + width]
 
     def exchange(base, source, target, bits, mine):
         other = partner(place, bits, 4)
@@ -843,7 +960,7 @@
     load_second = pltpu.make_async_copy(second_ref, grad_s, here_sem.at[0])
     load_cot = pltpu.make_async_copy(cot_ref, flow_s, here_sem.at[1])
     load_low = pltpu.make_async_copy(low_ref, low_s, here_sem.at[2])
-    load_x = pltpu.make_async_copy(x_ref, flow_s, here_sem.at[3])
+    load_x = pltpu.make_async_copy(xt_ref, low_t, here_sem.at[3])
     keep_out = pltpu.make_async_copy(out_s.at[place], out_res.at[place], here_sem.at[4])
     keep_dtok = pltpu.make_async_copy(flow_s.at[place], dtok_res.at[place], here_sem.at[5])
 
@@ -885,13 +1002,12 @@
         for bits in (2, 3, 1):
             exchange(OUTPUTS, out_s, out_res, bits, True).start()
         keep_out.start()
-        load_x.start()
 
     @pl.when(step < 4)
     def _():
-        @pl.loop(0, blocks)
-        def _(index):
-            rows = rows_of(index)
+        @pl.loop(0, wides)
+        def _(index):
+            rows = rows_of(index, WIDE)
             d_hidden = dot_nn(dmix_s[rows, :], wo_ref[0])
             d_inner = (d_hidden * slope_ref[0, rows, :].astype(F32)).astype(BF16)
             low_s[rows, :] = d_inner
@@ -904,23 +1020,22 @@
 
             grad_s[rows, :] += dot_nt(d_inner, wia_ref[0])
 
-        @pl.loop(0, model // (2 * share))
-        def _(z):
-            rows = pl.ds(pl.multiple_of(z * 2 * share, 2 * share), 2 * share)
+        @pl.loop(0, model // (4 * share))
+        def _(pair):
+            rows = rows_of(pair, 4 * share)
             for transposed, right, sent, held in (
                 (back_t, acts_ref.at[0], send_o, held_o), (low_t, low_s, send_i, held_i),
             ):
                 grads = dot_nn(transposed[rows, :], right[...]).astype(BF16)
-                for y in range(2):
-                    piece = grads[y * share : (y + 1) * share]
-
-                    @pl.when(step < 2)
-                    def _(y=y, piece=piece, sent=sent):
-                        sent[step, z, y] = piece
-
-                    @pl.when(step >= 2)
-                    def _(y=y, piece=piece, held=held):
-                        held[3 - step, z, y] = piece
+                pieces = grads.reshape(2, 2, share, model)
+
+                @pl.when(step < 2)
+                def _(pieces=pieces, sent=sent):
+                    sent[step, pl.ds(2 * pair, 2)] = pieces
+
+                @pl.when(step >= 2)
+                def _(pieces=pieces, held=held):
+                    held[3 - step, pl.ds(2 * pair, 2)] = pieces
 
     for number, j in ((0, 1), (1, 0)):
 
@@ -943,7 +1058,7 @@
         inner.add_core(0)
         inner.y_copy(0).start()
         outer.add_core(0)
-        load_x.wait()
+        load_x.start()
         for index in range(blocks):
             rows = slice(index * ROWS, (index + 1) * ROWS)
             load_first(index).wait()
@@ -959,7 +1074,7 @@
             lower = d_first.astype(BF16)
             dmix_s[rows, :] = lower
             back_t[:, rows] = lower.T
-            low_t[:, rows] = flow_s[index].T
+        load_x.wait()
         hop(SUMS, sums_s, sums_r, 0).start()
 
     @pl.when(step == 4)
@@ -975,22 +1090,27 @@
 
     @pl.when(step >= 4)
     def _():
-        for slot in range(4):
-            w_s[slot] = unpack(wia_ref.at[0], slot, width)
-        for sums in (dk_s, dv_s):
+        wmt_s[...] = wia_ref[0, :, 3 * width :].T
+        for sums in (dk_t, dv_t):
             sums[...] = jnp.zeros_like(sums)
 
+        @pl.loop(0, wides)
+        def _(index):
+            cols = rows_of(index, WIDE)
+            kt_s[:, cols] = key_ref[cols, :].T[:width]
+            d_att = dot_nn(wmt_s[...], back_t[:, cols]).astype(BF16)
+            do_s[:width, cols] = d_att
+            product = d_att.astype(F32) * att_ref[:, cols].astype(F32)
+            none = jnp.zeros((DOCS, WIDE), BF16)
+            for head in range(heads):
+                centre = column_sum(product[head_rows(head)])
+                do_s[extra_rows(head, width), cols] = parts_rows(-centre, none)
+
         @pl.loop(0, blocks)
         def _(index):
-            rows = rows_of(index)
-            kt_s[:, rows] = k_ref[rows, :].T
-
-        @pl.loop(0, blocks)
-        def _(index):
-            rows = rows_of(index)
-            back_rows(
-                rows, width, w_s, dmix_s[rows, :], q_ref, k_ref, v_ref, att_ref.at[0], kt_s,
-                dq_s, dk_s, dv_s,
+            attend_block_back(
+                rows_of(index), width, key_ref, value_ref, side_ref.at[0], do_s, kt_s, all_t,
+                dk_t, dv_t,
             )
 
             @pl.when((step == 4) & (index == 0))
@@ -1039,34 +1159,35 @@
                     reduce.add_y(1)
                     reduce.start_z(1)
 
-        @pl.loop(0, blocks)
-        def _(index):
-            rows = rows_of(index)
-            for_query, for_value = back_low(rows, width, dq_s, dk_s, dv_s, low_s)
-            for number, bits in enumerate(order):
-
-                @pl.when(step == 4 + number)
-                def _(bits=bits):
-                    late_s[0, pl.ds(partner(place, bits, 4), 1), :] += for_query
-                    late_s[0, pl.ds(4 + partner(place, bits, 4), 1), :] += for_value
+        all_t[width : 2 * width, :] = dk_t[...].astype(BF16)
+        all_t[2 * width :, :] = dv_t[...].astype(BF16)
+        for_all = dot_nt(jnp.ones((8, length), BF16), all_t[...])[:1]
+        for number, bits in enumerate(order):
+
+            @pl.when(step == 4 + number)
+            def _(bits=bits):
+                late_s[0, pl.ds(partner(place, bits, 4), 1), : 3 * width] = for_all
 
         for half, cols in enumerate(halves):
 
-            @pl.loop(0, model // (2 * share))
-            def _(z):
-                rows = pl.ds(pl.multiple_of(z * 2 * share, 2 * share), 2 * share)
-                slots = (0, 1) if half == 0 else (2, 3)
-                grads = back_weights(rows, width, slots, low_t, back_t, low_s, att_ref.at[0])
-                for y in range(2):
-                    piece = grads[y * share : (y + 1) * share]
-
-                    @pl.when(step < 6)
-                    def _(y=y, piece=piece):
-                        send_a[step - 4, z, y, :, cols] = piece
-
-                    @pl.when(step >= 6)
-                    def _(y=y, piece=piece):
-                        held_a[7 - step, z, y, :, cols] = piece
+            @pl.loop(0, model // (4 * share))
+            def _(pair):
+                rows = rows_of(pair, 4 * share)
+                if half == 0:
+                    grads = dot_nt(low_t[rows, :], all_t[: 2 * width, :])
+                else:
+                    for_value = dot_nt(low_t[rows, :], all_t[2 * width :, :])
+                    for_mixer = dot_nt(back_t[rows, :], att_ref[...])
+                    grads = jnp.concatenate([for_value, for_mixer], axis=1)
+                pieces = grads.astype(BF16).reshape(2, 2, share, model // 2)
+
+                @pl.when(step < 6)
+                def _(pieces=pieces):
+                    send_a[step - 4, pl.ds(2 * pair, 2), :, :, cols] = pieces
+
+                @pl.when(step >= 6)
+                def _(pieces=pieces):
+                    held_a[7 - step, pl.ds(2 * pair, 2), :, :, cols] = pieces
 
             for number, j in ((0, 1), (1, 0)):
 
@@ -1083,14 +1204,16 @@
         def _():
             hop(LATE_SUMS, late_s, late_r, 0).start()
 
-        @pl.loop(0, quarters)
-        def _(index):
-            rows = rows_of(index, part)
-            grad_s[rows, :] += back_tokens(rows, w_s, low_s)
+        @pl.loop(0, wides)
+        def _(index):
+            rows = rows_of(index, WIDE)
+            transposed = all_t[:, rows].T
+            grad_s[rows, :] += dot_nt(transposed, wia_ref[0, :, : 3 * width])
 
             @pl.when(step == 7)
             def _():
-                flow_s[index] = grad_s[rows, :].astype(BF16)
+                places = pl.ds(index * (WIDE // part), WIDE // part)
+                flow_s[places] = grad_s[rows, :].astype(BF16).reshape(WIDE // part, part, model)
 
     @pl.when(step == 7)
     def _():
@@ -1147,14 +1270,16 @@
     return [stepped(shape) if moves else resident(shape) for shape, moves in pairs]
 
 
-def near_forward(tokens, cotangent, shard_a, shard_i, shard_o, biases, augs, b_mixer, vectors):
+def near_forward(tokens, cotangent, shard_i, w_query, w_key, w_value, w_mixer, w_outer, docs, vectors):
     groups, part, model = tokens.shape
     length = groups * part
-    share = shard_a.shape[0]
+    share, width = w_query.shape
     whole = (groups, model // share, share, model)
-    attended = (groups, length, PAD)
+    sides = (groups, 2 * PAD, length)
     slopes = (groups, length, model)
     flat = (length, model)
+    shard = (share, model)
+    biases = (groups,) + vectors.shape
     anywhere = pl.BlockSpec(memory_space=pl.ANY)
 
     def early(shape):
@@ -1167,35 +1292,34 @@
             (1,) + shape[1:], lambda step: (jnp.maximum(step - 4, 0),) + (0,) * (len(shape) - 1)
         )
 
-    kept = [biases, *augs, b_mixer, vectors]
+    def vmem(*shape, kind=BF16):
+        return pltpu.VMEM(shape, kind)
+
+    kept = [w_query, w_key, w_value, w_mixer, w_outer, docs, vectors]
     return pl.pallas_call(
         forward_kernel,
         grid=(2 * groups,),
         out_shape=[
             jax.ShapeDtypeStruct((2 * groups, length, model), BF16),
-            jax.ShapeDtypeStruct(attended, BF16),
+            jax.ShapeDtypeStruct(sides, BF16),
             jax.ShapeDtypeStruct(slopes, BF16),
             jax.ShapeDtypeStruct(flat, F32),
             jax.ShapeDtypeStruct(flat, F32),
             jax.ShapeDtypeStruct(flat, BF16),
-            jax.ShapeDtypeStruct(tokens.shape, BF16),
+            jax.ShapeDtypeStruct((model, length), BF16),
             jax.ShapeDtypeStruct(tokens.shape, BF16),
             jax.ShapeDtypeStruct((2,) + whole, BF16),
             jax.ShapeDtypeStruct(whole, BF16),
         ],
-        in_specs=[anywhere] * 5 + [resident(each.shape) for each in kept],
-        out_specs=[stepped((2 * groups, length, model)), early(attended), late(slopes)]
+        in_specs=[anywhere] * 3 + [resident(each.shape) for each in kept],
+        out_specs=[stepped((2 * groups, length, model)), early(sides), late(slopes)]
         + [anywhere] * 7,
         scratch_shapes=[
-            pltpu.VMEM((4, model, PAD), BF16),
-            pltpu.VMEM(tokens.shape, BF16),
-            pltpu.VMEM(whole, BF16),
-            pltpu.VMEM(whole, BF16),
-            pltpu.VMEM(whole, BF16),
-            pltpu.VMEM((groups,) + biases.shape, F32),
-            pltpu.VMEM(flat, F32),
-            pltpu.VMEM(flat, F32),
-            pltpu.VMEM(flat, BF16),
+            vmem(*shard), vmem(*shard), vmem(model, 3 * PAD), vmem(model, PAD),
+            vmem(*tokens.shape), vmem(model, length), vmem(*whole), vmem(*whole), vmem(*whole),
+            vmem(*biases, kind=F32), vmem(length, PAD // 2), vmem(SEG, length),
+            vmem(width // HEAD, HEAD + SEG, length), vmem(length, PAD),
+            vmem(*flat, kind=F32), vmem(*flat, kind=F32), vmem(*flat),
             pltpu.SemaphoreType.DMA((FORWARD_WIRES,)),
             pltpu.SemaphoreType.DMA((FORWARD_WIRES,)),
             pltpu.SemaphoreType.DMA((13,)),
@@ -1204,7 +1328,7 @@
             vmem_limit_bytes=VMEM_LIMIT, collective_id=0, has_side_effects=True
         ),
         name="near_forward",
-    )(tokens, cotangent, shard_a, shard_i, shard_o, *kept)
+    )(tokens, cotangent, shard_i, *kept)
 
 
 def attend_plain(x, a_all, biases, qaug, kaug, vaug, b_mixer):
@@ -1310,10 +1434,11 @@
     )(x, a_all, d_mixed, d_first, q, k, v, attended)
 
 
-def near_backward(acts, attended, slopes, w_ia, w_o, vectors, second, first, low, x, cotangent):
-    quarters, part, model = x.shape
+def near_backward(acts, sides, slopes, w_ia, w_o, vectors, second, first, low, xt, cotangent):
+    quarters, part, model = cotangent.shape
     length = quarters * part
     share = model // 8
+    width = model // 4
     block = (4, 2, share, model)
     anywhere = pl.BlockSpec(memory_space=pl.ANY)
 
@@ -1339,28 +1464,28 @@
 
     final = [
         ((share, model), F32), ((share, model), F32), ((share, model), F32), ((16, model), F32),
-        ((8, PAD), F32),
+        ((8, model), F32),
     ]
     return pl.pallas_call(
         backward_kernel,
         grid=(8,),
-        out_shape=[jax.ShapeDtypeStruct(x.shape, BF16)] * 2
+        out_shape=[jax.ShapeDtypeStruct(cotangent.shape, BF16)] * 2
         + [jax.ShapeDtypeStruct(*each) for each in final],
         in_specs=[
-            ordered(acts.shape, acts_at), ordered(attended.shape, last_half),
+            ordered(acts.shape, acts_at), ordered(sides.shape, last_half),
             ordered(slopes.shape, first_half), ordered(w_ia.shape, weights_at),
             ordered(w_o.shape, first_half), resident(vectors.shape),
         ]
         + [anywhere] * 5,
         out_specs=[anywhere] * 2 + [resident(each[0]) for each in final],
         scratch_shapes=[
-            vmem(model, length), vmem(model, length), vmem(length, model), vmem(length, 3 * PAD),
-            vmem(*x.shape), vmem(*x.shape), vmem(length, model, kind=F32),
+            vmem(model, length), vmem(model, length), vmem(length, model), vmem(length, model),
+            vmem(*cotangent.shape), vmem(*cotangent.shape), vmem(length, model, kind=F32),
             vmem(2, ROWS, model, kind=F32),
-            vmem(4, model, PAD), vmem(PAD, length), vmem(PAD, length, kind=F32),
-            vmem(length, PAD, kind=F32), vmem(length, PAD, kind=F32),
-            vmem(6, 16, model, kind=F32), vmem(6, 8, PAD, kind=F32),
-            vmem(5, 16, model, kind=F32), vmem(5, 8, PAD, kind=F32),
+            vmem(width, model), vmem(PAD, length), vmem(width, length), vmem(3 * width, length),
+            vmem(width, length, kind=F32), vmem(width, length, kind=F32),
+            vmem(6, 16, model, kind=F32), vmem(6, 8, model, kind=F32),
+            vmem(5, 16, model, kind=F32), vmem(5, 8, model, kind=F32),
             vmem(2, *block), vmem(2, *block), vmem(2, *block), vmem(2, 4, share, model),
             vmem(2, 3, share, model), vmem(share, model),
             vmem(2, *block), vmem(2, *block), vmem(2, *block), vmem(1, 4, share, model),
@@ -1375,7 +1500,7 @@
             vmem_limit_bytes=VMEM_LIMIT, collective_id=1, has_side_effects=True
         ),
         name="near_backward",
-    )(acts, attended, slopes, w_ia, w_o, vectors, second, first, low, x, cotangent)
+    )(acts, sides, slopes, w_ia, w_o, vectors, second, first, low, xt, cotangent)
 
 
 def augment(labels, width):
@@ -1401,26 +1526,27 @@
     hidden = w_inner.shape[1]
     length = doc_ids.shape[2]
     model = tokens.shape[3]
-    near = groups == 4 and rings == 8
-
-    labels = lax.dynamic_index_in_dim(doc_ids[:, 0], place, 0, keepdims=False)
-    qaug, kaug, vaug = augment(labels, width)
-    shard_a = jnp.concatenate([w_query, w_key, w_value, w_mixer.T], axis=1)
-    shard_o = w_outer.T
-    spare = jnp.zeros((PAD - width,), F32)
-    biases = jnp.concatenate([b_query, spare, b_value, spare, b_inner])[None]
-    vectors = jnp.stack([gain_one, bias_one, b_outer, gain_two, bias_two] + [b_outer] * 3)
+    near = groups == 4 and rings == 8 and hidden == model and 4 * width == model
+
     if near:
-        acts, attended, slopes, first, second, low, x, cot, w_ia, w_o = near_forward(
-            tokens[:, 0], cotangent[:, 0], shard_a, w_inner, shard_o, biases, (qaug, kaug, vaug),
-            b_mixer[None], vectors,
+        spare = jnp.zeros((PAD - width,), F32)
+        vectors = jnp.concatenate(
+            [
+                b_mixer, gain_one, bias_one, b_outer, gain_two, bias_two, b_inner,
+                b_query, spare, b_value, spare, jnp.zeros((PAD,), F32),
+            ]
+        ).reshape(8, model)
+        acts, sides, slopes, first, second, low, xt, cot, w_ia, w_o = near_forward(
+            tokens[:, 0], cotangent[:, 0], w_inner, w_query, w_key, w_value, w_mixer, w_outer,
+            doc_ids, vectors,
         )
         out, d_tokens, ga, gi, go, tail, late = near_backward(
-            acts, attended, slopes, w_ia.reshape(2 * groups, model, model),
-            w_o.reshape(groups, model, model), vectors, second, first, low, x, cot,
+            acts, sides, slopes, w_ia.reshape(2 * groups, model, model),
+            w_o.reshape(groups, model, model), vectors, second, first, low, xt, cot,
         )
         own = lambda whole, start: lax.dynamic_index_in_dim(whole, start + place, 0, False)
-        dbq, dbv = own(late, 0)[:width], own(late, groups)[:width]
+        mine = own(late, 0)
+        dbq, dbv = mine[:width], mine[2 * width : 3 * width]
         dbi = own(tail, 0)
         tail = tail[2 * groups :]
         out, d_tokens = out[:, None], d_tokens[:, None].astype(F32)
@@ -1441,6 +1567,13 @@
             total = lax.psum_scatter(flat, ("tensor", "dp"), scatter_dimension=0, tiled=True)
             return total.astype(F32)
 
+        labels = lax.dynamic_index_in_dim(doc_ids[:, 0], place, 0, keepdims=False)
+        qaug, kaug, vaug = augment(labels, width)
+        shard_a = jnp.concatenate([w_query, w_key, w_value, w_mixer.T], axis=1)
+        shard_o = w_outer.T
+        spare = jnp.zeros((PAD - width,), F32)
+        biases = jnp.concatenate([b_query, spare, b_value, spare, b_inner])[None]
+        vectors = jnp.stack([gain_one, bias_one, b_outer, gain_two, bias_two] + [b_outer] * 3)
         x, cot = to_sequence(tokens), to_sequence(cotangent)
         a_all, wi, wo = gather(shard_a), gather(w_inner), gather(shard_o)
         every = lax.all_gather(biases, "tensor", axis=0)

time: 312 us -> 287 us (0.920)
  Pallas kernels: 286 us -> 270 us
  local copies, waits for them, and re-layouts: 15.9 us -> 10.4 us
  other arithmetic: 7.78 us -> 3.47 us
    pallas_call x1, Pallas kernels: 183 us -> 165 us  [near_backward(): pl.pallas_call(backward_kernel, grid=(8,), out_shape=[jax.ShapeDtypeStruc...]
    another operation x6 -> x0, local copies, waits for them, and re-layouts: 4.09 us -> none  [body(): jnp.stack([gain_one, bias_one, b_outer, gain_two, bias_two] + [b_outer] * 3)]
where the time goes in v5:
time: 287 us; the launch traced here: 284 us
  Pallas kernels  270 us (94%)
  local copies, waits for them, and re-layouts  10.4 us (4%)
  other arithmetic  3.47 us (1%)
    pallas_call x1, Pallas kernels, near_backward(): pl.pallas_call(backward_kernel, grid=(8,), out_shape=[jax.ShapeDtypeStruc...  165 us
    pallas_call x1, Pallas kernels, near_forward(): pl.pallas_call(forward_kernel, grid=(2 * groups,), out_shape=[jax.ShapeDt...  105 us

profile of v5, /device:TPU:0, one launch (start us, length us, event | category | flops | bytes accessed | tf_op | source)
XLA Modules:
  0.0 284.3 jit_solution(11696467486558757846)
XLA Ops:
  0.7 0.9 concatenate.3
  1.6 0.6 reshape.47.vec_ref
  2.2 1.7 copy.35.wo_ref
  3.9 104.6 %near_forward.1 = (bf16[8,1024,768]{2,1,0:T(8,128)(2,1)}, bf16[4,512,1024]{2,1,0:T(8,128)(2,1)}, bf16[4,1024,768]{2,1,0:T(8,128)(2,1)}, f32[1024,768]{1,0:T(8,12...) custom-call(bf16[4,256,768]{2,1,0:T(8,128)(2,1)} %bitcast.20, ...), custom_call_target="tpu_custom_call" | custom-call | tf_op jit(solution)/shard_map/near_forward/pallas_call | solution.py:1299
  108.5 165.1 %near_backward.1 = (bf16[4,256,768]{2,1,0:T(8,128)(2,1)}, bf16[4,256,768]{2,1,0:T(8,128)(2,1)}, f32[96,768]{1,0:T(8,128)}, f32[96,768]{1,0:T(8,128)}, f32[96,768...) custom-call(bf16[8,1024,768]{2,1,0:T(8,128)(2,1)} %get-tuple-element.34.acts_ref, ...), custom_call_target="tpu_custom_call" | custom-call | tf_op jit(solution)/shard_map/near_backward/pallas_call | solution.py:1469
  273.6 0.0 copy-start.1
  273.6 0.0 copy-start
  273.6 3.5 %bitcast_convert_fusion = f32[4,1,256,768]{3,2,1,0:T(8,128)} fusion(bf16[4,256,768]{2,1,0:T(8,128)(2,1)} %get-tuple-element.45), kind=kLoop, calls=%fused_computation | loop fusion | flops 786432 | bytes 4718592
  277.1 0.0 copy-start.3
  277.1 0.0 copy-start.2
  277.1 0.0 copy-done.1
  277.1 0.8 slice_bitcast_fusion
  277.9 0.7 copy.38
  278.6 1.7 slice_reduce_fusion
  280.4 1.4 fusion
  281.7 0.0 copy-done
  281.7 1.1 copy.42
  282.9 0.0 copy-done.3
  282.9 0.7 copy.43
  283.6 0.0 copy-done.2
  283.6 0.7 copy.44
  (2 shorter events, 0.0 us)
Async XLA Ops:
  273.6 3.5 %copy-start.1 = (f32[96,768]{1,0:T(8,128)S(1)}, f32[96,768]{1,0:T(8,128)}, u32[]{:S(2)}) copy-start(f32[96,768]{1,0:T(8,128)} %get-tuple-element.46) | copy-start | bytes 884740
  273.6 8.1 %copy-start = (bf16[4,256,768]{2,1,0:T(8,128)(2,1)S(1)}, bf16[4,256,768]{2,1,0:T(8,128)(2,1)}, u32[]{:S(2)}) copy-start(bf16[4,256,768]{2,1,0:T(8,128)(2,1)} %get-tuple-element.44) | copy-start | bytes 4718596
  277.1 5.8 %copy-start.3 = (f32[96,768]{1,0:T(8,128)S(1)}, f32[96,768]{1,0:T(8,128)}, u32[]{:S(2)}) copy-start(f32[96,768]{1,0:T(8,128)} %get-tuple-element.109) | copy-start | bytes 884740
  277.1 6.5 %copy-start.2 = (f32[96,768]{1,0:T(8,128)S(1)}, f32[96,768]{1,0:T(8,128)}, u32[]{:S(2)}) copy-start(f32[96,768]{1,0:T(8,128)} %get-tuple-element.50) | copy-start | bytes 884740

commit v6 on v5

--- a/solution.py
+++ b/solution.py
@@ -158,78 +158,113 @@
 
 PEERS = ((1, 0), (2, 0), (3, 0), (0, 1), (0, 2), (0, 4), (0, 6))
 TOKENS, COTS, BIASES, KIND_A = 0, 3, 6, 9
-KIND_I = KIND_A + 17
-KIND_O = KIND_I + 17
-FORWARD_WIRES = KIND_O + 10
+SHARD_WIRES, BLOCK_WIRES = 19, 11
+KIND_I = KIND_A + SHARD_WIRES
+KIND_O = KIND_I + SHARD_WIRES
+FORWARD_WIRES = KIND_O + BLOCK_WIRES
 
 
 class ShardGather:
     def __init__(self, wires, base, shard, whole):
         self.wires, self.base, self.shard, self.whole = wires, base, shard, whole
+        z = lax.div(wires.row, 2)
+        self.middle = (z == 1) | (z == 2)
 
     def at(self, slot, dp_bits):
         return self.whole.at[slot, partner(self.wires.row, dp_bits, 8)]
 
+    def own(self, slot):
+        return self.shard if slot == 0 else self.at(slot, 0)
+
     def cross_x(self):
         return self.wires.copy(self.base, self.shard, self.at(2, 0), 2, 0)
 
-    def along_z(self, slot, step, mine):
-        source = self.shard if slot == 0 else self.at(slot, 0)
+    def along_z(self, slot, step):
         number = self.base + 1 + 3 * (slot // 2) + step - 1
-        target = self.at(slot, 0) if mine else self.at(slot, 2 * step)
-        return self.wires.copy(number, source, target, 0, 2 * step)
-
-    def along_y(self, slot, step, mine):
-        source = self.shard if slot == 0 and step == 0 else self.at(slot, 2 * step)
+        return self.wires.copy(number, self.own(slot), self.at(slot, 0), 0, 2 * step)
+
+    def hand_on(self, slot):
+        number = self.base + 17 + slot // 2
+        return self.wires.copy(number, self.at(slot, 4), self.at(slot, 4), 0, 2)
+
+    def along_y(self, slot, step):
+        source = self.own(slot) if step == 0 else self.at(slot, 2 * step)
         number = self.base + 7 + 4 * (slot // 2) + step
-        target = self.at(slot, 2 * step) if mine else self.at(slot, 2 * step + 1)
-        return self.wires.copy(number, source, target, 0, 1)
-
-    def to_core(self, slot, mine):
+        return self.wires.copy(number, source, self.at(slot, 2 * step), 0, 1)
+
+    def to_core(self, slot):
         number = self.base + 15 + slot // 2
-        target = self.whole.at[slot + 1]
-        return self.wires.copy(number, self.whole.at[slot], target, 1, 0)
-
-    def start_z(self, slot):
-        for step in (1, 2, 3):
-            self.along_z(slot, step, True).start()
-
-    def wait_z(self, slot):
-        for step in (1, 2, 3):
-            self.along_z(slot, step, False).wait_recv()
-
-    def pass_y(self, slot):
-        for step in (1, 2, 3):
-            self.along_y(slot, step, True).start()
+        return self.wires.copy(number, self.whole.at[slot], self.whole.at[slot + 1], 1, 0)
+
+    def start(self, slot):
+        self.along_z(slot, 1).start()
+        self.along_z(slot, 2).start()
+
+        @pl.when(self.middle)
+        def _():
+            self.along_z(slot, 3).start()
+
+        self.along_y(slot, 0).start()
+
+    def advance(self, slot):
+        self.along_z(slot, 2).wait_recv()
+
+        @pl.when(self.middle)
+        def _():
+            self.hand_on(slot).start()
+
+        self.along_y(slot, 2).start()
+        self.along_z(slot, 1).wait_recv()
+        self.along_y(slot, 1).start()
+
+        @pl.when(self.middle)
+        def _():
+            self.along_z(slot, 3).wait_recv()
+
+        @pl.when(jnp.logical_not(self.middle))
+        def _():
+            self.hand_on(slot).wait_recv()
+
+        self.along_y(slot, 3).start()
 
     def wait_y(self, slot):
         for step in range(4):
-            self.along_y(slot, step, False).wait_recv()
-
-    def wait_sent(self, x_first=True):
-        for slot in (0, 2) if x_first else (0,):
-            for step in (1, 2, 3):
-                self.along_z(slot, step, True).wait_send()
+            self.along_y(slot, step).wait_recv()
+
+    def wait_sent(self, slots):
+        self.cross_x().wait_send()
+        for slot in slots:
+            for step in (1, 2):
+                self.along_z(slot, step).wait_send()
+
+            @pl.when(self.middle)
+            def _(slot=slot):
+                self.along_z(slot, 3).wait_send()
+                self.hand_on(slot).wait_send()
+
             for step in range(4):
-                self.along_y(slot, step, True).wait_send()
+                self.along_y(slot, step).wait_send()
         for slot in (0, 2):
-            self.to_core(slot, True).wait_send()
+            self.to_core(slot).wait_send()
 
 
 class BlockGather(ShardGather):
-    def along_z(self, slot, step, mine):
-        target = self.at(0, 0) if mine else self.at(0, 2 * step)
-        return self.wires.copy(self.base + step - 1, self.shard, target, 0, 2 * step)
-
-    def along_y(self, slot, step, mine):
-        source = self.shard if step == 0 else self.at(0, 2 * step)
-        target = self.at(0, 2 * step) if mine else self.at(0, 2 * step + 1)
-        return self.wires.copy(self.base + 3 + step, source, target, 0, 1)
+    def along_z(self, slot, step):
+        return self.wires.copy(
+            self.base + step - 1, self.shard, self.at(0, 0), 0, 2 * step
+        )
+
+    def hand_on(self, slot):
+        return self.wires.copy(self.base + 10, self.at(0, 4), self.at(0, 4), 0, 2)
+
+    def along_y(self, slot, step):
+        source = self.own(0) if step == 0 else self.at(0, 2 * step)
+        return self.wires.copy(self.base + 3 + step, source, self.at(0, 2 * step), 0, 1)
 
     def cross_x(self):
         return self.wires.copy(self.base + 7, self.whole.at[0], self.whole.at[2], 2, 0)
 
-    def to_core(self, slot, mine):
+    def to_core(self, slot):
         return self.wires.copy(
             self.base + 8 + slot // 2, self.whole.at[slot], self.whole.at[slot + 1], 1, 0
         )
@@ -287,35 +322,53 @@
 
 
 def attend_block(cols, width, key_ref, vt_s, side_ref):
-    outs = []
-    for head in range(width // HEAD):
-        docs = side_ref[extra_rows(head, width), cols]
+    heads = range(width // HEAD)
+    docs = side_ref[extra_rows(0, width), cols]
+
+    def score(head):
         queries = place_head(side_ref[head_rows(head), cols], docs, head, width)
-        scores = dot_nn(key_ref[...], queries)
-        highest = jnp.max(scores, axis=0, keepdims=True)
-        raw = jnp.exp2((scores - highest) * LOG2E).astype(BF16)
-        mixed = dot_nn(vt_s[head], raw)
-        total = mixed[HEAD : HEAD + 1]
-        outs.append((mixed[:HEAD] / total).astype(BF16))
-        logs = -(highest + jnp.log(total))
+        return dot_nn(key_ref[...], queries)
+
+    scores, highest, mixed = [score(0)], [], []
+    for head in heads:
+        if head + 1 < len(heads):
+            scores.append(score(head + 1))
+        highest.append(jnp.max(scores[head], axis=0, keepdims=True))
+        raw = jnp.exp2((scores[head] - highest[head]) * LOG2E).astype(BF16)
+        mixed.append(dot_nn(vt_s[head], raw))
+    for head in heads:
+        logs = -(highest[head] + jnp.log(mixed[head][HEAD : HEAD + 1]))
         side_ref[extra_rows(head, width), cols] = parts_rows(logs, docs[:DOCS])
+    outs = [(each[:HEAD] / each[HEAD : HEAD + 1]).astype(BF16) for each in mixed]
     return jnp.concatenate(outs, axis=0)
 
 
 def attend_block_back(cols, width, key_ref, value_ref, side_ref, do_s, kt_s, all_t, dk_t, dv_t):
-    for head in range(width // HEAD):
+    heads = range(width // HEAD)
+
+    def products(head):
         queries = side_ref[head_rows(head), cols]
         d_att = do_s[head_rows(head), cols]
         extra = extra_rows(head, width)
-        chances = jnp.exp2(
-            dot_nn(key_ref[...], place_head(queries, side_ref[extra, cols], head, width)) * LOG2E
-        )
+        scores = dot_nn(key_ref[...], place_head(queries, side_ref[extra, cols], head, width))
         d_chances = dot_nn(value_ref[...], place_head(d_att, do_s[extra, cols], head, width))
+        return queries, d_att, scores, d_chances
+
+    ahead = products(0)
+    d_queries, d_keys, d_values = [], [], []
+    for head in heads:
+        queries, d_att, scores, d_chances = ahead
+        if head + 1 < len(heads):
+            ahead = products(head + 1)
+        chances = jnp.exp2(scores * LOG2E)
         d_scores = (chances * d_chances).astype(BF16)
-        d_query = dot_nn(kt_s[head_rows(head), :], d_scores) * HEAD**-0.5
-        all_t[head_rows(head), cols] = d_query.astype(BF16)
-        dk_t[head_rows(head), :] += dot_nt(queries, d_scores)
-        dv_t[head_rows(head), :] += dot_nt(d_att, chances.astype(BF16))
+        d_queries.append(dot_nn(kt_s[head_rows(head), :], d_scores) * HEAD**-0.5)
+        d_keys.append(dot_nt(queries, d_scores))
+        d_values.append(dot_nt(d_att, chances.astype(BF16)))
+    for head in heads:
+        all_t[head_rows(head), cols] = d_queries[head].astype(BF16)
+        dk_t[head_rows(head), :] += d_keys[head]
+        dv_t[head_rows(head), :] += d_values[head]
 
 
 def forward_kernel(
@@ -375,8 +428,7 @@
         attn.cross_x().start()
         for bits in (1, 2, 3):
             bias_copy(bits, True).start()
-        attn.start_z(0)
-        attn.along_y(0, 0, True).start()
+        attn.start(0)
         for bits in (2, 3, 1):
             exchange(TOKENS, tok_ref, x_s, bits, True).start()
         so_s[...] = wo_ref[...].T
@@ -400,12 +452,10 @@
         for copy in local:
             copy.wait()
         attn.cross_x().wait_recv()
-        attn.start_z(2)
-        attn.along_y(2, 0, True).start()
-        attn.wait_z(0)
-        attn.pass_y(0)
+        attn.start(2)
+        attn.advance(0)
         attn.wait_y(0)
-        attn.to_core(0, True).start()
+        attn.to_core(0).start()
         inner.cross_x().start()
         for bits in (1, 2, 3):
             exchange(TOKENS, tok_ref, x_s, bits, False).wait_recv()
@@ -426,16 +476,16 @@
 
     @pl.when(step == 1)
     def _():
-        attn.to_core(0, False).wait_recv()
+        attn.to_core(0).wait_recv()
 
     @pl.when(step == 2)
     def _():
         attn.wait_y(2)
-        attn.to_core(2, True).start()
+        attn.to_core(2).start()
 
     @pl.when(step == 3)
     def _():
-        attn.to_core(2, False).wait_recv()
+        attn.to_core(2).wait_recv()
         keep_a.start()
 
     @pl.when(step < 4)
@@ -490,52 +540,37 @@
 
             @pl.when((step == 0) & (index == 0))
             def _():
-                outer.start_z(0)
-                outer.along_y(0, 0, True).start()
+                outer.start(0)
                 for bits in (2, 3, 1):
                     exchange(COTS, cot_ref, cot_out, bits, True).start()
 
             @pl.when((step == 0) & (index == 1))
             def _():
-                attn.wait_z(2)
-                attn.pass_y(2)
+                attn.advance(2)
 
             @pl.when((step == 0) & (index == 3))
             def _():
-                inner.start_z(0)
-                inner.along_y(0, 0, True).start()
-
-            @pl.when((step == 1) & (index == 1))
-            def _():
-                outer.wait_z(0)
-                outer.pass_y(0)
+                inner.cross_x().wait_recv()
+                inner.start(0)
 
             @pl.when((step == 1) & (index == 2))
             def _():
-                inner.cross_x().wait_recv()
-                inner.start_z(2)
-                inner.along_y(2, 0, True).start()
-
-            @pl.when((step == 2) & (index == 2))
+                outer.advance(0)
+                inner.start(2)
+
+            @pl.when((step == 2) & (index == 3))
             def _():
-                inner.wait_z(0)
-                inner.pass_y(0)
-
-            @pl.when((step == 2) & (index == 3))
+                inner.advance(0)
+
+            @pl.when((step == 3) & (index == 0))
             def _():
                 outer.wait_y(0)
                 outer.cross_x().start()
-                outer.to_core(0, True).start()
-
-            @pl.when((step == 3) & (index == 1))
-            def _():
-                inner.wait_y(0)
-                inner.to_core(0, True).start()
+                outer.to_core(0).start()
 
             @pl.when((step == 3) & (index == 3))
             def _():
-                inner.wait_z(2)
-                inner.pass_y(2)
+                inner.advance(2)
 
         @pl.loop(0, wides)
         def _(index):
@@ -555,23 +590,25 @@
             second_s[rows, :] = normed + b_outer
 
         keep_low.start()
+        inner.wait_y(0)
+        inner.to_core(0).start()
 
     @pl.when(step == 5)
     def _():
-        inner.to_core(0, False).wait_recv()
-        outer.to_core(0, False).wait_recv()
+        inner.to_core(0).wait_recv()
+        outer.to_core(0).wait_recv()
 
     @pl.when(step == 6)
     def _():
         inner.wait_y(2)
-        inner.to_core(2, True).start()
+        inner.to_core(2).start()
         outer.cross_x().wait_recv()
-        outer.to_core(2, True).start()
+        outer.to_core(2).start()
 
     @pl.when(step == 7)
     def _():
-        inner.to_core(2, False).wait_recv()
-        outer.to_core(2, False).wait_recv()
+        inner.to_core(2).wait_recv()
+        outer.to_core(2).wait_recv()
         keep_i.start()
         keep_o.start()
 
@@ -596,9 +633,9 @@
         keep_second.start()
         for bits in (1, 2, 3):
             exchange(COTS, cot_ref, cot_out, bits, False).wait_recv()
-        for gather in (attn, inner, outer):
-            gather.cross_x().wait_send()
-            gather.wait_sent(gather is not outer)
+        attn.wait_sent((0, 2))
+        inner.wait_sent((0, 2))
+        outer.wait_sent((0,))
         for bits in (1, 2, 3):
             exchange(TOKENS, tok_ref, x_s, bits, True).wait_send()
             exchange(COTS, cot_ref, cot_out, bits, True).wait_send()
@@ -896,12 +933,12 @@
                 self.z_copy(j, step).wait_send()
 
 
-OUTPUTS, TOKEN_GRADS, SUMS, LATE_SUMS = 0, 3, 6, 11
-RED_I = 16
+OUTPUTS, TOKEN_GRADS, SUMS, LATE_SUMS = 0, 3, 6, 16
+RED_I = 26
 RED_O = RED_I + Reduce.COUNT
 RED_A = RED_O + Reduce.COUNT
 BACKWARD_WIRES = RED_A + 2 * Reduce.COUNT
-HOPS = ((1, 0), (2, 0), (0, 1), (0, 2), (0, 4))
+BACK_PEERS = PEERS + ((0, 3), (0, 5), (0, 7))
 
 
 def slot_at(step):
@@ -913,7 +950,7 @@
     cot_ref,
     out_res, dtok_res, ga_res, gi_res, go_res, sum_res, late_res,
     low_t, back_t, dmix_s, low_s, flow_s, out_s, grad_s, first_s, wmt_s, do_s, kt_s, all_t, dk_t,
-    dv_t, sums_s, late_s, sums_r, late_r,
+    dv_t, sums_s, sums_o, sums_d, late_o, late_t, late_d,
     send_i, held_i, core_i, y_i, z_i, x_i, send_o, held_o, core_o, y_o, z_o, x_o,
     held_a, core_a, y_a, z_a, x_a,
     send_sem, recv_sem, here_sem,
@@ -947,15 +984,21 @@
             base + bits - 1, source.at[other], target.at[place if mine else other], bits, 0
         )
 
-    def hop(base, kept, got, number):
-        bits = HOPS[number]
-        return wires.copy(base + number, kept.at[number], got.at[number], *bits)
-
-    def next_hop(base, kept, got, number):
-        hop(base, kept, got, number).wait_recv()
-        kept[number + 1] = kept[number] + got[number]
-        if number + 1 < len(HOPS):
-            hop(base, kept, got, number + 1).start()
+    def by_tensor(bits):
+        return wires.copy(
+            SUMS + bits - 1, sums_s.at[place], sums_s.at[place], bits, 0
+        )
+
+    def by_rows(base, kept, bits):
+        return wires.copy(base + 2 + bits, kept.at[row], kept.at[row], 0, bits)
+
+    def late_copy(bits):
+        return wires.copy(LATE_SUMS + bits - 1, late_o.at[bits], late_t.at[bits], bits, 0)
+
+    def sum_rows(base, kept):
+        for bits in range(1, 8):
+            by_rows(base, kept, bits).wait_recv()
+        return sum((kept[number] for number in range(1, 8)), kept[0])
 
     load_second = pltpu.make_async_copy(second_ref, grad_s, here_sem.at[0])
     load_cot = pltpu.make_async_copy(cot_ref, flow_s, here_sem.at[1])
@@ -976,9 +1019,10 @@
         load_second.start()
         load_cot.start()
         load_low.start()
-        sums_s[0] = jnp.zeros_like(sums_s[0])
-        late_s[0] = jnp.zeros_like(late_s[0])
-        greet(wires, PEERS)
+        sums_s[place] = jnp.zeros_like(sums_s[0])
+        for bits in range(4):
+            late_o[bits] = jnp.zeros_like(late_o[0])
+        greet(wires, BACK_PEERS)
         load_second.wait()
         load_cot.wait()
         load_low.wait()
@@ -991,9 +1035,9 @@
             out_s[index] = (unit * gain_two + bias_two).astype(BF16)
             grads = flow_s[index].astype(F32)
             d_second = norm_back(grads, gain_two, unit, inverse)
-            sums_s[0, 8:9, :] += column_sum(d_second)
-            sums_s[0, 9:10, :] += column_sum(grads * unit)
-            sums_s[0, 10:11, :] += column_sum(grads)
+            sums_s[place, 8:9, :] += column_sum(d_second)
+            sums_s[place, 9:10, :] += column_sum(grads * unit)
+            sums_s[place, 10:11, :] += column_sum(grads)
             grad_s[rows, :] = d_second
             lower = d_second.astype(BF16)
             dmix_s[rows, :] = lower
@@ -1016,7 +1060,7 @@
 
                 @pl.when(step == number)
                 def _(bits=bits):
-                    sums_s[0, pl.ds(partner(place, bits, 4), 1), :] += for_inner
+                    sums_s[place, pl.ds(partner(place, bits, 4), 1), :] += for_inner
 
             grad_s[rows, :] += dot_nt(d_inner, wia_ref[0])
 
@@ -1067,15 +1111,16 @@
                 load_first(index + 2).start()
             grads = grad_s[rows, :]
             d_first = norm_back(grads, gain_one, unit, inverse)
-            sums_s[0, 11:12, :] += column_sum(d_first)
-            sums_s[0, 12:13, :] += column_sum(grads * unit)
-            sums_s[0, 13:14, :] += column_sum(grads)
+            sums_s[place, 11:12, :] += column_sum(d_first)
+            sums_s[place, 12:13, :] += column_sum(grads * unit)
+            sums_s[place, 13:14, :] += column_sum(grads)
             grad_s[rows, :] = d_first
             lower = d_first.astype(BF16)
             dmix_s[rows, :] = lower
             back_t[:, rows] = lower.T
         load_x.wait()
-        hop(SUMS, sums_s, sums_r, 0).start()
+        for bits in (1, 2, 3):
+            by_tensor(bits).start()
 
     @pl.when(step == 4)
     def _():
@@ -1115,30 +1160,31 @@
 
             @pl.when((step == 4) & (index == 0))
             def _():
-                next_hop(SUMS, sums_s, sums_r, 0)
                 inner.add_y(1)
                 inner.start_z(1)
 
-            @pl.when((step == 4) & (index == 1))
-            def _():
-                next_hop(SUMS, sums_s, sums_r, 1)
-
             @pl.when((step == 4) & (index == 3))
             def _():
-                next_hop(SUMS, sums_s, sums_r, 2)
                 inner.add_y(0)
                 inner.start_z(0)
                 outer.add_whole_x()
                 outer.y_copy(0).start()
 
-            @pl.when((step == 5) & (index == 0))
-            def _():
-                next_hop(SUMS, sums_s, sums_r, 3)
-
             @pl.when((step == 5) & (index == 1))
             def _():
-                next_hop(SUMS, sums_s, sums_r, 4)
                 inner.send_x()
+                for bits in (1, 2, 3):
+                    by_tensor(bits).wait_recv()
+                sums_o[...] = sums_s[0] + sums_s[1] + sums_s[2] + sums_s[3]
+                sums_d[row, :6, :] = sums_o[8:14, :]
+                sums_d[row, 6:7, :] = sums_o[pl.ds(place, 1), :]
+                sums_d[row, 7:, :] = jnp.zeros((1, model), F32)
+                for bits in range(1, 8):
+                    by_rows(SUMS, sums_d, bits).start()
+
+            @pl.when((step == 7) & (index == 1))
+            def _():
+                sum_res[...] = sum_rows(SUMS, sums_d)
 
             @pl.when((step == 5) & (index == 3))
             def _():
@@ -1161,12 +1207,20 @@
 
         all_t[width : 2 * width, :] = dk_t[...].astype(BF16)
         all_t[2 * width :, :] = dv_t[...].astype(BF16)
-        for_all = dot_nt(jnp.ones((8, length), BF16), all_t[...])[:1]
+        for_all = dot_nt(jnp.ones((8, length), BF16), all_t[...])
         for number, bits in enumerate(order):
 
             @pl.when(step == 4 + number)
             def _(bits=bits):
-                late_s[0, pl.ds(partner(place, bits, 4), 1), : 3 * width] = for_all
+                late_o[bits, :, : 3 * width] = for_all
+                if bits:
+                    late_copy(bits).start()
+                    return
+                for other in (1, 2, 3):
+                    late_copy(other).wait_recv()
+                late_d[row] = late_o[0] + late_t[1] + late_t[2] + late_t[3]
+                for other in range(1, 8):
+                    by_rows(LATE_SUMS, late_d, other).start()
 
         for half, cols in enumerate(halves):
 
@@ -1200,10 +1254,6 @@
                 attn[half].add_core(0)
                 attn[half].y_copy(0).start()
 
-        @pl.when(step == 7)
-        def _():
-            hop(LATE_SUMS, late_s, late_r, 0).start()
-
         @pl.loop(0, wides)
         def _(index):
             rows = rows_of(index, WIDE)
@@ -1220,15 +1270,12 @@
         for bits in (2, 3, 1):
             exchange(TOKEN_GRADS, flow_s, dtok_res, bits, True).start()
         keep_dtok.start()
-        next_hop(LATE_SUMS, late_s, late_r, 0)
         for reduce in attn:
             reduce.send_x()
+        for reduce in attn:
             reduce.add_y(0)
             reduce.start_z(0)
-        for number in range(1, len(HOPS)):
-            next_hop(LATE_SUMS, late_s, late_r, number)
-        sum_res[...] = sums_s[5]
-        late_res[...] = late_s[5]
+        late_res[...] = sum_rows(LATE_SUMS, late_d)
         for reduce, cols in zip(attn, halves):
             ga_res[:, cols] = reduce.total()
         for bits in (1, 2, 3):
@@ -1239,9 +1286,12 @@
                 exchange(base, source, target, bits, True).wait_send()
         keep_out.wait()
         keep_dtok.wait()
-        for number in range(len(HOPS)):
-            hop(SUMS, sums_s, sums_r, number).wait_send()
-            hop(LATE_SUMS, late_s, late_r, number).wait_send()
+        for bits in (1, 2, 3):
+            by_tensor(bits).wait_send()
+            late_copy(bits).wait_send()
+        for bits in range(1, 8):
+            by_rows(SUMS, sums_d, bits).wait_send()
+            by_rows(LATE_SUMS, late_d, bits).wait_send()
         for number, j in ((0, 1), (1, 0)):
             outer.core_copy(j, send_o.at[number]).wait_send()
             for reduce in attn:
@@ -1463,7 +1513,7 @@
         return pltpu.VMEM(shape, kind)
 
     final = [
-        ((share, model), F32), ((share, model), F32), ((share, model), F32), ((16, model), F32),
+        ((share, model), F32), ((share, model), F32), ((share, model), F32), ((8, model), F32),
         ((8, model), F32),
     ]
     return pl.pallas_call(
@@ -1484,8 +1534,8 @@
             vmem(2, ROWS, model, kind=F32),
             vmem(width, model), vmem(PAD, length), vmem(width, length), vmem(3 * width, length),
             vmem(width, length, kind=F32), vmem(width, length, kind=F32),
-            vmem(6, 16, model, kind=F32), vmem(6, 8, model, kind=F32),
-            vmem(5, 16, model, kind=F32), vmem(5, 8, model, kind=F32),
+            vmem(4, 16, model, kind=F32), vmem(16, model, kind=F32), vmem(8, 8, model, kind=F32),
+            vmem(4, 8, model, kind=F32), vmem(4, 8, model, kind=F32), vmem(8, 8, model, kind=F32),
             vmem(2, *block), vmem(2, *block), vmem(2, *block), vmem(2, 4, share, model),
             vmem(2, 3, share, model), vmem(share, model),
             vmem(2, *block), vmem(2, *block), vmem(2, *block), vmem(1, 4, share, model),
@@ -1544,11 +1594,8 @@
             acts, sides, slopes, w_ia.reshape(2 * groups, model, model),
             w_o.reshape(groups, model, model), vectors, second, first, low, xt, cot,
         )
-        own = lambda whole, start: lax.dynamic_index_in_dim(whole, start + place, 0, False)
-        mine = own(late, 0)
-        dbq, dbv = mine[:width], mine[2 * width : 3 * width]
-        dbi = own(tail, 0)
-        tail = tail[2 * groups :]
+        dbq, dbv = late[0, :width], late[0, 2 * width : 3 * width]
+        dbi = tail[6]
         out, d_tokens = out[:, None], d_tokens[:, None].astype(F32)
     else:
 

time: 287 us -> 268 us (0.934)
  Pallas kernels: 270 us -> 252 us
    pallas_call x1, Pallas kernels: 165 us -> 144 us  [near_backward(): pl.pallas_call(backward_kernel, grid=(8,), out_shape=[jax.ShapeDtypeStruc...]
    pallas_call x1, Pallas kernels: 105 us -> 108 us  [near_forward(): pl.pallas_call(forward_kernel, grid=(2 * groups,), out_shape=[jax.ShapeDt...]
where the time goes in v6:
time: 268 us; the launch traced here: 267 us
  Pallas kernels  252 us (94%)
  local copies, waits for them, and re-layouts  11.5 us (4%)
  other arithmetic  3.4 us (1%)
    pallas_call x1, Pallas kernels, near_backward(): pl.pallas_call(backward_kernel, grid=(8,), out_shape=[jax.ShapeDtypeStruc...  144 us
    pallas_call x1, Pallas kernels, near_forward(): pl.pallas_call(forward_kernel, grid=(2 * groups,), out_shape=[jax.ShapeDt...  108 us

profile of v6, /device:TPU:0, one launch (start us, length us, event | category | flops | bytes accessed | tf_op | source)
XLA Modules:
  0.0 267.2 jit_solution(8740984161917638549)
XLA Ops:
  0.7 0.9 concatenate.3
  1.6 0.6 reshape.45.vec_ref
  2.2 1.7 copy.35.wo_ref
  3.9 107.6 %near_forward.1 = (bf16[8,1024,768]{2,1,0:T(8,128)(2,1)}, bf16[4,512,1024]{2,1,0:T(8,128)(2,1)}, bf16[4,1024,768]{2,1,0:T(8,128)(2,1)}, f32[1024,768]{1,0:T(8,12...) custom-call(bf16[4,256,768]{2,1,0:T(8,128)(2,1)} %bitcast.20, ...), custom_call_target="tpu_custom_call" | custom-call | tf_op jit(solution)/shard_map/near_forward/pallas_call | solution.py:1349
  111.6 144.0 %near_backward.1 = (bf16[4,256,768]{2,1,0:T(8,128)(2,1)}, bf16[4,256,768]{2,1,0:T(8,128)(2,1)}, f32[96,768]{1,0:T(8,128)}, f32[96,768]{1,0:T(8,128)}, f32[96,768...) custom-call(bf16[8,1024,768]{2,1,0:T(8,128)(2,1)} %get-tuple-element.34.acts_ref, ...), custom_call_target="tpu_custom_call" | custom-call | tf_op jit(solution)/shard_map/near_backward/pallas_call | solution.py:1519
  255.6 0.0 copy-start
  255.6 1.4 fusion
  257.0 1.7 slice_reduce_fusion
  258.6 1.8 slice_bitcast_fusion
  260.5 0.7 copy.38
  261.2 0.0 copy-start.2
  261.2 0.0 copy-start.1
  261.2 3.4 %bitcast_convert_fusion = f32[4,1,256,768]{3,2,1,0:T(8,128)} fusion(bf16[4,256,768]{2,1,0:T(8,128)(2,1)} %get-tuple-element.45), kind=kLoop, calls=%fused_computation | loop fusion | flops 786432 | bytes 4718592
  264.6 0.0 copy-done
  264.6 1.1 copy.42
  265.8 0.0 copy-done.2
  265.8 0.7 copy.43
  266.5 0.0 copy-done.1
  266.5 0.7 copy.44
  (2 shorter events, 0.0 us)
Async XLA Ops:
  255.6 9.1 %copy-start = (bf16[4,256,768]{2,1,0:T(8,128)(2,1)S(1)}, bf16[4,256,768]{2,1,0:T(8,128)(2,1)}, u32[]{:S(2)}) copy-start(bf16[4,256,768]{2,1,0:T(8,128)(2,1)} %get-tuple-element.44) | copy-start | bytes 4718596
  261.2 4.5 %copy-start.2 = (f32[96,768]{1,0:T(8,128)S(1)}, f32[96,768]{1,0:T(8,128)}, u32[]{:S(2)}) copy-start(f32[96,768]{1,0:T(8,128)} %get-tuple-element.109) | copy-start | bytes 884740
  261.2 5.3 %copy-start.1 = (f32[96,768]{1,0:T(8,128)S(1)}, f32[96,768]{1,0:T(8,128)}, u32[]{:S(2)}) copy-start(f32[96,768]{1,0:T(8,128)} %get-tuple-element.50) | copy-start | bytes 884740

commit v7 on v6

--- a/solution.py
+++ b/solution.py
@@ -158,15 +158,16 @@
 
 PEERS = ((1, 0), (2, 0), (3, 0), (0, 1), (0, 2), (0, 4), (0, 6))
 TOKENS, COTS, BIASES, KIND_A = 0, 3, 6, 9
-SHARD_WIRES, BLOCK_WIRES = 19, 11
+SHARD_WIRES, BLOCK_WIRES = 19, 18
 KIND_I = KIND_A + SHARD_WIRES
 KIND_O = KIND_I + SHARD_WIRES
 FORWARD_WIRES = KIND_O + BLOCK_WIRES
 
 
 class ShardGather:
-    def __init__(self, wires, base, shard, whole):
+    def __init__(self, wires, base, shard, whole, across=False):
         self.wires, self.base, self.shard, self.whole = wires, base, shard, whole
+        self.across = across
         z = lax.div(wires.row, 2)
         self.middle = (z == 1) | (z == 2)
 
@@ -188,8 +189,11 @@
         return self.wires.copy(number, self.at(slot, 4), self.at(slot, 4), 0, 2)
 
     def along_y(self, slot, step):
+        number = self.base + 7 + 4 * (slot // 2) + step
+        if slot and self.across:
+            other = 2 * step + 1
+            return self.wires.copy(number, self.at(0, other), self.at(2, other), 2, 0)
         source = self.own(slot) if step == 0 else self.at(slot, 2 * step)
-        number = self.base + 7 + 4 * (slot // 2) + step
         return self.wires.copy(number, source, self.at(slot, 2 * step), 0, 1)
 
     def to_core(self, slot):
@@ -197,26 +201,33 @@
         return self.wires.copy(number, self.whole.at[slot], self.whole.at[slot + 1], 1, 0)
 
     def start(self, slot):
+        self.along_z(slot, 2).start()
         self.along_z(slot, 1).start()
-        self.along_z(slot, 2).start()
 
         @pl.when(self.middle)
         def _():
             self.along_z(slot, 3).start()
 
-        self.along_y(slot, 0).start()
-
     def advance(self, slot):
+        self.advance_near(slot)
+        self.advance_far(slot)
+
+    def advance_near(self, slot):
         self.along_z(slot, 2).wait_recv()
 
         @pl.when(self.middle)
         def _():
             self.hand_on(slot).start()
 
-        self.along_y(slot, 2).start()
+        self.pass_y(slot, 2)
         self.along_z(slot, 1).wait_recv()
-        self.along_y(slot, 1).start()
-
+        self.pass_y(slot, 1)
+
+    def pass_y(self, slot, step):
+        if not (slot and self.across):
+            self.along_y(slot, step).start()
+
+    def advance_far(self, slot):
         @pl.when(self.middle)
         def _():
             self.along_z(slot, 3).wait_recv()
@@ -225,14 +236,13 @@
         def _():
             self.hand_on(slot).wait_recv()
 
-        self.along_y(slot, 3).start()
+        self.pass_y(slot, 3)
 
     def wait_y(self, slot):
         for step in range(4):
             self.along_y(slot, step).wait_recv()
 
     def wait_sent(self, slots):
-        self.cross_x().wait_send()
         for slot in slots:
             for step in (1, 2):
                 self.along_z(slot, step).wait_send()
@@ -255,19 +265,39 @@
         )
 
     def hand_on(self, slot):
-        return self.wires.copy(self.base + 10, self.at(0, 4), self.at(0, 4), 0, 2)
+        return self.wires.copy(self.base + 7, self.at(0, 4), self.at(0, 4), 0, 2)
 
     def along_y(self, slot, step):
         source = self.own(0) if step == 0 else self.at(0, 2 * step)
         return self.wires.copy(self.base + 3 + step, source, self.at(0, 2 * step), 0, 1)
 
-    def cross_x(self):
-        return self.wires.copy(self.base + 7, self.whole.at[0], self.whole.at[2], 2, 0)
+    def cross(self, bits):
+        source = self.own(0) if bits == 0 else self.at(0, bits)
+        return self.wires.copy(self.base + 8 + bits, source, self.at(2, bits), 2, 0)
 
     def to_core(self, slot):
         return self.wires.copy(
-            self.base + 8 + slot // 2, self.whole.at[slot], self.whole.at[slot + 1], 1, 0
-        )
+            self.base + 16 + slot // 2, self.whole.at[slot], self.whole.at[slot + 1], 1, 0
+        )
+
+    def advance(self, slot):
+        super().advance(slot)
+        for bits in (0, 4, 2, 6):
+            self.cross(bits).start()
+
+    def wait_y(self, slot):
+        super().wait_y(slot)
+        for bits in (1, 3, 5, 7):
+            self.cross(bits).start()
+
+    def wait_x(self):
+        for bits in range(8):
+            self.cross(bits).wait_recv()
+
+    def wait_sent(self, slots):
+        super().wait_sent(slots)
+        for bits in range(8):
+            self.cross(bits).wait_send()
 
 
 def gelu_parts(values):
@@ -388,7 +418,7 @@
     blocks = length // ROWS
     wides = length // WIDE
     wires = Wires(send_sem, recv_sem, place, row)
-    attn = ShardGather(wires, KIND_A, sa_s, a_s)
+    attn = ShardGather(wires, KIND_A, sa_s, a_s, True)
     inner = ShardGather(wires, KIND_I, si_ref, i_s)
     outer = BlockGather(wires, KIND_O, so_s, o_s)
     b_mixer, gain_one, bias_one, b_outer = (vec_ref[i : i + 1, :] for i in range(4))
@@ -425,11 +455,10 @@
             [wq_ref[...], wk_ref[...], wv_ref[...], wm_ref[...].T], axis=1
         )
         greet(wires, PEERS)
-        attn.cross_x().start()
-        for bits in (1, 2, 3):
+        attn.start(0)
+        attn.along_y(0, 0).start()
+        for bits in (2, 3, 1):
             bias_copy(bits, True).start()
-        attn.start(0)
-        for bits in (2, 3, 1):
             exchange(TOKENS, tok_ref, x_s, bits, True).start()
         so_s[...] = wo_ref[...].T
         for copy in local:
@@ -451,11 +480,16 @@
             vt_s[head, HEAD:, :] = jnp.ones((SEG, length), BF16)
         for copy in local:
             copy.wait()
-        attn.cross_x().wait_recv()
-        attn.start(2)
-        attn.advance(0)
+        attn.advance_near(0)
+        outer.start(0)
+        attn.advance_far(0)
+        outer.along_y(0, 0).start()
+        inner.along_y(0, 0).start()
+        attn.cross_x().start()
         attn.wait_y(0)
         attn.to_core(0).start()
+        for number in range(4):
+            attn.along_y(2, number).start()
         inner.cross_x().start()
         for bits in (1, 2, 3):
             exchange(TOKENS, tok_ref, x_s, bits, False).wait_recv()
@@ -530,6 +564,12 @@
             (PAD - width - heads * SEG, length), BF16
         )
 
+        @pl.when(step == 1)
+        def _():
+            attn.advance_near(2)
+            inner.cross_x().wait_recv()
+            inner.start(0)
+
         @pl.loop(0, blocks)
         def _(index):
             cols = rows_of(index)
@@ -540,37 +580,33 @@
 
             @pl.when((step == 0) & (index == 0))
             def _():
-                outer.start(0)
+                attn.cross_x().wait_recv()
+                attn.start(2)
+
+            @pl.when((step == 0) & (index == 1))
+            def _():
+                outer.advance(0)
+
+            @pl.when((step == 1) & (index == 1))
+            def _():
+                attn.advance_far(2)
+
+            @pl.when((step == 1) & (index == 3))
+            def _():
+                outer.wait_y(0)
+                outer.to_core(0).start()
+                inner.start(2)
+                inner.along_y(2, 0).start()
+
+            @pl.when((step == 2) & (index == 1))
+            def _():
+                inner.advance(0)
+
+            @pl.when((step == 3) & (index == 0))
+            def _():
+                inner.advance(2)
                 for bits in (2, 3, 1):
                     exchange(COTS, cot_ref, cot_out, bits, True).start()
-
-            @pl.when((step == 0) & (index == 1))
-            def _():
-                attn.advance(2)
-
-            @pl.when((step == 0) & (index == 3))
-            def _():
-                inner.cross_x().wait_recv()
-                inner.start(0)
-
-            @pl.when((step == 1) & (index == 2))
-            def _():
-                outer.advance(0)
-                inner.start(2)
-
-            @pl.when((step == 2) & (index == 3))
-            def _():
-                inner.advance(0)
-
-            @pl.when((step == 3) & (index == 0))
-            def _():
-                outer.wait_y(0)
-                outer.cross_x().start()
-                outer.to_core(0).start()
-
-            @pl.when((step == 3) & (index == 3))
-            def _():
-                inner.advance(2)
 
         @pl.loop(0, wides)
         def _(index):
@@ -602,7 +638,7 @@
     def _():
         inner.wait_y(2)
         inner.to_core(2).start()
-        outer.cross_x().wait_recv()
+        outer.wait_x()
         outer.to_core(2).start()
 
     @pl.when(step == 7)
@@ -633,8 +669,9 @@
         keep_second.start()
         for bits in (1, 2, 3):
             exchange(COTS, cot_ref, cot_out, bits, False).wait_recv()
-        attn.wait_sent((0, 2))
-        inner.wait_sent((0, 2))
+        for gather in (attn, inner):
+            gather.cross_x().wait_send()
+            gather.wait_sent((0, 2))
         outer.wait_sent((0,))
         for bits in (1, 2, 3):
             exchange(TOKENS, tok_ref, x_s, bits, True).wait_send()

time: 268 us -> 256 us (0.955)
  Pallas kernels: 252 us -> 240 us
    pallas_call x1, Pallas kernels: 108 us -> 97.3 us  [near_forward(): pl.pallas_call(forward_kernel, grid=(2 * groups,), out_shape=[jax.ShapeDt...]
where the time goes in v7:
time: 256 us
  Pallas kernels  240 us (94%)
  local copies, waits for them, and re-layouts  11.5 us (4%)
  other arithmetic  3.4 us (1%)
    pallas_call x1, Pallas kernels, near_backward(): pl.pallas_call(backward_kernel, grid=(8,), out_shape=[jax.ShapeDtypeStruc...  143 us
    pallas_call x1, Pallas kernels, near_forward(): pl.pallas_call(forward_kernel, grid=(2 * groups,), out_shape=[jax.ShapeDt...  97.3 us

profile of v7, /device:TPU:0, one launch (start us, length us, event | category | flops | bytes accessed | tf_op | source)
XLA Modules:
  0.0 255.7 jit_solution(8095930266948068808)
XLA Ops:
  0.7 0.9 concatenate.3
  1.6 0.6 reshape.45.vec_ref
  2.2 1.7 copy.35.wo_ref
  3.9 97.3 %near_forward.1 = (bf16[8,1024,768]{2,1,0:T(8,128)(2,1)}, bf16[4,512,1024]{2,1,0:T(8,128)(2,1)}, bf16[4,1024,768]{2,1,0:T(8,128)(2,1)}, f32[1024,768]{1,0:T(8,12...) custom-call(bf16[4,256,768]{2,1,0:T(8,128)(2,1)} %bitcast.20, ...), custom_call_target="tpu_custom_call" | custom-call | tf_op jit(solution)/shard_map/near_forward/pallas_call | solution.py:1386
  101.2 142.9 %near_backward.1 = (bf16[4,256,768]{2,1,0:T(8,128)(2,1)}, bf16[4,256,768]{2,1,0:T(8,128)(2,1)}, f32[96,768]{1,0:T(8,128)}, f32[96,768]{1,0:T(8,128)}, f32[96,768...) custom-call(bf16[8,1024,768]{2,1,0:T(8,128)(2,1)} %get-tuple-element.34.acts_ref, ...), custom_call_target="tpu_custom_call" | custom-call | tf_op jit(solution)/shard_map/near_backward/pallas_call | solution.py:1556
  244.0 0.0 copy-start
  244.1 1.4 fusion
  245.5 1.7 slice_reduce_fusion
  247.1 1.8 slice_bitcast_fusion
  249.0 0.7 copy.38
  249.7 0.0 copy-start.2
  249.7 0.0 copy-start.1
  249.7 3.4 %bitcast_convert_fusion = f32[4,1,256,768]{3,2,1,0:T(8,128)} fusion(bf16[4,256,768]{2,1,0:T(8,128)(2,1)} %get-tuple-element.45), kind=kLoop, calls=%fused_computation | loop fusion | flops 786432 | bytes 4718592
  253.1 0.0 copy-done
  253.1 1.1 copy.42
  254.2 0.0 copy-done.2
  254.3 0.7 copy.43
  255.0 0.0 copy-done.1
  255.0 0.7 copy.44
  (2 shorter events, 0.0 us)
Async XLA Ops:
  244.0 9.1 %copy-start = (bf16[4,256,768]{2,1,0:T(8,128)(2,1)S(1)}, bf16[4,256,768]{2,1,0:T(8,128)(2,1)}, u32[]{:S(2)}) copy-start(bf16[4,256,768]{2,1,0:T(8,128)(2,1)} %get-tuple-element.44) | copy-start | bytes 4718596
  249.7 4.5 %copy-start.2 = (f32[96,768]{1,0:T(8,128)S(1)}, f32[96,768]{1,0:T(8,128)}, u32[]{:S(2)}) copy-start(f32[96,768]{1,0:T(8,128)} %get-tuple-element.109) | copy-start | bytes 884740
  249.7 5.3 %copy-start.1 = (f32[96,768]{1,0:T(8,128)S(1)}, f32[96,768]{1,0:T(8,128)}, u32[]{:S(2)}) copy-start(f32[96,768]{1,0:T(8,128)} %get-tuple-element.50) | copy-start | bytes 884740

commit v8 on v7

--- a/solution.py
+++ b/solution.py
@@ -460,7 +460,7 @@
         for bits in (2, 3, 1):
             bias_copy(bits, True).start()
             exchange(TOKENS, tok_ref, x_s, bits, True).start()
-        so_s[...] = wo_ref[...].T
+        so_s[...] = wo_ref[...]
         for copy in local:
             copy.start()
         own_cot.start()
@@ -567,8 +567,6 @@
         @pl.when(step == 1)
         def _():
             attn.advance_near(2)
-            inner.cross_x().wait_recv()
-            inner.start(0)
 
         @pl.loop(0, blocks)
         def _(index):
@@ -587,6 +585,10 @@
             def _():
                 outer.advance(0)
 
+            @pl.when((step == 0) & (index == 3))
+            def _():
+                inner.start(0)
+
             @pl.when((step == 1) & (index == 1))
             def _():
                 attn.advance_far(2)
@@ -595,6 +597,7 @@
             def _():
                 outer.wait_y(0)
                 outer.to_core(0).start()
+                inner.cross_x().wait_recv()
                 inner.start(2)
                 inner.along_y(2, 0).start()
 
@@ -602,9 +605,12 @@
             def _():
                 inner.advance(0)
 
+            @pl.when((step == 3) & (index == 2))
+            def _():
+                inner.advance(2)
+
             @pl.when((step == 3) & (index == 0))
             def _():
-                inner.advance(2)
                 for bits in (2, 3, 1):
                     exchange(COTS, cot_ref, cot_out, bits, True).start()
 
@@ -974,7 +980,7 @@
 RED_I = 26
 RED_O = RED_I + Reduce.COUNT
 RED_A = RED_O + Reduce.COUNT
-BACKWARD_WIRES = RED_A + 2 * Reduce.COUNT
+BACKWARD_WIRES = RED_A + 3 * Reduce.COUNT
 BACK_PEERS = PEERS + ((0, 3), (0, 5), (0, 7))
 
 
@@ -1007,10 +1013,12 @@
     outer = Reduce(wires, RED_O, held_o, core_o, y_o, z_o, x_o)
     halves = (slice(0, model // 2), slice(model // 2, model))
     send_a = send_i
+    thirds = [slice(number * PAD, (number + 1) * PAD) for number in range(model // PAD)]
     attn = [
-        Reduce(wires, RED_A + half * Reduce.COUNT, held_a, core_a, y_a, z_a, x_a, cols)
-        for half, cols in enumerate(halves)
+        Reduce(wires, RED_A + number * Reduce.COUNT, held_a, core_a, y_a, z_a, x_a, cols)
+        for number, cols in enumerate(thirds)
     ]
+    ready = (attn[:1], attn[1:])
     gain_one, gain_two, bias_two = (vec_ref[i : i + 1, :] for i in (1, 4, 5))
     key_ref, value_ref = (acts_ref.at[0, :, i * PAD : (i + 1) * PAD] for i in range(2))
     att_ref = side_ref.at[0, PAD : PAD + width]
@@ -1101,22 +1109,19 @@
 
             grad_s[rows, :] += dot_nt(d_inner, wia_ref[0])
 
-        @pl.loop(0, model // (4 * share))
-        def _(pair):
-            rows = rows_of(pair, 4 * share)
-            for transposed, right, sent, held in (
-                (back_t, acts_ref.at[0], send_o, held_o), (low_t, low_s, send_i, held_i),
-            ):
-                grads = dot_nn(transposed[rows, :], right[...]).astype(BF16)
-                pieces = grads.reshape(2, 2, share, model)
-
-                @pl.when(step < 2)
-                def _(pieces=pieces, sent=sent):
-                    sent[step, pl.ds(2 * pair, 2)] = pieces
-
-                @pl.when(step >= 2)
-                def _(pieces=pieces, held=held):
-                    held[3 - step, pl.ds(2 * pair, 2)] = pieces
+        for transposed, right, sent, held in (
+            (back_t, acts_ref.at[0], send_o, held_o), (low_t, low_s, send_i, held_i),
+        ):
+            grads = dot_nn(transposed[...], right[...]).astype(BF16)
+            pieces = grads.reshape(4, 2, share, model)
+
+            @pl.when(step < 2)
+            def _(pieces=pieces, sent=sent):
+                sent[step] = pieces
+
+            @pl.when(step >= 2)
+            def _(pieces=pieces, held=held):
+                held[3 - step] = pieces
 
     for number, j in ((0, 1), (1, 0)):
 
@@ -1164,12 +1169,6 @@
         for number, j in ((0, 1), (1, 0)):
             inner.core_copy(j, send_i.at[number]).wait_send()
 
-    @pl.when(step == 7)
-    def _():
-        for reduce in attn:
-            reduce.add_core(1)
-            reduce.y_copy(1).start()
-
     @pl.when(step >= 4)
     def _():
         wmt_s[...] = wia_ref[0, :, 3 * width :].T
@@ -1236,9 +1235,10 @@
             def _():
                 go_res[...] = outer.total_z(0)
 
-            @pl.when((step == 7) & (index == 3))
-            def _():
-                for reduce in attn:
+            for number, reduce in zip((0, 1, 3), attn):
+
+                @pl.when((step == 7) & (index == number))
+                def _(reduce=reduce):
                     reduce.add_y(1)
                     reduce.start_z(1)
 
@@ -1284,12 +1284,16 @@
 
                 @pl.when(step == 4 + number)
                 def _(number=number, j=j):
-                    attn[half].core_copy(j, send_a.at[number]).start()
-
-            @pl.when(step == 7)
-            def _():
-                attn[half].add_core(0)
-                attn[half].y_copy(0).start()
+                    for reduce in ready[half]:
+                        reduce.core_copy(j, send_a.at[number]).start()
+
+            for j in (1, 0):
+
+                @pl.when(step == 7 - j)
+                def _(j=j):
+                    for reduce in ready[half]:
+                        reduce.add_core(j)
+                        reduce.y_copy(j).start()
 
         @pl.loop(0, wides)
         def _(index):
@@ -1308,12 +1312,11 @@
             exchange(TOKEN_GRADS, flow_s, dtok_res, bits, True).start()
         keep_dtok.start()
         for reduce in attn:
-            reduce.send_x()
-        for reduce in attn:
             reduce.add_y(0)
             reduce.start_z(0)
+            reduce.send_x()
         late_res[...] = sum_rows(LATE_SUMS, late_d)
-        for reduce, cols in zip(attn, halves):
+        for reduce, cols in zip(attn, thirds):
             ga_res[:, cols] = reduce.total()
         for bits in (1, 2, 3):
             for base, source, target in (
@@ -1624,7 +1627,7 @@
             ]
         ).reshape(8, model)
         acts, sides, slopes, first, second, low, xt, cot, w_ia, w_o = near_forward(
-            tokens[:, 0], cotangent[:, 0], w_inner, w_query, w_key, w_value, w_mixer, w_outer,
+            tokens[:, 0], cotangent[:, 0], w_inner, w_query, w_key, w_value, w_mixer, w_outer.T,
             doc_ids, vectors,
         )
         out, d_tokens, ga, gi, go, tail, late = near_backward(

time: 256 us -> 251 us (0.980)
  Pallas kernels: 240 us -> 237 us
where the time goes in v8:
time: 251 us
  Pallas kernels  237 us (94%)
  local copies, waits for them, and re-layouts  9.74 us (4%)
  other arithmetic  3.4 us (1%)
    pallas_call x1, Pallas kernels, near_backward(): pl.pallas_call(backward_kernel, grid=(8,), out_shape=[jax.ShapeDtypeStruc...  140 us
    pallas_call x1, Pallas kernels, near_forward(): pl.pallas_call(forward_kernel, grid=(2 * groups,), out_shape=[jax.ShapeDt...  96.3 us

profile of v8, /device:TPU:0, one launch (start us, length us, event | category | flops | bytes accessed | tf_op | source)
XLA Modules:
  0.0 250.6 jit_solution(11145550442004510281)
XLA Ops:
  0.7 0.9 concatenate.3
  1.6 0.6 reshape.45.vec_ref
  2.2 96.3 %near_forward.1 = (bf16[8,1024,768]{2,1,0:T(8,128)(2,1)}, bf16[4,512,1024]{2,1,0:T(8,128)(2,1)}, bf16[4,1024,768]{2,1,0:T(8,128)(2,1)}, f32[1024,768]{1,0:T(8,12...) custom-call(bf16[4,256,768]{2,1,0:T(8,128)(2,1)} %bitcast.21, ...), custom_call_target="tpu_custom_call" | custom-call | tf_op jit(solution)/shard_map/near_forward/pallas_call | solution.py:1389
  98.5 140.4 %near_backward.1 = (bf16[4,256,768]{2,1,0:T(8,128)(2,1)}, bf16[4,256,768]{2,1,0:T(8,128)(2,1)}, f32[96,768]{1,0:T(8,128)}, f32[96,768]{1,0:T(8,128)}, f32[96,768...) custom-call(bf16[8,1024,768]{2,1,0:T(8,128)(2,1)} %get-tuple-element.34.acts_ref, ...), custom_call_target="tpu_custom_call" | custom-call | tf_op jit(solution)/shard_map/near_backward/pallas_call | solution.py:1559
  238.9 0.0 copy-start
  238.9 1.4 fusion
  240.3 1.7 slice_reduce_fusion
  242.0 1.8 slice_bitcast_fusion
  243.8 0.7 copy.37
  244.6 0.0 copy-start.2
  244.6 0.0 copy-start.1
  244.6 3.4 %bitcast_convert_fusion = f32[4,1,256,768]{3,2,1,0:T(8,128)} fusion(bf16[4,256,768]{2,1,0:T(8,128)(2,1)} %get-tuple-element.45), kind=kLoop, calls=%fused_computation | loop fusion | flops 786432 | bytes 4718592
  248.0 0.0 copy-done
  248.0 1.1 copy.41
  249.1 0.0 copy-done.2
  249.1 0.7 copy.42
  249.8 0.0 copy-done.1
  249.8 0.7 copy.43
  (2 shorter events, 0.0 us)
Async XLA Ops:
  238.9 9.1 %copy-start = (bf16[4,256,768]{2,1,0:T(8,128)(2,1)S(1)}, bf16[4,256,768]{2,1,0:T(8,128)(2,1)}, u32[]{:S(2)}) copy-start(bf16[4,256,768]{2,1,0:T(8,128)(2,1)} %get-tuple-element.44) | copy-start | bytes 4718596
  244.6 4.5 %copy-start.2 = (f32[96,768]{1,0:T(8,128)S(1)}, f32[96,768]{1,0:T(8,128)}, u32[]{:S(2)}) copy-start(f32[96,768]{1,0:T(8,128)} %get-tuple-element.109) | copy-start | bytes 884740
  244.6 5.3 %copy-start.1 = (f32[96,768]{1,0:T(8,128)S(1)}, f32[96,768]{1,0:T(8,128)}, u32[]{:S(2)}) copy-start(f32[96,768]{1,0:T(8,128)} %get-tuple-element.50) | copy-start | bytes 884740

commit v9 on v8

--- a/solution.py
+++ b/solution.py
@@ -1199,7 +1199,7 @@
                 inner.add_y(1)
                 inner.start_z(1)
 
-            @pl.when((step == 4) & (index == 3))
+            @pl.when((step == 5) & (index == 0))
             def _():
                 inner.add_y(0)
                 inner.start_z(0)
@@ -1222,7 +1222,7 @@
             def _():
                 sum_res[...] = sum_rows(SUMS, sums_d)
 
-            @pl.when((step == 5) & (index == 3))
+            @pl.when((step == 6) & (index == 1))
             def _():
                 outer.add_y(0)
                 outer.start_z(0)
@@ -1231,7 +1231,7 @@
             def _():
                 gi_res[...] = inner.total()
 
-            @pl.when((step == 6) & (index == 3))
+            @pl.when((step == 7) & (index == 2))
             def _():
                 go_res[...] = outer.total_z(0)
 
@@ -1295,22 +1295,28 @@
                         reduce.add_core(j)
                         reduce.y_copy(j).start()
 
-        @pl.loop(0, wides)
-        def _(index):
-            rows = rows_of(index, WIDE)
-            transposed = all_t[:, rows].T
-            grad_s[rows, :] += dot_nt(transposed, wia_ref[0, :, : 3 * width])
-
-            @pl.when(step == 7)
-            def _():
-                places = pl.ds(index * (WIDE // part), WIDE // part)
-                flow_s[places] = grad_s[rows, :].astype(BF16).reshape(WIDE // part, part, model)
+            if half == 0:
+
+                @pl.loop(0, wides)
+                def _(index):
+                    rows = rows_of(index, WIDE)
+                    transposed = all_t[:, rows].T
+                    grad_s[rows, :] += dot_nt(transposed, wia_ref[0, :, : 3 * width])
+
+                    @pl.when(step == 7)
+                    def _():
+                        places = pl.ds(index * (WIDE // part), WIDE // part)
+                        flow_s[places] = grad_s[rows, :].astype(BF16).reshape(WIDE // part, part, model)
+
+                @pl.when(step == 7)
+                def _():
+                    for bits in (2, 3, 1):
+                        exchange(TOKEN_GRADS, flow_s, dtok_res, bits, True).start()
+                    keep_dtok.start()
+
 
     @pl.when(step == 7)
     def _():
-        for bits in (2, 3, 1):
-            exchange(TOKEN_GRADS, flow_s, dtok_res, bits, True).start()
-        keep_dtok.start()
         for reduce in attn:
             reduce.add_y(0)
             reduce.start_z(0)

time: 251 us -> 243 us (0.968)
  Pallas kernels: 237 us -> 229 us
    pallas_call x1, Pallas kernels: 140 us -> 133 us  [near_backward(): pl.pallas_call(backward_kernel, grid=(8,), out_shape=[jax.ShapeDtypeStruc...]
where the time goes in v9:
time: 243 us
  Pallas kernels  229 us (94%)
  local copies, waits for them, and re-layouts  9.74 us (4%)
  other arithmetic  3.4 us (1%)
    pallas_call x1, Pallas kernels, near_backward(): pl.pallas_call(backward_kernel, grid=(8,), out_shape=[jax.ShapeDtypeStruc...  133 us
    pallas_call x1, Pallas kernels, near_forward(): pl.pallas_call(forward_kernel, grid=(2 * groups,), out_shape=[jax.ShapeDt...  96.3 us

profile of v9, /device:TPU:0, one launch (start us, length us, event | category | flops | bytes accessed | tf_op | source)
XLA Modules:
  0.0 242.9 jit_solution(18285739851058540877)
XLA Ops:
  0.7 0.9 concatenate.3
  1.6 0.6 reshape.45.vec_ref
  2.2 96.3 %near_forward.1 = (bf16[8,1024,768]{2,1,0:T(8,128)(2,1)}, bf16[4,512,1024]{2,1,0:T(8,128)(2,1)}, bf16[4,1024,768]{2,1,0:T(8,128)(2,1)}, f32[1024,768]{1,0:T(8,12...) custom-call(bf16[4,256,768]{2,1,0:T(8,128)(2,1)} %bitcast.21, ...), custom_call_target="tpu_custom_call" | custom-call | tf_op jit(solution)/shard_map/near_forward/pallas_call | solution.py:1395
  98.5 132.8 %near_backward.1 = (bf16[4,256,768]{2,1,0:T(8,128)(2,1)}, bf16[4,256,768]{2,1,0:T(8,128)(2,1)}, f32[96,768]{1,0:T(8,128)}, f32[96,768]{1,0:T(8,128)}, f32[96,768...) custom-call(bf16[8,1024,768]{2,1,0:T(8,128)(2,1)} %get-tuple-element.34.acts_ref, ...), custom_call_target="tpu_custom_call" | custom-call | tf_op jit(solution)/shard_map/near_backward/pallas_call | solution.py:1565
  231.3 0.0 copy-start
  231.3 1.4 fusion
  232.7 1.7 slice_reduce_fusion
  234.4 1.8 slice_bitcast_fusion
  236.2 0.7 copy.37
  237.0 0.0 copy-start.2
  237.0 0.0 copy-start.1
  237.0 3.4 %bitcast_convert_fusion = f32[4,1,256,768]{3,2,1,0:T(8,128)} fusion(bf16[4,256,768]{2,1,0:T(8,128)(2,1)} %get-tuple-element.45), kind=kLoop, calls=%fused_computation | loop fusion | flops 786432 | bytes 4718592
  240.4 0.0 copy-done
  240.4 1.1 copy.41
  241.5 0.0 copy-done.2
  241.5 0.7 copy.42
  242.2 0.0 copy-done.1
  242.2 0.7 copy.43
  (2 shorter events, 0.0 us)
Async XLA Ops:
  231.3 9.1 %copy-start = (bf16[4,256,768]{2,1,0:T(8,128)(2,1)S(1)}, bf16[4,256,768]{2,1,0:T(8,128)(2,1)}, u32[]{:S(2)}) copy-start(bf16[4,256,768]{2,1,0:T(8,128)(2,1)} %get-tuple-element.44) | copy-start | bytes 4718596
  237.0 4.5 %copy-start.2 = (f32[96,768]{1,0:T(8,128)S(1)}, f32[96,768]{1,0:T(8,128)}, u32[]{:S(2)}) copy-start(f32[96,768]{1,0:T(8,128)} %get-tuple-element.109) | copy-start | bytes 884740
  237.0 5.3 %copy-start.1 = (f32[96,768]{1,0:T(8,128)S(1)}, f32[96,768]{1,0:T(8,128)}, u32[]{:S(2)}) copy-start(f32[96,768]{1,0:T(8,128)} %get-tuple-element.50) | copy-start | bytes 884740

commit v10 on v9

--- a/solution.py
+++ b/solution.py
@@ -1094,9 +1094,9 @@
 
     @pl.when(step < 4)
     def _():
-        @pl.loop(0, wides)
+        @pl.loop(0, 1)
         def _(index):
-            rows = rows_of(index, WIDE)
+            rows = rows_of(index, length)
             d_hidden = dot_nn(dmix_s[rows, :], wo_ref[0])
             d_inner = (d_hidden * slope_ref[0, rows, :].astype(F32)).astype(BF16)
             low_s[rows, :] = d_inner
@@ -1297,16 +1297,16 @@
 
             if half == 0:
 
-                @pl.loop(0, wides)
+                @pl.loop(0, 1)
                 def _(index):
-                    rows = rows_of(index, WIDE)
+                    rows = rows_of(index, length)
                     transposed = all_t[:, rows].T
                     grad_s[rows, :] += dot_nt(transposed, wia_ref[0, :, : 3 * width])
 
                     @pl.when(step == 7)
                     def _():
-                        places = pl.ds(index * (WIDE // part), WIDE // part)
-                        flow_s[places] = grad_s[rows, :].astype(BF16).reshape(WIDE // part, part, model)
+                        places = pl.ds(0, quarters)
+                        flow_s[places] = grad_s[rows, :].astype(BF16).reshape(quarters, part, model)
 
                 @pl.when(step == 7)
                 def _():

time: 243 us -> 237 us (0.975)
  Pallas kernels: 229 us -> 223 us
    pallas_call x1, Pallas kernels: 133 us -> 126 us  [near_backward(): pl.pallas_call(backward_kernel, grid=(8,), out_shape=[jax.ShapeDtypeStruc...]
where the time goes in v10:
time: 237 us; the launch traced here: 236 us
  Pallas kernels  223 us (94%)
  local copies, waits for them, and re-layouts  9.74 us (4%)
  other arithmetic  3.4 us (1%)
    pallas_call x1, Pallas kernels, near_backward(): pl.pallas_call(backward_kernel, grid=(8,), out_shape=[jax.ShapeDtypeStruc...  126 us
    pallas_call x1, Pallas kernels, near_forward(): pl.pallas_call(forward_kernel, grid=(2 * groups,), out_shape=[jax.ShapeDt...  96.3 us

profile of v10, /device:TPU:0, one launch (start us, length us, event | category | flops | bytes accessed | tf_op | source)
XLA Modules:
  0.0 236.4 jit_solution(6726901634702977913)
XLA Ops:
  0.7 0.9 concatenate.3
  1.6 0.6 reshape.45.vec_ref
  2.2 96.3 %near_forward.1 = (bf16[8,1024,768]{2,1,0:T(8,128)(2,1)}, bf16[4,512,1024]{2,1,0:T(8,128)(2,1)}, bf16[4,1024,768]{2,1,0:T(8,128)(2,1)}, f32[1024,768]{1,0:T(8,12...) custom-call(bf16[4,256,768]{2,1,0:T(8,128)(2,1)} %bitcast.21, ...), custom_call_target="tpu_custom_call" | custom-call | tf_op jit(solution)/shard_map/near_forward/pallas_call | solution.py:1395
  98.5 126.3 %near_backward.1 = (bf16[4,256,768]{2,1,0:T(8,128)(2,1)}, bf16[4,256,768]{2,1,0:T(8,128)(2,1)}, f32[96,768]{1,0:T(8,128)}, f32[96,768]{1,0:T(8,128)}, f32[96,768...) custom-call(bf16[8,1024,768]{2,1,0:T(8,128)(2,1)} %get-tuple-element.34.acts_ref, ...), custom_call_target="tpu_custom_call" | custom-call | tf_op jit(solution)/shard_map/near_backward/pallas_call | solution.py:1565
  224.8 0.0 copy-start
  224.8 1.4 fusion
  226.2 1.7 slice_reduce_fusion
  227.9 1.8 slice_bitcast_fusion
  229.7 0.7 copy.37
  230.5 0.0 copy-start.2
  230.5 0.0 copy-start.1
  230.5 3.4 %bitcast_convert_fusion = f32[4,1,256,768]{3,2,1,0:T(8,128)} fusion(bf16[4,256,768]{2,1,0:T(8,128)(2,1)} %get-tuple-element.45), kind=kLoop, calls=%fused_computation | loop fusion | flops 786432 | bytes 4718592
  233.9 0.0 copy-done
  233.9 1.1 copy.41
  235.0 0.0 copy-done.2
  235.0 0.7 copy.42
  235.7 0.0 copy-done.1
  235.7 0.7 copy.43
  (2 shorter events, 0.0 us)
Async XLA Ops:
  224.8 9.1 %copy-start = (bf16[4,256,768]{2,1,0:T(8,128)(2,1)S(1)}, bf16[4,256,768]{2,1,0:T(8,128)(2,1)}, u32[]{:S(2)}) copy-start(bf16[4,256,768]{2,1,0:T(8,128)(2,1)} %get-tuple-element.44) | copy-start | bytes 4718596
  230.5 4.5 %copy-start.2 = (f32[96,768]{1,0:T(8,128)S(1)}, f32[96,768]{1,0:T(8,128)}, u32[]{:S(2)}) copy-start(f32[96,768]{1,0:T(8,128)} %get-tuple-element.109) | copy-start | bytes 884740
  230.5 5.3 %copy-start.1 = (f32[96,768]{1,0:T(8,128)S(1)}, f32[96,768]{1,0:T(8,128)}, u32[]{:S(2)}) copy-start(f32[96,768]{1,0:T(8,128)} %get-tuple-element.50) | copy-start | bytes 884740
